TPU v7x, 32 devices: a whole 2x2x4 slice. The times are simulated.
32 devices in a mesh: dp: 8 (over z, y), head: 4 (over x, core).
Axes of the slice: x: 2, y: 2, z: 4, core: 2. Of those that a mesh axis runs over, the one named last changes fastest.
Arguments:
- tokens: bfloat16 [18816, 768], P(('dp', 'head')), may hold values from -6 to 6
- cotangent: bfloat16 [18816, 768], P(('dp', 'head')), may hold values from -6 to 6
- crop_counts: int32 [32], P('dp'), may hold values from 2 to 12, as said below
- pad_mask: int32 [384, 49], P('dp'), may hold values from 0 to 1, as said below
- region_ids: int32 [384, 49], P('dp'), may hold values from 0 to 3, as said below
- rel_index: int32 [49, 49], replicated, may hold values from 0 to 168, as said below
- norm_gain: bfloat16 [2, 2, 768], P(None, None, 'dp'), may hold values from 0.5 to 1.5
- norm_shift: bfloat16 [2, 2, 768], P(None, None, 'dp'), may hold values from -3 to 3
- qkv_weight: bfloat16 [2, 768, 3, 768], P(None, 'dp', None, 'head'), may hold values from -0.21875 to 0.21875
- qv_bias: bfloat16 [2, 2, 768], P(None, None, 'dp'), may hold values from -3 to 3
- bias_table: bfloat16 [2, 24, 169], P(None, 'head'), may hold values from -5 to 5
- proj_weight: bfloat16 [2, 768, 768], P(None, 'head', 'dp'), may hold values from -0.875 to 0.875
- fc1_weight: bfloat16 [2, 768, 3072], P(None, 'dp', 'head'), may hold values from -0.21875 to 0.21875
- fc1_bias: bfloat16 [2, 3072], P(None, 'dp'), may hold values from -3 to 3
- fc2_weight: bfloat16 [2, 3072, 768], P(None, 'head', 'dp'), may hold values from -0.109375 to 0.109375
- out_bias: bfloat16 [2, 2, 768], P(None, None, 'dp'), may hold values from -3 to 3
Outputs:
- output: float32 [18816, 768], P(('dp', 'head'))
- tokens_grad: float32 [18816, 768], P(('dp', 'head'))
- norm_gain_grad: float32 [2, 2, 768], P(None, None, 'dp')
- norm_shift_grad: float32 [2, 2, 768], P(None, None, 'dp')
- qkv_weight_grad: float32 [2, 768, 3, 768], P(None, 'dp', None, 'head')
- qv_bias_grad: float32 [2, 2, 768], P(None, None, 'dp')
- bias_table_grad: float32 [2, 24, 169], P(None, 'head')
- proj_weight_grad: float32 [2, 768, 768], P(None, 'head', 'dp')
- fc1_weight_grad: float32 [2, 768, 3072], P(None, 'dp', 'head')
- fc1_bias_grad: float32 [2, 3072], P(None, 'dp')
- fc2_weight_grad: float32 [2, 3072, 768], P(None, 'head', 'dp')
- out_bias_grad: float32 [2, 2, 768], P(None, None, 'dp')
Inputs may be any that keep to these rules, and one draw needn't show every extreme that they name: `crop_counts`: each image has at least 2 crops and one image has exactly 2; among the images of each aligned block of 4 images at least one has 12. `pad_mask`: windows whose slot (window mod 12) is below 2 are all ones; every other window has ones on one square of 3 x 3 positions and zeros elsewhere. `region_ids`: in each window the positions fall into four rectangles, cut by one row boundary and one column boundary. `rel_index`: entry (i, j) depends only on the offset between positions i and j, and different offsets have different entries.
All inputs are finite; a program needn't handle non-finite values.
Results may differ from a plain program's by a relative error of at most 0.022.
Values may be sent and summed in bfloat16 or wider, within the bound.
No kernel may reach another device: no remote copies, remote signals or barrier semaphores. Data moves between devices by JAX's collectives and lax.ppermute only.
A program may use at most 256 MiB of HBM per device.

v0:
```python
import jax
import jax.numpy as jnp
from jax import lax
from jax.sharding import PartitionSpec as P

WSIDE = 7
SHIFT = 3
CROP_MAX = 12
BLOCKS = 2
WTOK = 49


EPSILON = 1e-05
MASKED = -100.0
HIGHEST = lax.Precision.HIGHEST


def layer_norm(values, gain, shift):
    centre = jnp.mean(values, axis=-1, keepdims=True)
    centred = values - centre
    spread = jnp.mean(centred * centred, axis=-1, keepdims=True)
    return centred * lax.rsqrt(spread + EPSILON) * gain + shift


def gelu_exact(values):
    return jax.nn.gelu(values, approximate=False)


def matmul(left, right):
    return jnp.dot(left, right, preferred_element_type=jnp.float32)


def matmul_tn(left, right):
    return lax.dot_general(
        left, right, (((0,), (0,)), ((), ())), preferred_element_type=jnp.float32
    )


def matmul_nt(left, right):
    return lax.dot_general(
        left, right, (((1,), (1,)), ((), ())), preferred_element_type=jnp.float32
    )


def roll_tokens(values, step):
    shape = values.shape
    grid = values.reshape((shape[0], WSIDE, WSIDE) + shape[2:])
    return jnp.roll(grid, (step, step), axis=(1, 2)).reshape(shape)


def to_windows(values, heads, shifted):
    grid = values.reshape(values.shape[0] // WTOK, WTOK, heads, values.shape[1] // heads)
    if shifted:
        grid = roll_tokens(grid, -SHIFT)
    return grid


def from_windows(values, shifted):
    if shifted:
        values = roll_tokens(values, SHIFT)
    return values.reshape(values.shape[0] * values.shape[1], values.shape[2] * values.shape[3])


def attention_mask(pad_mask, region_ids, shifted):
    valid = pad_mask
    if shifted:
        valid = roll_tokens(pad_mask, -SHIFT)
    allowed = jnp.broadcast_to(valid[:, None, :] == 1, (valid.shape[0], WTOK, WTOK))
    if shifted:
        allowed = allowed & (region_ids[:, :, None] == region_ids[:, None, :])
    return jnp.where(allowed, 0.0, MASKED).astype(jnp.float32)


def window_scores(query, key, position_bias, additive):
    raw = jnp.einsum("wqhd,wkhd->whqk", query, key, preferred_element_type=jnp.float32)
    return raw + position_bias[None] + additive[:, None]


def place_slot(values, index, total, axis):
    shape = list(values.shape)
    shape[axis] = total
    return lax.dynamic_update_slice_in_dim(
        jnp.zeros(shape, values.dtype), values, index * values.shape[axis], axis
    )


def shards(
    tokens,
    cotangent,
    crop_counts,
    pad_mask,
    region_ids,
    rel_index,
    norm_gain,
    norm_shift,
    qkv_weight,
    qv_bias,
    bias_table,
    proj_weight,
    fc1_weight,
    fc1_bias,
    fc2_weight,
    out_bias,
):
    rows_dev = tokens.shape[0]
    width = tokens.shape[1]
    win_dev = pad_mask.shape[0]
    local_width = qkv_weight.shape[3]
    local_heads = bias_table.shape[1]
    rel_count = bias_table.shape[2]
    dp_width = norm_gain.shape[2]
    dp_hidden = fc1_bias.shape[1]
    heads_total = local_heads * lax.axis_size("head")
    scale = (local_width // local_heads) ** (-0.5)
    head_index = lax.axis_index("head")
    dp_index = lax.axis_index("dp")
    window_counts = jnp.repeat(crop_counts, CROP_MAX)
    slots = jnp.arange(win_dev, dtype=jnp.int32) % CROP_MAX
    live_windows = (slots < window_counts).astype(jnp.float32)
    live_group = jnp.repeat(live_windows, WTOK)
    live = lax.dynamic_slice_in_dim(live_group, head_index * rows_dev, rows_dev, 0)[:, None]
    masks = (
        attention_mask(pad_mask, region_ids, False),
        attention_mask(pad_mask, region_ids, True),
    )
    position_table = (
        jnp.arange(rel_count, dtype=jnp.int32)[:, None] == rel_index.reshape(1, -1)
    ).astype(jnp.float32)
    kept = []
    residual = tokens.astype(jnp.float32)
    for block in range(BLOCKS):
        shifted = block % 2 == 1
        additive = masks[block % 2]
        fc1_part = fc1_weight[block]
        fc2_part = fc2_weight[block]
        fc1_part, fc2_part = (
            lax.all_gather(fc1_part, "head", axis=1, tiled=True),
            lax.all_gather(fc2_part, "head", axis=0, tiled=True),
        )
        gathered = (
            lax.all_gather(qkv_weight[block], "dp", axis=0, tiled=True),
            lax.all_gather(proj_weight[block], "dp", axis=1, tiled=True),
            lax.all_gather(fc1_part, "dp", axis=0, tiled=True),
            lax.all_gather(fc2_part, "dp", axis=1, tiled=True),
            lax.all_gather(norm_gain[block], "dp", axis=1, tiled=True),
            lax.all_gather(norm_shift[block], "dp", axis=1, tiled=True),
            lax.all_gather(qv_bias[block], "dp", axis=1, tiled=True),
            lax.all_gather(fc1_bias[block], "dp", axis=0, tiled=True),
            lax.all_gather(out_bias[block], "dp", axis=1, tiled=True),
        )
        qkv_all, proj_local, fc1_used, fc2_used, gains, shifts, qv_all, hidden_bias, out_all = (
            gathered
        )
        gains = gains.astype(jnp.float32)
        shifts = shifts.astype(jnp.float32)
        out_all = out_all.astype(jnp.float32)
        qkv_matrix = qkv_all.reshape(width, 3 * local_width)
        q_bias = lax.dynamic_slice_in_dim(
            qv_all[0], head_index * local_width, local_width, 0
        ).astype(jnp.float32)
        v_bias = lax.dynamic_slice_in_dim(
            qv_all[1], head_index * local_width, local_width, 0
        ).astype(jnp.float32)
        table = bias_table[block].astype(jnp.float32)
        position_bias = jnp.dot(table, position_table, precision=HIGHEST).reshape(
            local_heads, WTOK, WTOK
        )
        normed = layer_norm(residual, gains[0], shifts[0]).astype(jnp.bfloat16)
        projected = matmul(lax.all_gather(normed, "head", axis=0, tiled=True), qkv_matrix)
        query = ((projected[:, :local_width] + q_bias) * scale).astype(jnp.bfloat16)
        key = projected[:, local_width : 2 * local_width].astype(jnp.bfloat16)
        value = (projected[:, 2 * local_width :] + v_bias).astype(jnp.bfloat16)
        query_w = to_windows(query, local_heads, shifted)
        key_w = to_windows(key, local_heads, shifted)
        value_w = to_windows(value, local_heads, shifted)
        scores = window_scores(query_w, key_w, position_bias, additive)
        peak = jnp.max(scores, axis=-1, keepdims=True)
        expo = jnp.exp(scores - peak)
        totals = jnp.sum(expo, axis=-1, keepdims=True)
        weights = (expo / totals).astype(jnp.bfloat16)
        log_total = peak + jnp.log(totals)
        attended = jnp.einsum(
            "whqk,wkhd->wqhd", weights, value_w, preferred_element_type=jnp.float32
        )
        attended = from_windows(attended, shifted).astype(jnp.bfloat16)
        qkv_whole = None
        attn_branch = lax.psum_scatter(
            matmul(attended, proj_local).astype(jnp.bfloat16),
            "head",
            scatter_dimension=0,
            tiled=True,
        ).astype(jnp.float32)
        mixed = residual + live * (attn_branch + out_all[0])
        normed2 = layer_norm(mixed, gains[1], shifts[1]).astype(jnp.bfloat16)
        pre_hidden = matmul(normed2, fc1_used) + hidden_bias.astype(jnp.float32)
        hidden = gelu_exact(pre_hidden).astype(jnp.bfloat16)
        mlp_branch = matmul(hidden, fc2_used)
        kept.append(
            (
                residual,
                mixed,
                normed,
                normed2,
                query_w,
                key_w,
                value_w,
                weights,
                log_total,
                attended,
                pre_hidden,
                hidden,
                qkv_matrix,
                proj_local,
                fc1_used,
                fc2_used,
                gains,
                shifts,
                position_bias,
                qkv_whole,
            )
        )
        residual = mixed + live * (mlp_branch + out_all[1])
    grad_rows = cotangent.astype(jnp.float32)
    weight_grads = [None] * BLOCKS
    small_terms = [None] * BLOCKS
    for block in reversed(range(BLOCKS)):
        shifted = block % 2 == 1
        additive = masks[block % 2]
        (
            block_input,
            mixed,
            normed,
            normed2,
            query_w,
            key_w,
            value_w,
            weights,
            log_total,
            attended,
            pre_hidden,
            hidden,
            qkv_matrix,
            proj_local,
            fc1_used,
            fc2_used,
            gains,
            shifts,
            position_bias,
            qkv_whole,
        ) = kept[block]
        branch_grad = (live * grad_rows).astype(jnp.bfloat16)
        second_bias_grad = jnp.sum(branch_grad, axis=0, dtype=jnp.float32)
        _, gelu_pull = jax.vjp(gelu_exact, pre_hidden)
        hidden_grad = matmul_nt(branch_grad, fc2_used)
        pre_grad = gelu_pull(hidden_grad)[0].astype(jnp.bfloat16)
        fc2_grad = matmul_tn(hidden, branch_grad)
        fc1_grad = matmul_tn(normed2, pre_grad)
        hidden_bias_grad = jnp.sum(pre_grad, axis=0, dtype=jnp.float32)
        normed2_grad = matmul_nt(pre_grad, fc1_used)
        _, second_pull = jax.vjp(layer_norm, mixed, gains[1], shifts[1])
        mixed_part, gain2_grad, shift2_grad = second_pull(normed2_grad)
        mixed_grad = grad_rows + mixed_part
        attn_grad = (live * mixed_grad).astype(jnp.bfloat16)
        first_bias_grad = jnp.sum(attn_grad, axis=0, dtype=jnp.float32)
        attn_group, normed_group = (
            lax.all_gather(attn_grad, "head", axis=0, tiled=True),
            lax.all_gather(normed, "head", axis=0, tiled=True),
        )
        attended_grad = matmul_nt(attn_group, proj_local).astype(jnp.bfloat16)
        proj_grad = matmul_tn(attended, attn_group)
        grad_w = to_windows(attended_grad, local_heads, shifted)
        scores = window_scores(query_w, key_w, position_bias, additive)
        probs = jnp.exp(scores - log_total)
        prob_grad = jnp.einsum(
            "wqhd,wkhd->whqk", grad_w, value_w, preferred_element_type=jnp.float32
        )
        row_dot = jnp.sum(probs * prob_grad, axis=-1, keepdims=True)
        score_grad = (probs * (prob_grad - row_dot)).astype(jnp.bfloat16)
        score_total = jnp.sum(score_grad, axis=0, dtype=jnp.float32).reshape(
            local_heads, WTOK * WTOK
        )
        table_grad = lax.dot_general(
            score_total,
            position_table,
            (((1,), (1,)), ((), ())),
            precision=HIGHEST,
            preferred_element_type=jnp.float32,
        )
        query_grad = (
            scale
            * jnp.einsum("whqk,wkhd->wqhd", score_grad, key_w, preferred_element_type=jnp.float32)
        ).astype(jnp.bfloat16)
        key_grad = jnp.einsum(
            "whqk,wqhd->wkhd", score_grad, query_w, preferred_element_type=jnp.float32
        ).astype(jnp.bfloat16)
        value_grad = jnp.einsum(
            "whqk,wqhd->wkhd", weights, grad_w, preferred_element_type=jnp.float32
        ).astype(jnp.bfloat16)
        qkv_grad = jnp.concatenate(
            [
                from_windows(query_grad, shifted),
                from_windows(key_grad, shifted),
                from_windows(value_grad, shifted),
            ],
            axis=1,
        )
        q_bias_grad = jnp.sum(qkv_grad[:, :local_width], axis=0, dtype=jnp.float32)
        v_bias_grad = jnp.sum(qkv_grad[:, 2 * local_width :], axis=0, dtype=jnp.float32)
        qkv_grad_matrix = matmul_tn(normed_group, qkv_grad).reshape(width, 3, local_width)
        normed_grad = lax.psum_scatter(
            matmul_nt(qkv_grad, qkv_matrix).astype(jnp.bfloat16),
            "head",
            scatter_dimension=0,
            tiled=True,
        ).astype(jnp.float32)
        _, first_pull = jax.vjp(layer_norm, block_input, gains[0], shifts[0])
        input_part, gain1_grad, shift1_grad = first_pull(normed_grad)
        grad_rows = mixed_grad + input_part
        reduced = (
            lax.psum_scatter(qkv_grad_matrix, "dp", scatter_dimension=0, tiled=True),
            lax.psum_scatter(proj_grad, "dp", scatter_dimension=1, tiled=True),
            lax.psum_scatter(fc1_grad, "dp", scatter_dimension=0, tiled=True),
            lax.psum_scatter(fc2_grad, "dp", scatter_dimension=1, tiled=True),
        )
        fc1_shard = reduced[2]
        fc2_shard = reduced[3]
        fc1_shard, fc2_shard = (
            lax.psum_scatter(
                fc1_shard.astype(jnp.bfloat16), "head", scatter_dimension=1, tiled=True
            ).astype(jnp.float32),
            lax.psum_scatter(
                fc2_shard.astype(jnp.bfloat16), "head", scatter_dimension=0, tiled=True
            ).astype(jnp.float32),
        )
        weight_grads[block] = (reduced[0], reduced[1], fc1_shard, fc2_shard)
        small_terms[block] = (
            jnp.stack([gain1_grad, gain2_grad]),
            jnp.stack([shift1_grad, shift2_grad]),
            place_slot(jnp.stack([q_bias_grad, v_bias_grad]), head_index, width, 1),
            hidden_bias_grad,
            jnp.stack([first_bias_grad, second_bias_grad]),
            place_slot(table_grad, head_index, heads_total, 0),
        )
    gain_terms = jnp.stack([small_terms[index][0] for index in range(BLOCKS)])
    shift_terms = jnp.stack([small_terms[index][1] for index in range(BLOCKS)])
    qv_terms = jnp.stack([small_terms[index][2] for index in range(BLOCKS)])
    hidden_terms = jnp.stack([small_terms[index][3] for index in range(BLOCKS)])
    bias_terms = jnp.stack([small_terms[index][4] for index in range(BLOCKS)])
    table_terms = jnp.stack([small_terms[index][5] for index in range(BLOCKS)])
    gain_sum, shift_sum, qv_sum, hidden_sum, bias_sum, table_sum = lax.psum(
        (gain_terms, shift_terms, qv_terms, hidden_terms, bias_terms, table_terms), ("dp", "head")
    )
    norm_gain_grad = lax.dynamic_slice_in_dim(gain_sum, dp_index * dp_width, dp_width, 2)
    norm_shift_grad = lax.dynamic_slice_in_dim(shift_sum, dp_index * dp_width, dp_width, 2)
    qv_bias_grad = lax.dynamic_slice_in_dim(qv_sum, dp_index * dp_width, dp_width, 2)
    fc1_bias_grad = lax.dynamic_slice_in_dim(hidden_sum, dp_index * dp_hidden, dp_hidden, 1)
    out_bias_grad = lax.dynamic_slice_in_dim(bias_sum, dp_index * dp_width, dp_width, 2)
    bias_table_grad = lax.dynamic_slice_in_dim(table_sum, head_index * local_heads, local_heads, 1)
    qkv_weight_grad = jnp.stack([weight_grads[index][0] for index in range(BLOCKS)])
    proj_weight_grad = jnp.stack([weight_grads[index][1] for index in range(BLOCKS)])
    fc1_weight_grad = jnp.stack([weight_grads[index][2] for index in range(BLOCKS)])
    fc2_weight_grad = jnp.stack([weight_grads[index][3] for index in range(BLOCKS)])
    return (
        residual,
        grad_rows,
        norm_gain_grad,
        norm_shift_grad,
        qkv_weight_grad,
        qv_bias_grad,
        bias_table_grad,
        proj_weight_grad,
        fc1_weight_grad,
        fc1_bias_grad,
        fc2_weight_grad,
        out_bias_grad,
    )


def solution(mesh):
    placed = (
        P(("dp", "head"), None),
        P(("dp", "head"), None),
        P("dp"),
        P("dp", None),
        P("dp", None),
        P(),
        P(None, None, "dp"),
        P(None, None, "dp"),
        P(None, "dp", None, "head"),
        P(None, None, "dp"),
        P(None, "head", None),
        P(None, "head", "dp"),
        P(None, "dp", "head"),
        P(None, "dp"),
        P(None, "head", "dp"),
        P(None, None, "dp"),
    )
    return jax.shard_map(
        shards,
        mesh=mesh,
        in_specs=placed,
        out_specs=(
            P(("dp", "head"), None),
            P(("dp", "head"), None),
            P(None, None, "dp"),
            P(None, None, "dp"),
            P(None, "dp", None, "head"),
            P(None, None, "dp"),
            P(None, "head", None),
            P(None, "head", "dp"),
            P(None, "dp", "head"),
            P(None, "dp"),
            P(None, "head", "dp"),
            P(None, None, "dp"),
        ),
        check_vma=False,
    )
```

profile of v0, /device:TPU:0, one launch (start us, length us, event | category | flops | bytes accessed | tf_op | source)
XLA Modules:
  0.0 2369.5 jit_solution(8027044349468587520)
XLA Ops:
  11.9 32.7 %all-gather = bf16[1,2,768]{1,0,2:T(2,128)(2,1)S(1)} all-gather(bf16[1,2,96]{1,0,2:T(2,128)(2,1)S(1)} %copy.270), channel_id=2, replica_groups=mesh['dp'=8,'head'=4] {'dp'}, dimensions={2}, use_global_device_ids=true | all-gather | bytes 3456 | tf_op jit(solution)/shard_map/all_gather | solution.py:145
  49.7 31.0 %all-gather.1 = bf16[1,2,768]{1,0,2:T(2,128)(2,1)S(1)} all-gather(bf16[1,2,96]{1,0,2:T(2,128)(2,1)S(1)} %copy.271), channel_id=3, replica_groups=mesh['dp'=8,'head'=4] {'dp'}, dimensions={2}, use_global_device_ids=true | all-gather | bytes 3456 | tf_op jit(solution)/shard_map/all_gather | solution.py:146
  112.2 31.8 %all-gather.3 = bf16[1,2,768]{1,0,2:T(2,128)(2,1)S(1)} all-gather(bf16[1,2,96]{1,0,2:T(2,128)(2,1)S(1)} %copy.273), channel_id=5, replica_groups=mesh['dp'=8,'head'=4] {'dp'}, dimensions={2}, use_global_device_ids=true | all-gather | bytes 3456 | tf_op jit(solution)/shard_map/all_gather | solution.py:147
  144.0 32.9 %all-gather.5 = bf16[1,2,768]{1,0,2:T(2,128)(2,1)S(1)} all-gather(bf16[1,2,96]{1,0,2:T(2,128)(2,1)S(1)} %copy.276), channel_id=7, replica_groups=mesh['dp'=8,'head'=4] {'dp'}, dimensions={2}, use_global_device_ids=true | all-gather | bytes 3456 | tf_op jit(solution)/shard_map/all_gather | solution.py:149
  181.8 32.3 %all-gather.11 = bf16[1,2,768]{1,0,2:T(2,128)(2,1)S(1)} all-gather(bf16[1,2,96]{1,0,2:T(2,128)(2,1)S(1)} %copy.277), channel_id=13, replica_groups=mesh['dp'=8,'head'=4] {'dp'}, dimensions={2}, use_global_device_ids=true | all-gather | bytes 3456 | tf_op jit(solution)/shard_map/all_gather | solution.py:145
  219.1 32.5 %all-gather.12 = bf16[1,2,768]{1,0,2:T(2,128)(2,1)S(1)} all-gather(bf16[1,2,96]{1,0,2:T(2,128)(2,1)S(1)} %copy.278), channel_id=14, replica_groups=mesh['dp'=8,'head'=4] {'dp'}, dimensions={2}, use_global_device_ids=true | all-gather | bytes 3456 | tf_op jit(solution)/shard_map/all_gather | solution.py:146
  253.7 34.8 %all-gather.4 = bf16[1,192,768]{1,0,2:T(2,128)(2,1)S(1)} all-gather(bf16[1,192,96]{1,0,2:T(2,128)(2,1)S(1)} %copy.275), channel_id=6, replica_groups=mesh['dp'=8,'head'=4] {'dp'}, dimensions={2}, use_global_device_ids=true | all-gather | bytes 331776 | tf_op jit(solution)/shard_map/all_gather | solution.py:142
  289.0 39.3 %all-gather.2 = bf16[1,768,3,192]{3,2,0,1:T(4,128)(2,1)S(1)} all-gather(bf16[1,96,3,192]{3,2,0,1:T(4,128)(2,1)} %copy.272), channel_id=4, replica_groups=mesh['dp'=8,'head'=4] {'dp'}, dimensions={1}, use_global_device_ids=true | all-gather | bytes 995328 | tf_op jit(solution)/shard_map/all_gather | solution.py:141
  383.3 36.0 %fusion = bf16[592,768]{1,0:T(8,128)(2,1)} fusion(bf16[2352,768]{1,0:T(8,128)(2,1)} %convolution_convert_fusion.3), kind=kCustom, calls=%all-reduce-scatter | all-reduce-scatter fusion | flops 1818625 | bytes 4522496
  514.6 32.1 %all-gather.14 = bf16[1,2,768]{1,0,2:T(2,128)(2,1)S(1)} all-gather(bf16[1,2,96]{1,0,2:T(2,128)(2,1)S(1)} %copy.280), channel_id=16, replica_groups=mesh['dp'=8,'head'=4] {'dp'}, dimensions={2}, use_global_device_ids=true | all-gather | bytes 3456 | tf_op jit(solution)/shard_map/all_gather | solution.py:147
  546.7 32.6 %all-gather.16 = bf16[1,2,768]{1,0,2:T(2,128)(2,1)S(1)} all-gather(bf16[1,2,96]{1,0,2:T(2,128)(2,1)S(1)} %copy.283), channel_id=18, replica_groups=mesh['dp'=8,'head'=4] {'dp'}, dimensions={2}, use_global_device_ids=true | all-gather | bytes 3456 | tf_op jit(solution)/shard_map/all_gather | solution.py:149
  582.2 34.7 %all-gather.15 = bf16[1,192,768]{1,0,2:T(2,128)(2,1)S(1)} all-gather(bf16[1,192,96]{1,0,2:T(2,128)(2,1)S(1)} %copy.282), channel_id=17, replica_groups=mesh['dp'=8,'head'=4] {'dp'}, dimensions={2}, use_global_device_ids=true | all-gather | bytes 331776 | tf_op jit(solution)/shard_map/all_gather | solution.py:142
  618.5 37.6 %all-gather.13 = bf16[1,768,3,192]{3,2,0,1:T(4,128)(2,1)S(1)} all-gather(bf16[1,96,3,192]{3,2,0,1:T(4,128)(2,1)} %copy.279), channel_id=15, replica_groups=mesh['dp'=8,'head'=4] {'dp'}, dimensions={1}, use_global_device_ids=true | all-gather | bytes 995328 | tf_op jit(solution)/shard_map/all_gather | solution.py:141
  797.5 36.0 %fusion.1 = bf16[592,768]{1,0:T(8,128)(2,1)} fusion(bf16[2352,768]{1,0:T(8,128)(2,1)} %convolution_convert_fusion.2), kind=kCustom, calls=%all-reduce-scatter.1 | all-reduce-scatter fusion | flops 1818625 | bytes 4522496
  1092.4 35.5 %fusion.2 = bf16[592,768]{1,0:T(8,128)(2,1)S(1)} fusion(bf16[2352,768]{1,0:T(8,128)(2,1)} %convolution_convert_fusion.1), kind=kCustom, calls=%all-reduce-scatter.2 | all-reduce-scatter fusion | flops 1818625 | bytes 4522496
  1293.2 38.8 %fusion.3 = bf16[592,768]{1,0:T(8,128)(2,1)} fusion(bf16[2352,768]{1,0:T(8,128)(2,1)} %convolution_convert_fusion), kind=kCustom, calls=%all-reduce-scatter.3 | all-reduce-scatter fusion | flops 1818625 | bytes 4522496
  1375.3 149.4 %reduce-scatter.29.cloned.1.call-done = f32[96,3072]{1,0:T(8,128)} async-done(((f32[768,3072]{1,0:T(8,128)}), f32[96,3072]{1,0:T(8,128)}) %reduce-scatter.29.cloned.1.call-update) | async-done | bytes 1179664 | tf_op jit(solution)/shard_map/reduce_scatter | solution.py:322
  1527.0 163.9 %reduce-scatter.41.cloned.1.call-done = f32[3072,96]{0,1:T(8,128)} async-done(((f32[3072,768]{0,1:T(8,128)}), f32[3072,96]{0,1:T(8,128)}) %reduce-scatter.41.cloned.1.call-update) | async-done | bytes 1179664 | tf_op jit(solution)/shard_map/reduce_scatter | solution.py:323
  1700.9 54.8 %reduce-scatter.47.cloned.1.call-done = f32[96,192]{1,0:T(8,128)} async-done(((f32[768,192]{1,0:T(8,128)}), f32[96,192]{1,0:T(8,128)}) %reduce-scatter.47.cloned.1.call-update) | async-done | bytes 73744
  1756.7 165.5 %reduce-scatter.37.cloned.1.call-done = f32[3072,96]{0,1:T(8,128)} async-done(((f32[3072,768]{0,1:T(8,128)}), f32[3072,96]{0,1:T(8,128)}) %reduce-scatter.37.cloned.1.call-update) | async-done | bytes 1179664 | tf_op jit(solution)/shard_map/reduce_scatter | solution.py:323
  1927.6 126.2 %all-reduce.11.cloned.1.call-done = (f32[2,2,768]{2,1,0:T(2,128)}, f32[2,2,768]{2,1,0:T(2,128)}, f32[2,2,768]{2,1,0:T(2,128)}, f32[2,24,169]{2,0,1:T(2,128)}, f32[2,3072]{1,0:T(2,128)}, /*index=5*/f32[2,2,768]{2,1,0:T(2,128)}) async-done(((f32[2,2,768]{2,1,0:T(2,128)}, f32[2,2,768]{2,1,0:T(2,128)}, f32[2,2,768]{2,1,0:T(2,128)}, f32[2,24,169]{2,0,1:T(2,128)}, f32[2,3072]{1,0:T(2,128)}, ...) | async-done | bytes 106192 | tf_op jit(solution)/shard_map/psum | solution.py:350
  2061.7 57.9 %reduce-scatter.45.cloned.1.call-done = f32[96,192]{1,0:T(8,128)} async-done(((f32[768,192]{1,0:T(8,128)}), f32[96,192]{1,0:T(8,128)}) %reduce-scatter.45.cloned.1.call-update) | async-done | bytes 73744
  2121.3 69.6 %reduce-scatter.27.cloned.1.call-done = f32[96,3,192]{2,0,1:T(8,128)} async-done(((f32[768,3,192]{2,0,1:T(8,128)}), f32[96,3,192]{2,0,1:T(8,128)}) %reduce-scatter.27.cloned.1.call-update) | async-done | bytes 221200 | tf_op jit(solution)/shard_map/reduce_scatter | solution.py:320
  2191.0 71.4 %reduce-scatter.25.cloned.1.call-done = f32[96,3,192]{2,0,1:T(8,128)} async-done(((f32[768,3,192]{2,0,1:T(8,128)}), f32[96,3,192]{2,0,1:T(8,128)}) %reduce-scatter.25.cloned.1.call-update) | async-done | bytes 221200 | tf_op jit(solution)/shard_map/reduce_scatter | solution.py:320
  (592 shorter events, 942.9 us)
Async XLA Ops:
  7.2 325.3 %all-gather.43.cloned.1.call-start = ((), (), s32[]{:S(2)}) async-start(), calls=%async_computation.26 | async-start | bytes 4546560 | tf_op jit(solution)/shard_map/all_gather | solution.py:169
  87.2 372.9 %all-gather.35.cloned.1.call-start = ((), (), s32[]{:S(2)}) async-start(), calls=%async_computation.22 | async-start | bytes 5308416 | tf_op jit(solution)/shard_map/all_gather | solution.py:143
  95.9 387.3 %all-gather.37.cloned.1.call-start = ((), (), s32[]{:S(2)}) async-start(), calls=%async_computation.23 | async-start | bytes 5308416 | tf_op jit(solution)/shard_map/all_gather | solution.py:144
  108.3 552.8 %all-gather.45.cloned.1.call-start = ((), (), s32[]{:S(2)}) async-start(), calls=%async_computation.27 | async-start | bytes 4546560 | tf_op jit(solution)/shard_map/all_gather | solution.py:169
  420.1 33.3 %collective-permute-start = (bf16[12,768]{1,0:T(8,128)(2,1)S(1)}, bf16[12,768]{1,0:T(8,128)(2,1)S(1)}, u32[]{:S(2)}, u32[]{:S(2)}) collective-permute-start(bf16[12,768]{1,0:T(8,128)(2,1)S(1)} %slice.402), channel_id=1, source_target_pairs={{0,1},{1,2},{2,3},{4,5},{5,6},{6,7},{8,9},{9,10},{10,11},{12,13},{... | collective-permute-start | bytes 55304
  491.9 385.4 %all-gather.39.cloned.1.call-start = ((), (), s32[]{:S(2)}) async-start(), calls=%async_computation.24 | async-start | bytes 5308416 | tf_op jit(solution)/shard_map/all_gather | solution.py:143
  500.0 400.8 %all-gather.41.cloned.1.call-start = ((), (), s32[]{:S(2)}) async-start(), calls=%async_computation.25 | async-start | bytes 5308416 | tf_op jit(solution)/shard_map/all_gather | solution.py:144
  511.8 435.8 %all-gather.47.cloned.1.call-start = ((), (), s32[]{:S(2)}) async-start(), calls=%async_computation.28 | async-start | bytes 4546560 | tf_op jit(solution)/shard_map/all_gather | solution.py:266
  834.3 33.5 %collective-permute-start.1 = (bf16[12,768]{1,0:T(8,128)(2,1)S(1)}, bf16[12,768]{1,0:T(8,128)(2,1)S(1)}, u32[]{:S(2)}, u32[]{:S(2)}) collective-permute-start(bf16[12,768]{1,0:T(8,128)(2,1)S(1)} %slice.403), channel_id=1, source_target_pairs={{0,1},{1,2},{2,3},{4,5},{5,6},{6,7},{8,9},{9,10},{10,11},{12,13},{... | collective-permute-start | bytes 55304
  919.1 288.4 %all-gather.49.cloned.1.call-start = ((), (), s32[]{:S(2)}) async-start(), calls=%async_computation.29 | async-start | bytes 4546560 | tf_op jit(solution)/shard_map/all_gather | solution.py:266
  1156.1 217.0 %reduce-scatter.33.cloned.1.call-start = ((), (), s32[]{:S(2)}) async-start(), calls=%async_computation.16 | async-start | bytes 10616832 | tf_op jit(solution)/shard_map/reduce_scatter | solution.py:322
  1166.1 358.7 %reduce-scatter.29.cloned.1.call-start = ((), (), s32[]{:S(2)}) async-start(), calls=%async_computation.14 | async-start | bytes 10616832 | tf_op jit(solution)/shard_map/reduce_scatter | solution.py:322
  1177.5 513.4 %reduce-scatter.41.cloned.1.call-start = ((), (), s32[]{:S(2)}) async-start(), calls=%async_computation.20 | async-start | bytes 10616832 | tf_op jit(solution)/shard_map/reduce_scatter | solution.py:323
  1187.4 568.3 %reduce-scatter.47.cloned.1.call-start = ((), (), s32[]{:S(2)}) async-start(), calls=%async_computation.31 | async-start | bytes 884736
  1192.4 729.7 %reduce-scatter.37.cloned.1.call-start = ((), (), s32[]{:S(2)}) async-start(), calls=%async_computation.18 | async-start | bytes 10616832 | tf_op jit(solution)/shard_map/reduce_scatter | solution.py:323
  1202.3 851.6 %all-reduce.11.cloned.1.call-start = ((), (), s32[]{:S(2)}) async-start(), calls=%async_computation.32 | async-start | bytes 245760 | tf_op jit(solution)/shard_map/psum | solution.py:350
  1332.7 3.7 collective-permute-start.3
  1348.0 771.6 %reduce-scatter.45.cloned.1.call-start = ((), (), s32[]{:S(2)}) async-start(), calls=%async_computation.30 | async-start | bytes 884736
  1352.9 838.0 %reduce-scatter.27.cloned.1.call-start = ((), (), s32[]{:S(2)}) async-start(), calls=%async_computation.13 | async-start | bytes 2654208 | tf_op jit(solution)/shard_map/reduce_scatter | solution.py:320
  1363.5 898.9 %reduce-scatter.25.cloned.1.call-start = ((), (), s32[]{:S(2)}) async-start(), calls=%async_computation.12 | async-start | bytes 2654208 | tf_op jit(solution)/shard_map/reduce_scatter | solution.py:320
  1373.0 913.4 %reduce-scatter.35.cloned.1.call-start = ((), (), s32[]{:S(2)}) async-start(), calls=%async_computation.17 | async-start | bytes 737280 | tf_op jit(solution)/shard_map/reduce_scatter | solution.py:328
  1375.3 936.3 %reduce-scatter.31.cloned.1.call-start = ((), (), s32[]{:S(2)}) async-start(), calls=%async_computation.15 | async-start | bytes 737280 | tf_op jit(solution)/shard_map/reduce_scatter | solution.py:328
  1526.9 809.2 %reduce-scatter.43.cloned.1.call-start = ((), (), s32[]{:S(2)}) async-start(), calls=%async_computation.21 | async-start | bytes 737280 | tf_op jit(solution)/shard_map/reduce_scatter | solution.py:331
  1693.1 667.6 %reduce-scatter.39.cloned.1.call-start = ((), (), s32[]{:S(2)}) async-start(), calls=%async_computation.19 | async-start | bytes 737280 | tf_op jit(solution)/shard_map/reduce_scatter | solution.py:331
  (114 other events, 4485.7 us)
Sparse Core Ops, SparseCore 0:
  87.3 35.5 all-gather.42
  125.1 90.6 all-gather.34
  218.0 114.5 all-gather.36
  492.0 32.1 all-gather.44
  526.3 104.7 all-gather.38
  633.2 82.8 all-gather.40
  919.3 28.2 all-gather.46
  1156.2 35.3 all-gather.48
  1195.2 163.4 reduce-scatter.32
  1362.2 162.5 reduce-scatter.28
  1528.3 162.5 reduce-scatter.40
  1694.1 61.5 reduce-scatter.46
  1759.7 162.3 reduce-scatter.36
  1930.1 123.6 all-reduce.10
  2057.4 62.2 reduce-scatter.44
  2123.0 67.9 reduce-scatter.26
  2194.3 67.9 reduce-scatter.24
  2265.3 21.1 reduce-scatter.34
  2289.5 22.0 reduce-scatter.30
  2314.0 22.0 reduce-scatter.42
  2338.6 22.0 reduce-scatter.38
where the time goes:
time: 2380 us; the launch traced here: 2370 us
  waiting for transfers between devices  981 us (41%)
  blocking collectives  642 us (27%)
  local copies, waits for them, and re-layouts  356 us (15%)
  matrix products  257 us (11%)
  other arithmetic  110 us (5%)
    reduce_scatter x2, waiting for transfers between devices, shards(): lax.psum_scatter(fc2_grad, 'dp', scatter_dimension=1, tiled=True)  329 us
    reduce_scatter x2, waiting for transfers between devices, shards(): lax.psum_scatter(fc1_grad, 'dp', scatter_dimension=0, tiled=True)  149 us
    unnamed x4, blocking collectives  146 us
    reduce_scatter x2, waiting for transfers between devices, shards(): lax.psum_scatter(qkv_grad_matrix, 'dp', scatter_dimension=0, tiled=True)  141 us
    psum x1, waiting for transfers between devices, shards(): lax.psum((gain_terms, shift_terms, qv_terms, hidden_terms, bias_terms, ta...  126 us
    unnamed x27, waiting for transfers between devices  114 us
    dot_general x8, matrix products, matmul(): return jnp.dot(left, right, preferred_element_type=jnp.float32)  77.6 us
    all_gather x2, blocking collectives, shards(): lax.all_gather(qkv_weight[block], 'dp', axis=0, tiled=True)  76.9 us
  transfers between devices with their start and end apart: 25, of which 14 were waited for; matrix products, arithmetic and copies ran while one was open for 26% of the time, Pallas kernels for 0%

commit v1 on v0

v1 whole, which is shorter than its diff:
```python
import jax
import jax.numpy as jnp
from jax import lax
from jax.sharding import PartitionSpec as P

WSIDE = 7
SHIFT = 3
CROP_MAX = 12
BLOCKS = 2
WTOK = 49

EPSILON = 1e-05
MASKED = -100.0
BF16 = jnp.bfloat16
F32 = jnp.float32


def layer_norm(values, gain, shift):
    centre = jnp.mean(values, axis=-1, keepdims=True)
    centred = values - centre
    spread = jnp.mean(centred * centred, axis=-1, keepdims=True)
    return centred * lax.rsqrt(spread + EPSILON) * gain + shift


def matmul(left, right):
    return jnp.dot(left, right, preferred_element_type=F32)


def matmul_tn(left, right):
    return lax.dot_general(left, right, (((0,), (0,)), ((), ())), preferred_element_type=F32)


def matmul_nt(left, right):
    return lax.dot_general(left, right, (((1,), (1,)), ((), ())), preferred_element_type=F32)


def swap(values, axis, bit):
    size = lax.axis_size(axis)
    return lax.ppermute(values, axis, [(i, i ^ (1 << bit)) for i in range(size)])


def bit_of(axis, bit):
    return (lax.axis_index(axis) >> bit) & 1


def bits_in(axis):
    return lax.axis_size(axis).bit_length() - 1


def join(mine, other, axis, bit, dim):
    upper = bit_of(axis, bit) == 1
    return jnp.where(
        upper, jnp.stack([other, mine], axis=dim), jnp.stack([mine, other], axis=dim)
    )


def pick(values, index, dim):
    return lax.dynamic_index_in_dim(values, index, dim, keepdims=False)


def gather_rows(shard, late):
    rows, width = shard.shape
    held = shard[None]
    for bit in range(1, bits_in("dp")):
        held = join(held, swap(held, "dp", bit), "dp", bit, 0).reshape(-1, rows, width)
    if late:
        pair = [held, swap(held, "head", 1)]
        pair = [join(one, swap(one, "dp", 0), "dp", 0, 1) for one in pair]
    else:
        held = join(held, swap(held, "dp", 0), "dp", 0, 1)
        pair = [held, swap(held, "head", 1)]
    full = [pair[0], swap(pair[0], "head", 0), pair[1], swap(pair[1], "head", 0)]
    return [one.reshape(-1, width) for one in full]


def scatter_rows(pieces, late):
    width = pieces[0].shape[1]
    shards = lax.axis_size("dp")
    rows = pieces[0].shape[0] // shards

    def half(values, bit, dim):
        own = bit_of("dp", bit)
        kept = pick(values, own, dim)
        sent = pick(values, 1 - own, dim)
        return kept.astype(F32) + swap(sent.astype(BF16), "dp", bit).astype(F32)

    near = pieces[0].astype(F32) + swap(pieces[1].astype(BF16), "head", 0).astype(F32)
    far = pieces[2].astype(F32) + swap(pieces[3].astype(BF16), "head", 0).astype(F32)
    if late:
        near, far = [
            half(one.reshape(shards // 2, 2, rows, width), 0, 1) for one in (near, far)
        ]
        held = near + swap(far.astype(BF16), "head", 1).astype(F32)
    else:
        held = near + swap(far.astype(BF16), "head", 1).astype(F32)
        held = half(held.reshape(shards // 2, 2, rows, width), 0, 1)
    for bit in reversed(range(1, bits_in("dp"))):
        held = half(held.reshape(2, -1, rows, width), bit, 0)
    return held.reshape(rows, width)


def sum_all(values):
    for axis in ("head", "dp"):
        for bit in range(bits_in(axis)):
            values = values + swap(values, axis, bit)
    return values


def gather_small(values):
    held = values[None]
    for bit in range(bits_in("head")):
        held = join(held, swap(held, "head", bit), "head", bit, 0).reshape(-1, values.shape[0])
    held = held[None]
    for bit in range(bits_in("dp")):
        other = swap(held, "dp", bit)
        held = join(held, other, "dp", bit, 0).reshape((-1,) + held.shape[1:])
    return held


def attention_mask(pad, region):
    allowed = (pad[:, None, :] == 1) & (region[:, :, None] == region[:, None, :])
    return jnp.where(allowed, 0.0, MASKED).astype(F32)


def unshift(values):
    grid = values.reshape(values.shape[:-1] + (WSIDE, WSIDE))
    return jnp.roll(grid, (SHIFT, SHIFT), axis=(-2, -1)).reshape(values.shape)


def norm_back(values, gain, error):
    centre = jnp.mean(values, axis=-1, keepdims=True)
    centred = values - centre
    scale = lax.rsqrt(jnp.mean(centred * centred, axis=-1, keepdims=True) + EPSILON)
    normal = centred * scale
    flow = error * gain
    grad = (
        flow
        - jnp.mean(flow, axis=-1, keepdims=True)
        - normal * jnp.mean(flow * normal, axis=-1, keepdims=True)
    ) * scale
    return grad, jnp.sum(error * normal, axis=0), jnp.sum(error, axis=0)


def shards(
    tokens,
    cotangent,
    crop_counts,
    pad_mask,
    region_ids,
    rel_index,
    norm_gain,
    norm_shift,
    qkv_weight,
    qv_bias,
    bias_table,
    proj_weight,
    fc1_weight,
    fc1_bias,
    fc2_weight,
    out_bias,
):
    rows = tokens.shape[0]
    width = tokens.shape[1]
    wins = rows // WTOK
    local_width = qkv_weight.shape[3]
    local_heads = bias_table.shape[1]
    rel_count = bias_table.shape[2]
    dp_width = norm_gain.shape[2]
    dp_hidden = fc1_bias.shape[1]
    pieces = lax.axis_size("head")
    heads_total = local_heads * pieces
    head_dim = local_width // local_heads
    scale = head_dim ** (-0.5)
    head_index = lax.axis_index("head")
    dp_index = lax.axis_index("dp")
    relative = [head_index ^ e for e in range(pieces)]

    parts = []
    for block in range(BLOCKS):
        attn = jnp.concatenate(
            [qkv_weight[block].reshape(-1, 3 * local_width), proj_weight[block].T], axis=1
        )
        parts.append((attn, fc1_weight[block], fc2_weight[block].T))
    small = jnp.concatenate(
        [item.reshape(-1) for item in (norm_gain, norm_shift, qv_bias, out_bias, fc1_bias, bias_table)]
    )
    small = jnp.pad(small, (0, -small.shape[0] % 128))
    small_all = gather_small(small)
    weights_all = [
        [gather_rows(parts[block][kind], (block + kind) % 2 == 1) for kind in range(3)]
        for block in range(BLOCKS)
    ]
    offset = 0
    vectors = []
    for item in (norm_gain, norm_shift, qv_bias, out_bias):
        count = item.size
        piece = small_all[:, 0, offset : offset + count].reshape(-1, BLOCKS, 2, dp_width)
        vectors.append(piece.transpose(1, 2, 0, 3).reshape(BLOCKS, 2, width).astype(F32))
        offset += count
    gains, shifts, qv_all, out_all = vectors
    hidden_bias = small_all[:, 0, offset : offset + fc1_bias.size].reshape(-1, BLOCKS, dp_hidden)
    hidden_bias = hidden_bias.transpose(1, 0, 2).reshape(BLOCKS, pieces, -1).astype(F32)
    offset += fc1_bias.size
    tables = small_all[0, :, offset : offset + bias_table.size]
    tables = tables.reshape(pieces, BLOCKS, local_heads, rel_count)
    qv_pieces = qv_all.reshape(BLOCKS, 2, pieces, local_width)

    counts = jnp.repeat(crop_counts, CROP_MAX)
    slots = jnp.arange(pad_mask.shape[0], dtype=jnp.int32) % CROP_MAX
    live_all = (slots < counts).astype(F32)
    live_windows = lax.dynamic_slice_in_dim(live_all, head_index * wins, wins, 0)
    live = jnp.repeat(live_windows, WTOK)[:, None]
    pad = lax.dynamic_slice_in_dim(pad_mask, head_index * wins, wins, 0)
    region = unshift(lax.dynamic_slice_in_dim(region_ids, head_index * wins, wins, 0))
    masks = (attention_mask(pad, jnp.zeros_like(region)), attention_mask(pad, region))
    shifted_index = unshift(unshift(rel_index).T).T
    onehots = [
        (jnp.arange(rel_count, dtype=jnp.int32)[:, None] == index.reshape(1, -1)).astype(BF16)
        for index in (rel_index, shifted_index)
    ]

    kept = []
    residual = tokens.astype(F32)
    for block in range(BLOCKS):
        attn_w, fc1_w, fc2_w = weights_all[block]
        additive = masks[block % 2]
        normed = layer_norm(residual, gains[block, 0], shifts[block, 0]).astype(BF16)
        branch = 0.0
        saved_attn = []
        for e in range(pieces):
            rel = relative[e]
            qkv_w = attn_w[e][:, : 3 * local_width]
            proj_w = attn_w[e][:, 3 * local_width :]
            projected = matmul(normed, qkv_w)
            q_bias = pick(qv_pieces[block, 0], rel, 0)
            v_bias = pick(qv_pieces[block, 1], rel, 0)
            query = ((projected[:, :local_width] + q_bias) * scale).astype(BF16)
            key = projected[:, local_width : 2 * local_width].astype(BF16)
            value = (projected[:, 2 * local_width :] + v_bias).astype(BF16)
            query, key, value = [
                item.reshape(wins, WTOK, local_heads, head_dim) for item in (query, key, value)
            ]
            table = pick(tables[:, block], rel, 0)
            bias = matmul(table, onehots[block % 2]).reshape(local_heads, WTOK, WTOK)
            scores = jnp.einsum("wqhd,wkhd->whqk", query, key, preferred_element_type=F32)
            scores = scores + bias[None] + additive[:, None]
            peak = jnp.max(scores, axis=-1, keepdims=True)
            expo = jnp.exp(scores - peak)
            probs = (expo / jnp.sum(expo, axis=-1, keepdims=True)).astype(BF16)
            attended = jnp.einsum("whqk,wkhd->wqhd", probs, value, preferred_element_type=F32)
            attended = attended.reshape(rows, local_width).astype(BF16)
            branch = branch + matmul_nt(attended, proj_w)
            saved_attn.append((query, key, value, probs, attended))
        mixed = residual + live * (branch + out_all[block, 0])
        normed2 = layer_norm(mixed, gains[block, 1], shifts[block, 1]).astype(BF16)
        saved_mlp = []
        branch2 = 0.0
        for e in range(pieces):
            before = matmul(normed2, fc1_w[e]) + pick(hidden_bias[block], relative[e], 0)
            cdf = 0.5 * (1.0 + lax.erf(before * (0.5**0.5)))
            slope = cdf + before * jnp.exp(-0.5 * before * before) * 0.3989422804014327
            hidden = (before * cdf).astype(BF16)
            branch2 = branch2 + matmul_nt(hidden, fc2_w[e])
            saved_mlp.append((slope.astype(BF16), hidden))
        kept.append((residual, mixed, normed, normed2, saved_attn, saved_mlp))
        residual = mixed + live * (branch2 + out_all[block, 1])

    grad_rows = cotangent.astype(F32)
    shard_grads = [None] * BLOCKS
    small_sums = [None] * BLOCKS
    for block in reversed(range(BLOCKS)):
        attn_w, fc1_w, fc2_w = weights_all[block]
        block_input, mixed, normed, normed2, saved_attn, saved_mlp = kept[block]
        branch_grad = (live * grad_rows).astype(BF16)
        second_bias = jnp.sum(branch_grad, axis=0, dtype=F32)
        fc2_grads, fc1_grads, hidden_grads = [], [], []
        error2 = 0.0
        for e in range(pieces):
            slope, hidden = saved_mlp[e]
            fc2_grads.append(matmul_tn(branch_grad, hidden).astype(BF16))
            pre_grad = (slope * matmul(branch_grad, fc2_w[e])).astype(BF16)
            fc1_grads.append(matmul_tn(normed2, pre_grad).astype(BF16))
            hidden_grads.append(jnp.sum(pre_grad, axis=0, dtype=F32))
            error2 = error2 + matmul_nt(pre_grad, fc1_w[e])
        mixed_part, gain2, shift2 = norm_back(mixed, gains[block, 1], error2)
        mixed_grad = grad_rows + mixed_part
        attn_grad = (live * mixed_grad).astype(BF16)
        first_bias = jnp.sum(attn_grad, axis=0, dtype=F32)
        attn_grads = []
        q_grads, v_grads, table_grads = [], [], []
        error1 = 0.0
        for e in range(pieces):
            query, key, value, probs, attended = saved_attn[e]
            qkv_w = attn_w[e][:, : 3 * local_width]
            proj_w = attn_w[e][:, 3 * local_width :]
            proj_grad = matmul_tn(attn_grad, attended)
            grad_w = matmul(attn_grad, proj_w).astype(BF16)
            grad_w = grad_w.reshape(wins, WTOK, local_heads, head_dim)
            prob_grad = jnp.einsum("wqhd,wkhd->whqk", grad_w, value, preferred_element_type=F32)
            wide = probs.astype(F32)
            row_dot = jnp.sum(wide * prob_grad, axis=-1, keepdims=True)
            score_grad = (wide * (prob_grad - row_dot)).astype(BF16)
            score_total = jnp.sum(score_grad, axis=0, dtype=F32)
            table_grads.append(
                lax.dot_general(
                    score_total.reshape(local_heads, -1),
                    onehots[block % 2].astype(F32),
                    (((1,), (1,)), ((), ())),
                    precision=lax.Precision.HIGHEST,
                    preferred_element_type=F32,
                )
            )
            query_grad = scale * jnp.einsum(
                "whqk,wkhd->wqhd", score_grad, key, preferred_element_type=F32
            )
            key_grad = jnp.einsum(
                "whqk,wqhd->wkhd", score_grad, query, preferred_element_type=F32
            )
            value_grad = jnp.einsum("whqk,wqhd->wkhd", probs, grad_w, preferred_element_type=F32)
            qkv_grad = jnp.concatenate(
                [
                    item.astype(BF16).reshape(rows, local_width)
                    for item in (query_grad, key_grad, value_grad)
                ],
                axis=1,
            )
            sums = jnp.sum(qkv_grad, axis=0, dtype=F32)
            q_grads.append(sums[:local_width])
            v_grads.append(sums[2 * local_width :])
            attn_grads.append(
                jnp.concatenate([matmul_tn(normed, qkv_grad), proj_grad], axis=1).astype(BF16)
            )
            error1 = error1 + matmul_nt(qkv_grad, qkv_w)
        input_part, gain1, shift1 = norm_back(block_input, gains[block, 0], error1)
        grad_rows = mixed_grad + input_part
        shard_grads[block] = [
            scatter_rows(grads, (block + kind) % 2 == 1)
            for kind, grads in enumerate((attn_grads, fc1_grads, fc2_grads))
        ]

        def placed(items):
            whole = jnp.stack(items)
            return jnp.stack([pick(whole, relative[e], 0) for e in range(pieces)]).reshape(-1)

        small_sums[block] = sum_all(
            jnp.concatenate(
                [
                    gain1,
                    gain2,
                    shift1,
                    shift2,
                    placed(q_grads),
                    placed(v_grads),
                    first_bias,
                    second_bias,
                    placed(hidden_grads),
                    placed(table_grads),
                ]
            )
        )

    totals = jnp.stack(small_sums)

    def own(values):
        return lax.dynamic_slice_in_dim(values, dp_index * dp_width, dp_width, 2)

    small_grads = []
    for index in range(4):
        part = totals[:, 2 * index * width : 2 * (index + 1) * width]
        small_grads.append(own(part.reshape(BLOCKS, 2, width)))
    offset = 8 * width
    hidden_total = totals[:, offset : offset + pieces * fc1_weight.shape[2]]
    fc1_bias_grad = lax.dynamic_slice_in_dim(hidden_total, dp_index * dp_hidden, dp_hidden, 1)
    offset += hidden_total.shape[1]
    table_total = totals[:, offset:].reshape(BLOCKS, heads_total, rel_count)
    bias_table_grad = lax.dynamic_slice_in_dim(
        table_total, head_index * local_heads, local_heads, 1
    )
    qkv_weight_grad = jnp.stack(
        [item[0][:, : 3 * local_width].reshape(-1, 3, local_width) for item in shard_grads]
    )
    proj_weight_grad = jnp.stack([item[0][:, 3 * local_width :].T for item in shard_grads])
    fc1_weight_grad = jnp.stack([item[1] for item in shard_grads])
    fc2_weight_grad = jnp.stack([item[2].T for item in shard_grads])
    return (
        residual,
        grad_rows,
        small_grads[0],
        small_grads[1],
        qkv_weight_grad,
        small_grads[2],
        bias_table_grad,
        proj_weight_grad,
        fc1_weight_grad,
        fc1_bias_grad,
        fc2_weight_grad,
        small_grads[3],
    )


def solution(mesh):
    placed = (
        P(("dp", "head"), None),
        P(("dp", "head"), None),
        P("dp"),
        P("dp", None),
        P("dp", None),
        P(),
        P(None, None, "dp"),
        P(None, None, "dp"),
        P(None, "dp", None, "head"),
        P(None, None, "dp"),
        P(None, "head", None),
        P(None, "head", "dp"),
        P(None, "dp", "head"),
        P(None, "dp"),
        P(None, "head", "dp"),
        P(None, None, "dp"),
    )
    return jax.shard_map(
        shards,
        mesh=mesh,
        in_specs=placed,
        out_specs=(
            P(("dp", "head"), None),
            P(("dp", "head"), None),
            P(None, None, "dp"),
            P(None, None, "dp"),
            P(None, "dp", None, "head"),
            P(None, None, "dp"),
            P(None, "head", None),
            P(None, "head", "dp"),
            P(None, "dp", "head"),
            P(None, "dp"),
            P(None, "head", "dp"),
            P(None, None, "dp"),
        ),
        check_vma=False,
    )
```

time: 2380 us -> 1130 us (0.47)
  waiting for transfers between devices: 981 us -> 235 us
  blocking collectives: 642 us -> 0 us
  matrix products: 257 us -> 362 us
  starting transfers between devices: 6 us -> 76.3 us
  local copies, waits for them, and re-layouts: 356 us -> 301 us
  other arithmetic: 110 us -> 140 us
    reduce_scatter x10 -> x0, waiting for transfers between devices: 714 us -> none  [the longest x2 329 us: shards(): lax.psum_scatter(fc2_grad, 'dp', scatter_dimension=1, tiled=True)]
    all_gather x18 -> x0, blocking collectives: 495 us -> none  [the longest x2 76.9 us: shards(): lax.all_gather(qkv_weight[block], 'dp', axis=0, tiled=True)]
    ppermute x0 -> x93, waiting for transfers between devices: none -> 235 us  [swap(): return lax.ppermute(values, axis, [(i, i ^ 1 << bit) for i in range(size)])]
    unnamed x4 -> x0, blocking collectives: 146 us -> none
    psum x1 -> x0, waiting for transfers between devices: 126 us -> none  [shards(): lax.psum((gain_terms, shift_terms, qv_terms, hidden_terms, bias_terms, ta...]
    unnamed x27 -> x0, waiting for transfers between devices: 114 us -> none
    slice x39 -> x40, local copies, waits for them, and re-layouts: 83.9 us -> 7.2 us  [the longest x2 1.36 us: shards(): parts.append((attn, fc1_weight[block], fc2_weight[block].T))]
    ppermute x0 -> x93, starting transfers between devices: none -> 76.3 us  [swap(): return lax.ppermute(values, axis, [(i, i ^ 1 << bit) for i in range(size)])]
  transfers between devices with their start and end apart: 25 -> 93, of which waited for: 14 -> 33; matrix products, arithmetic and copies ran while one was open for 26% -> 43% of each run, Pallas kernels for 0% -> 0%
where the time goes in v1:
time: 1130 us; the launch traced here: 1120 us
  matrix products  362 us (32%)
  local copies, waits for them, and re-layouts  301 us (27%)
  waiting for transfers between devices  235 us (21%)
  other arithmetic  140 us (12%)
  starting transfers between devices  76.3 us (7%)
    ppermute x93, waiting for transfers between devices, swap(): return lax.ppermute(values, axis, [(i, i ^ 1 << bit) for i in range(size)])  235 us
    dot_general x32, matrix products, matmul_nt(): lax.dot_general(left, right, (((1,), (1,)), ((), ())), preferred_element_...  99.7 us
    dot_general x40, matrix products, matmul(): return jnp.dot(left, right, preferred_element_type=F32)  98.5 us
    ppermute x93, starting transfers between devices, swap(): return lax.ppermute(values, axis, [(i, i ^ 1 << bit) for i in range(size)])  76.3 us
    dot_general x32, matrix products, matmul_tn(): lax.dot_general(left, right, (((0,), (0,)), ((), ())), preferred_element_...  63.9 us
    unnamed x707, local copies, waits for them, and re-layouts  62.3 us
    select_n x34, other arithmetic, join(): jnp.where(upper, jnp.stack([other, mine], axis=dim), jnp.stack([mine, oth...  48.1 us
    reshape x24, local copies, waits for them, and re-layouts, shards(): item.reshape(wins, WTOK, local_heads, head_dim)  44.5 us
  transfers between devices with their start and end apart: 93, of which 33 were waited for; matrix products, arithmetic and copies ran while one was open for 43% of the time, Pallas kernels for 0%

profile of v1, /device:TPU:0, one launch (start us, length us, event | category | flops | bytes accessed | tf_op | source)
XLA Modules:
  0.0 1120.1 jit_solution(846516553018225782)
XLA Ops:
  105.0 5.3 collective-permute-done.6
  113.1 14.0 %collective-permute-done.12 = bf16[2,96,768]{1,2,0:T(8,128)(2,1)} collective-permute-done((bf16[2,96,768]{1,2,0:T(8,128)(2,1)}, bf16[2,96,768]{1,2,0:T(8,128)(2,1)}, u32[]{:S(2)}, u32[]{:S(2)}) %collective-permute-start.12) | collective-permute-done | bytes 294944 | tf_op jit(solution)/shard_map/ppermute | solution.py:39
  129.0 6.4 collective-permute-done.15
  143.8 4.3 collective-permute-done.25
  152.4 4.1 collective-permute-done.32
  197.7 17.0 %collective-permute-done.33 = bf16[4,96,768]{2,1,0:T(8,128)(2,1)S(1)} collective-permute-done((bf16[4,96,768]{2,1,0:T(8,128)(2,1)}, bf16[4,96,768]{2,1,0:T(8,128)(2,1)S(1)}, u32[]{:S(2)}, u32[]{:S(2)}) %collective-permute-start.33) | collective-permute-done | bytes 589856 | tf_op jit(solution)/shard_map/ppermute | solution.py:39
  230.4 9.6 collective-permute-done.29
  243.2 6.4 collective-permute-done.41
  313.9 4.1 multiply_convert_fusion.17
  372.0 3.9 fusion.551
  417.4 4.2 fusion.561
  462.8 4.1 convert_reduce_fusion.9
  585.3 5.5 multiply_reduce_fusion.1
  784.6 6.3 fusion.44
  902.9 25.9 %collective-permute-done.63 = bf16[4,96,768]{2,1,0:T(8,128)(2,1)} collective-permute-done((bf16[4,96,768]{2,1,0:T(8,128)(2,1)}, bf16[4,96,768]{2,1,0:T(8,128)(2,1)}, u32[]{:S(2)}, u32[]{:S(2)}) %collective-permute-start.63) | collective-permute-done | bytes 589856 | tf_op jit(solution)/shard_map/ppermute | solution.py:39
  933.2 8.1 collective-permute-done.61
  945.2 8.0 collective-permute-done.68
  954.0 29.1 %collective-permute-done.71 = bf16[4,96,768]{2,1,0:T(8,128)(2,1)S(1)} collective-permute-done((bf16[4,96,768]{2,1,0:T(8,128)(2,1)S(1)}, bf16[4,96,768]{2,1,0:T(8,128)(2,1)S(1)}, u32[]{:S(2)}, u32[]{:S(2)}) %collective-permute-start.71) | collective-permute-done | bytes 589856 | tf_op jit(solution)/shard_map/ppermute | solution.py:39
  992.7 15.8 %collective-permute-done.76 = bf16[768,768]{1,0:T(8,128)(2,1)} collective-permute-done((bf16[768,768]{1,0:T(8,128)(2,1)}, bf16[768,768]{1,0:T(8,128)(2,1)}, u32[]{:S(2)}, u32[]{:S(2)}) %collective-permute-start.76) | collective-permute-done | bytes 1179680 | tf_op jit(solution)/shard_map/ppermute | solution.py:39
  1013.5 18.9 %collective-permute-done.56 = bf16[768,768]{0,1:T(8,128)(2,1)} collective-permute-done((bf16[768,768]{0,1:T(8,128)(2,1)}, bf16[768,768]{0,1:T(8,128)(2,1)}, u32[]{:S(2)}, u32[]{:S(2)}) %collective-permute-start.56) | collective-permute-done | bytes 1179680 | tf_op jit(solution)/shard_map/ppermute | solution.py:39
  1075.8 16.1 %collective-permute-done.84 = bf16[2,96,768]{2,1,0:T(8,128)(2,1)} collective-permute-done((bf16[2,96,768]{2,1,0:T(8,128)(2,1)}, bf16[2,96,768]{2,1,0:T(8,128)(2,1)}, u32[]{:S(2)}, u32[]{:S(2)}) %collective-permute-start.84) | collective-permute-done | bytes 294944 | tf_op jit(solution)/shard_map/ppermute | solution.py:39
  1093.1 5.3 collective-permute-done.78
  1099.5 6.1 collective-permute-done.58
  1108.8 7.2 collective-permute-done.59
  (1506 shorter events, 878.9 us)
Async XLA Ops:
  59.7 50.6 %collective-permute-start.6 = (bf16[2,96,768]{1,2,0:T(8,128)(2,1)}, bf16[2,96,768]{1,2,0:T(8,128)(2,1)}, u32[]{:S(2)}, u32[]{:S(2)}) collective-permute-start(bf16[2,96,768]{1,2,0:T(8,128)(2,1)} %maximum_select_fusion.15), channel_id=1, source_target_pairs={{0,16},{4,20},{8,24},{12,28},{16,0},{20,4},{24,8},{28,12},{1,17},{... | collective-permute-start | bytes 884744 | tf_op jit(solution)/shard_map/ppermute | solution.py:39
  62.1 65.0 %collective-permute-start.12 = (bf16[2,96,768]{1,2,0:T(8,128)(2,1)}, bf16[2,96,768]{1,2,0:T(8,128)(2,1)}, u32[]{:S(2)}, u32[]{:S(2)}) collective-permute-start(bf16[2,96,768]{1,2,0:T(8,128)(2,1)} %maximum_select_fusion.17), channel_id=1, source_target_pairs={{0,16},{4,20},{8,24},{12,28},{16,0},{20,4},{24,8},{28,12},{1,17},{... | collective-permute-start | bytes 884744 | tf_op jit(solution)/shard_map/ppermute | solution.py:39
  67.2 68.2 %collective-permute-start.15 = (bf16[2,96,768]{1,2,0:T(8,128)(2,1)}, bf16[2,96,768]{1,2,0:T(8,128)(2,1)S(1)}, u32[]{:S(2)}, u32[]{:S(2)}) collective-permute-start(bf16[2,96,768]{1,2,0:T(8,128)(2,1)} %maximum_select_fusion.19), channel_id=1, source_target_pairs={{0,16},{4,20},{8,24},{12,28},{16,0},{20,4},{24,8},{28,12},{1,17},{... | collective-permute-start | bytes 884744 | tf_op jit(solution)/shard_map/ppermute | solution.py:39
  70.6 77.5 %collective-permute-start.25 = (bf16[2,96,768]{1,2,0:T(8,128)(2,1)}, bf16[2,96,768]{1,2,0:T(8,128)(2,1)}, u32[]{:S(2)}, u32[]{:S(2)}) collective-permute-start(bf16[2,96,768]{1,2,0:T(8,128)(2,1)} %maximum_select_fusion.21), channel_id=1, source_target_pairs={{0,16},{4,20},{8,24},{12,28},{16,0},{20,4},{24,8},{28,12},{1,17},{... | collective-permute-start | bytes 884744 | tf_op jit(solution)/shard_map/ppermute | solution.py:39
  75.6 81.0 %collective-permute-start.32 = (bf16[2,96,768]{1,2,0:T(8,128)(2,1)}, bf16[2,96,768]{1,2,0:T(8,128)(2,1)}, u32[]{:S(2)}, u32[]{:S(2)}) collective-permute-start(bf16[2,96,768]{1,2,0:T(8,128)(2,1)} %maximum_select_fusion.23), channel_id=1, source_target_pairs={{0,16},{4,20},{8,24},{12,28},{16,0},{20,4},{24,8},{28,12},{1,17},{... | collective-permute-start | bytes 884744 | tf_op jit(solution)/shard_map/ppermute | solution.py:39
  110.2 53.2 %collective-permute-start.35 = (bf16[2,96,768]{1,2,0:T(8,128)(2,1)}, bf16[2,96,768]{1,2,0:T(8,128)(2,1)}, u32[]{:S(2)}, u32[]{:S(2)}) collective-permute-start(bf16[2,96,768]{1,2,0:T(8,128)(2,1)} %maximum_select_fusion.25), channel_id=1, source_target_pairs={{0,16},{4,20},{8,24},{12,28},{16,0},{20,4},{24,8},{28,12},{1,17},{... | collective-permute-start | bytes 884744 | tf_op jit(solution)/shard_map/ppermute | solution.py:39
  190.8 61.8 %collective-permute-start.8 = (bf16[4,2,96,768]{3,2,1,0:T(8,128)(2,1)}, bf16[4,2,96,768]{3,2,1,0:T(8,128)(2,1)S(1)}, u32[]{:S(2)}, u32[]{:S(2)}) collective-permute-start(bf16[4,2,96,768]{3,2,1,0:T(8,128)(2,1)} %maximum_select_fusion), channel_id=1, source_target_pairs={{0,1},{1,0},{2,3},{3,2},{4,5},{5,4},{6,7},{7,6},{8,9},{9,8},{10,11... | collective-permute-start | bytes 3538952 | tf_op jit(solution)/shard_map/ppermute | solution.py:39
  217.3 50.5 %collective-permute-start.9 = (bf16[4,2,96,768]{3,2,1,0:T(8,128)(2,1)}, bf16[4,2,96,768]{3,2,1,0:T(8,128)(2,1)}, u32[]{:S(2)}, u32[]{:S(2)}) collective-permute-start(bf16[4,2,96,768]{3,2,1,0:T(8,128)(2,1)} %maximum_select_fusion), channel_id=1, source_target_pairs={{0,2},{1,3},{2,0},{3,1},{4,6},{5,7},{6,4},{7,5},{8,10},{9,11},{10,... | collective-permute-start | bytes 3538952 | tf_op jit(solution)/shard_map/ppermute | solution.py:39
  227.4 94.3 %collective-permute-start.18 = (bf16[4,2,96,768]{3,2,1,0:T(8,128)(2,1)}, bf16[4,2,96,768]{3,2,1,0:T(8,128)(2,1)}, u32[]{:S(2)}, u32[]{:S(2)}) collective-permute-start(bf16[4,2,96,768]{3,2,1,0:T(8,128)(2,1)} %maximum_select_fusion.2), channel_id=1, source_target_pairs={{0,1},{1,0},{2,3},{3,2},{4,5},{5,4},{6,7},{7,6},{8,9},{9,8},{10,11... | collective-permute-start | bytes 3538952 | tf_op jit(solution)/shard_map/ppermute | solution.py:39
  240.0 82.0 %collective-permute-start.21 = (bf16[4,2,96,768]{3,2,1,0:T(8,128)(2,1)}, bf16[4,2,96,768]{3,2,1,0:T(8,128)(2,1)}, u32[]{:S(2)}, u32[]{:S(2)}) collective-permute-start(bf16[4,2,96,768]{3,2,1,0:T(8,128)(2,1)} %maximum_select_fusion.2), channel_id=1, source_target_pairs={{0,2},{1,3},{2,0},{3,1},{4,6},{5,7},{6,4},{7,5},{8,10},{9,11},{10,... | collective-permute-start | bytes 3538952 | tf_op jit(solution)/shard_map/ppermute | solution.py:39
  249.6 63.8 %collective-permute-start.17 = (bf16[4,2,96,768]{3,2,1,0:T(8,128)(2,1)}, bf16[4,2,96,768]{3,2,1,0:T(8,128)(2,1)}, u32[]{:S(2)}, u32[]{:S(2)}) collective-permute-start(bf16[4,2,96,768]{3,2,1,0:T(8,128)(2,1)} %maximum_select_fusion.1), channel_id=1, source_target_pairs={{0,1},{1,0},{2,3},{3,2},{4,5},{5,4},{6,7},{7,6},{8,9},{9,8},{10,11... | collective-permute-start | bytes 3538952 | tf_op jit(solution)/shard_map/ppermute | solution.py:39
  252.6 180.1 %collective-permute-start.37 = (bf16[4,2,96,768]{3,2,1,0:T(8,128)(2,1)}, bf16[4,2,96,768]{3,2,1,0:T(8,128)(2,1)}, u32[]{:S(2)}, u32[]{:S(2)}) collective-permute-start(bf16[4,2,96,768]{3,2,1,0:T(8,128)(2,1)} %maximum_select_fusion.6), channel_id=1, source_target_pairs={{0,1},{1,0},{2,3},{3,2},{4,5},{5,4},{6,7},{7,6},{8,9},{9,8},{10,11... | collective-permute-start | bytes 3538952 | tf_op jit(solution)/shard_map/ppermute | solution.py:39
  321.7 117.8 %collective-permute-start.38 = (bf16[4,2,96,768]{3,2,1,0:T(8,128)(2,1)}, bf16[4,2,96,768]{3,2,1,0:T(8,128)(2,1)}, u32[]{:S(2)}, u32[]{:S(2)}) collective-permute-start(bf16[4,2,96,768]{3,2,1,0:T(8,128)(2,1)} %maximum_select_fusion.7), channel_id=1, source_target_pairs={{0,1},{1,0},{2,3},{3,2},{4,5},{5,4},{6,7},{7,6},{8,9},{9,8},{10,11... | collective-permute-start | bytes 3538952 | tf_op jit(solution)/shard_map/ppermute | solution.py:39
  332.6 76.2 %collective-permute-start.30 = (bf16[4,2,96,768]{3,2,1,0:T(8,128)(2,1)}, bf16[4,2,96,768]{3,2,1,0:T(8,128)(2,1)}, u32[]{:S(2)}, u32[]{:S(2)}) collective-permute-start(bf16[4,2,96,768]{3,2,1,0:T(8,128)(2,1)} %maximum_select_fusion.5), channel_id=1, source_target_pairs={{0,1},{1,0},{2,3},{3,2},{4,5},{5,4},{6,7},{7,6},{8,9},{9,8},{10,11... | collective-permute-start | bytes 3538952 | tf_op jit(solution)/shard_map/ppermute | solution.py:39
  335.6 127.2 %collective-permute-start.43 = (bf16[4,2,96,768]{3,2,1,0:T(8,128)(2,1)}, bf16[4,2,96,768]{3,2,1,0:T(8,128)(2,1)}, u32[]{:S(2)}, u32[]{:S(2)}) collective-permute-start(bf16[4,2,96,768]{3,2,1,0:T(8,128)(2,1)} %maximum_select_fusion.8), channel_id=1, source_target_pairs={{0,1},{1,0},{2,3},{3,2},{4,5},{5,4},{6,7},{7,6},{8,9},{9,8},{10,11... | collective-permute-start | bytes 3538952 | tf_op jit(solution)/shard_map/ppermute | solution.py:39
  339.5 121.1 %collective-permute-start.42 = (bf16[4,2,96,768]{3,2,1,0:T(8,128)(2,1)}, bf16[4,2,96,768]{3,2,1,0:T(8,128)(2,1)}, u32[]{:S(2)}, u32[]{:S(2)}) collective-permute-start(bf16[4,2,96,768]{3,2,1,0:T(8,128)(2,1)} %collective-permute-done.39), channel_id=1, source_target_pairs={{0,1},{1,0},{2,3},{3,2},{4,5},{5,4},{6,7},{7,6},{8,9},{9,8},{10,11... | collective-permute-start | bytes 3538952 | tf_op jit(solution)/shard_map/ppermute | solution.py:39
  769.0 90.0 %collective-permute-start.88 = (bf16[768,768]{1,0:T(8,128)(2,1)}, bf16[768,768]{1,0:T(8,128)(2,1)}, u32[]{:S(2)}, u32[]{:S(2)}) collective-permute-start(bf16[768,768]{1,0:T(8,128)(2,1)} %convolution_convert_fusion), channel_id=1, source_target_pairs={{0,1},{1,0},{2,3},{3,2},{4,5},{5,4},{6,7},{7,6},{8,9},{9,8},{10,11... | collective-permute-start | bytes 3538952 | tf_op jit(solution)/shard_map/ppermute | solution.py:39
  878.8 52.1 %collective-permute-start.87 = (bf16[4,96,768]{2,1,0:T(8,128)(2,1)}, bf16[4,96,768]{2,1,0:T(8,128)(2,1)}, u32[]{:S(2)}, u32[]{:S(2)}) collective-permute-start(bf16[4,96,768]{2,1,0:T(8,128)(2,1)} %fusion.208), channel_id=1, source_target_pairs={{0,4},{4,0},{8,12},{12,8},{16,20},{20,16},{24,28},{28,24},{1,5},{5... | collective-permute-start | bytes 1769480 | tf_op jit(solution)/shard_map/ppermute | solution.py:39
  883.8 47.2 %collective-permute-start.70 = (bf16[4,96,768]{2,1,0:T(8,128)(2,1)}, bf16[4,96,768]{2,1,0:T(8,128)(2,1)}, u32[]{:S(2)}, u32[]{:S(2)}) collective-permute-start(bf16[4,96,768]{2,1,0:T(8,128)(2,1)} %fusion.210), channel_id=1, source_target_pairs={{0,4},{4,0},{8,12},{12,8},{16,20},{20,16},{24,28},{28,24},{1,5},{5... | collective-permute-start | bytes 1769480 | tf_op jit(solution)/shard_map/ppermute | solution.py:39
  930.9 52.3 %collective-permute-start.80 = (bf16[768,768]{1,0:T(8,128)(2,1)S(1)}, bf16[768,768]{1,0:T(8,128)(2,1)S(1)}, u32[]{:S(2)}, u32[]{:S(2)}) collective-permute-start(bf16[768,768]{1,0:T(8,128)(2,1)S(1)} %copy-done.305), channel_id=1, source_target_pairs={{0,1},{1,0},{2,3},{3,2},{4,5},{5,4},{6,7},{7,6},{8,9},{9,8},{10,11... | collective-permute-start | bytes 3538952 | tf_op jit(solution)/shard_map/ppermute | solution.py:39
  953.2 55.3 %collective-permute-start.76 = (bf16[768,768]{1,0:T(8,128)(2,1)}, bf16[768,768]{1,0:T(8,128)(2,1)}, u32[]{:S(2)}, u32[]{:S(2)}) collective-permute-start(bf16[768,768]{1,0:T(8,128)(2,1)} %add_convert_fusion.1), channel_id=1, source_target_pairs={{0,2},{1,3},{2,0},{3,1},{4,6},{5,7},{6,4},{7,5},{8,10},{9,11},{10,... | collective-permute-start | bytes 3538952 | tf_op jit(solution)/shard_map/ppermute | solution.py:39
  983.3 49.2 %collective-permute-start.56 = (bf16[768,768]{0,1:T(8,128)(2,1)}, bf16[768,768]{0,1:T(8,128)(2,1)}, u32[]{:S(2)}, u32[]{:S(2)}) collective-permute-start(bf16[768,768]{0,1:T(8,128)(2,1)} %add_convert_fusion.2), channel_id=1, source_target_pairs={{0,2},{1,3},{2,0},{3,1},{4,6},{5,7},{6,4},{7,5},{8,10},{9,11},{10,... | collective-permute-start | bytes 3538952 | tf_op jit(solution)/shard_map/ppermute | solution.py:39
  986.4 52.8 %collective-permute-start.91 = (bf16[2,96,768]{2,1,0:T(8,128)(2,1)}, bf16[2,96,768]{2,1,0:T(8,128)(2,1)}, u32[]{:S(2)}, u32[]{:S(2)}) collective-permute-start(bf16[2,96,768]{2,1,0:T(8,128)(2,1)} %fusion.341), channel_id=1, source_target_pairs={{0,16},{4,20},{8,24},{12,28},{16,0},{20,4},{24,8},{28,12},{1,17},{... | collective-permute-start | bytes 884744 | tf_op jit(solution)/shard_map/ppermute | solution.py:39
  991.4 53.8 %collective-permute-start.72 = (bf16[2,96,768]{2,1,0:T(8,128)(2,1)S(1)}, bf16[2,96,768]{2,1,0:T(8,128)(2,1)}, u32[]{:S(2)}, u32[]{:S(2)}) collective-permute-start(bf16[2,96,768]{2,1,0:T(8,128)(2,1)S(1)} %fusion.338), channel_id=1, source_target_pairs={{0,16},{4,20},{8,24},{12,28},{16,0},{20,4},{24,8},{28,12},{1,17},{... | collective-permute-start | bytes 884744 | tf_op jit(solution)/shard_map/ppermute | solution.py:39
  (398 other events, 3996.3 us)

commit v2 on v1

v2 whole, which is shorter than its diff:
```python
import functools

import jax
import jax.numpy as jnp
from jax import lax
from jax.experimental import pallas as pl
from jax.experimental.pallas import tpu as pltpu
from jax.sharding import PartitionSpec as P

WSIDE = 7
SHIFT = 3
CROP_MAX = 12
BLOCKS = 2
WTOK = 49
PADDED = 56
PIECES = 4

EPSILON = 1e-05
MASKED = -100.0
ABSENT = -1e30
BF16 = jnp.bfloat16
F32 = jnp.float32


def dot(left, right, left_dim=1, right_dim=0):
    return lax.dot_general(
        left, right, (((left_dim,), (right_dim,)), ((), ())), preferred_element_type=F32
    )


def normalize(values):
    centred = values - jnp.mean(values, axis=-1, keepdims=True)
    scale = lax.rsqrt(jnp.mean(centred * centred, axis=-1, keepdims=True) + EPSILON)
    return centred * scale, scale


def spread_heads(values, heads):
    columns = values.shape[1]
    owner = lax.broadcasted_iota(jnp.int32, values.shape, 1) // (columns // heads)
    return jnp.concatenate(
        [jnp.where(owner == head, values, 0.0) for head in range(heads)], axis=0
    ).astype(BF16)


def merge_heads(values, heads):
    rows = values.shape[0] // heads
    columns = values.shape[1]
    owner = lax.broadcasted_iota(jnp.int32, (rows, columns), 1) // (columns // heads)
    total = values[:rows]
    for head in range(1, heads):
        total = jnp.where(owner == head, values[head * rows : (head + 1) * rows], total)
    return total


def attention_forward_kernel(
    heads,
    scale,
    x_ref,
    w0,
    w1,
    w2,
    w3,
    vec_ref,
    qv_ref,
    bias_ref,
    mask_ref,
    live_ref,
    mixed_ref,
    normed_ref,
    normed2_ref,
    q_ref,
    k_ref,
    v_ref,
    p_ref,
    att_ref,
    qs,
    ks,
    vs,
    atts,
):
    rows = x_ref.shape[0]
    columns = q_ref.shape[2]
    wins = rows // PADDED
    chunk = 2 * PADDED
    weights = (w0, w1, w2, w3)

    def first_norm(step, _):
        span = pl.ds(pl.multiple_of(step * chunk, chunk), chunk)
        normal, _ = normalize(x_ref[span, :])
        normed_ref[span, :] = (normal * vec_ref[0:1, :] + vec_ref[1:2, :]).astype(BF16)
        return 0

    lax.fori_loop(0, rows // chunk, first_norm, 0)
    for e in range(PIECES):
        qkv = dot(normed_ref[...], weights[e][:, : 3 * columns])
        query = ((qkv[:, :columns] + qv_ref[e, 0:1, :]) * scale).astype(BF16)
        key = qkv[:, columns : 2 * columns].astype(BF16)
        value = (qkv[:, 2 * columns :] + qv_ref[e, 1:2, :]).astype(BF16)
        q_ref[e] = query
        k_ref[e] = key
        v_ref[e] = value
        qs[e] = query.astype(F32)
        ks[e] = key.astype(F32)
        vs[e] = value.astype(F32)

    def window(w, _):
        span = pl.ds(pl.multiple_of(w * PADDED, PADDED), PADDED)
        mask = mask_ref[w]
        for e in range(PIECES):
            keys = spread_heads(ks[e, span, :], heads)
            scores = dot(keys, qs[e, span, :].astype(BF16), 1, 1) + bias_ref[e]
            scores = scores.reshape(heads, PADDED, PADDED) + mask[None]
            expo = jnp.exp(scores - jnp.max(scores, axis=1, keepdims=True))
            probs = expo * (1.0 / jnp.sum(expo, axis=1, keepdims=True))
            probs = probs.reshape(heads * PADDED, PADDED)
            p_ref[e, w] = probs.astype(BF16)
            values = spread_heads(vs[e, span, :], heads)
            atts[e, span, :] = dot(probs.T.astype(BF16), values)
        return 0

    lax.fori_loop(0, wins, window, 0)
    branch = None
    for e in range(PIECES):
        attended = atts[e].astype(BF16)
        att_ref[e] = attended
        part = dot(attended, weights[e][:, 3 * columns :], 1, 1)
        branch = part if branch is None else branch + part
    mixed_ref[...] = branch

    def second_norm(step, _):
        span = pl.ds(pl.multiple_of(step * chunk, chunk), chunk)
        mixed = x_ref[span, :] + live_ref[span, :] * (mixed_ref[span, :] + vec_ref[2:3, :])
        mixed_ref[span, :] = mixed
        normal, _ = normalize(mixed)
        normed2_ref[span, :] = (normal * vec_ref[3:4, :] + vec_ref[4:5, :]).astype(BF16)
        return 0

    lax.fori_loop(0, rows // chunk, second_norm, 0)


def attention_forward(x, weights, vectors, qv, bias, mask, live, heads, scale):
    rows, width = x.shape
    columns = qv.shape[2]
    wins = rows // PADDED
    shape = jax.ShapeDtypeStruct
    return pl.pallas_call(
        functools.partial(attention_forward_kernel, heads, scale),
        out_shape=(
            shape((rows, width), F32),
            shape((rows, width), BF16),
            shape((rows, width), BF16),
            shape((PIECES, rows, columns), BF16),
            shape((PIECES, rows, columns), BF16),
            shape((PIECES, rows, columns), BF16),
            shape((PIECES, wins, heads * PADDED, PADDED), BF16),
            shape((PIECES, rows, columns), BF16),
        ),
        scratch_shapes=[pltpu.VMEM((PIECES, rows, columns), F32)] * 4,
        compiler_params=pltpu.CompilerParams(vmem_limit_bytes=60 * 2**20),
        cost_estimate=pl.CostEstimate(
            flops=int(2.5e9 * 1.3), bytes_accessed=30_000_000, transcendentals=2_000_000
        ),
        name="attention_forward",
    )(x, *weights, vectors, qv, bias, mask, live)


def ffn_forward_kernel(
    mixed_ref, normed2_ref, a0, a1, a2, a3, b0, b1, b2, b3, bias_ref, vec_ref, live_ref,
    out_ref, hidden_ref, slope_ref,
):
    rows = mixed_ref.shape[0]
    chunk = 2 * PADDED
    first = (a0, a1, a2, a3)
    second = (b0, b1, b2, b3)
    for e in range(PIECES):
        hidden_ref[e] = jnp.zeros(hidden_ref.shape[1:], BF16)
    total = None
    for e in range(PIECES):
        before = dot(normed2_ref[...], first[e][...]) + bias_ref[e]
        cdf = 0.5 * (1.0 + lax.erf(before * (0.5**0.5)))
        density = jnp.exp(-0.5 * before * before) * 0.3989422804014327
        hidden_ref[e] = (before * cdf).astype(BF16)
        slope_ref[e] = (cdf + before * density).astype(BF16)
        part = dot(hidden_ref[e], second[e][...], 1, 1)
        total = part if total is None else total + part
    out_ref[...] = total

    def finish(step, _):
        span = pl.ds(pl.multiple_of(step * chunk, chunk), chunk)
        out_ref[span, :] = mixed_ref[span, :] + live_ref[span, :] * (
            out_ref[span, :] + vec_ref[5:6, :]
        )
        return 0

    lax.fori_loop(0, rows // chunk, finish, 0)


def ffn_forward(mixed, normed2, first, second, bias, vectors, live):
    rows, width = mixed.shape
    shape = jax.ShapeDtypeStruct
    return pl.pallas_call(
        ffn_forward_kernel,
        out_shape=(
            shape((rows, width), F32),
            shape((PIECES, rows, width), BF16),
            shape((PIECES, rows, width), BF16),
        ),
        compiler_params=pltpu.CompilerParams(vmem_limit_bytes=60 * 2**20),
        name="ffn_forward",
    )(mixed, normed2, *first, *second, bias, vectors, live)


def norm_back_rows(values, gain, error):
    normal, scale = normalize(values)
    flow = error * gain
    grad = (
        flow
        - jnp.mean(flow, axis=-1, keepdims=True)
        - normal * jnp.mean(flow * normal, axis=-1, keepdims=True)
    ) * scale
    return grad, jnp.sum(error * normal, axis=0, keepdims=True), jnp.sum(error, axis=0, keepdims=True)


def ffn_backward_kernel(
    grad_ref, mixed_ref, slope_ref, a0, a1, a2, a3, b0, b1, b2, b3, vec_ref, live_ref,
    branch_ref, pre_ref, mixed_grad_ref, attn_grad_ref, small_ref, hidden_bias_ref,
):
    rows, width = grad_ref.shape
    chunk = 2 * PADDED
    first = (a0, a1, a2, a3)
    second = (b0, b1, b2, b3)

    def start(step, total):
        span = pl.ds(pl.multiple_of(step * chunk, chunk), chunk)
        branch = (live_ref[span, :] * grad_ref[span, :]).astype(BF16)
        branch_ref[span, :] = branch
        return total + jnp.sum(branch.astype(F32), axis=0, keepdims=True)

    zero = jnp.zeros((1, width), F32)
    small_ref[3:4, :] = lax.fori_loop(0, rows // chunk, start, zero)
    error = None
    for e in range(PIECES):
        flow = dot(branch_ref[...], second[e][...])
        pre = (slope_ref[e].astype(F32) * flow).astype(BF16)
        pre_ref[e] = pre
        hidden_bias_ref[e] = jnp.sum(pre.astype(F32), axis=0, keepdims=True)
        part = dot(pre_ref[e], first[e][...], 1, 1)
        error = part if error is None else error + part
    mixed_grad_ref[...] = error

    def finish(step, totals):
        span = pl.ds(pl.multiple_of(step * chunk, chunk), chunk)
        back, gain_part, shift_part = norm_back_rows(
            mixed_ref[span, :], vec_ref[3:4, :], mixed_grad_ref[span, :]
        )
        mixed_grad = grad_ref[span, :] + back
        mixed_grad_ref[span, :] = mixed_grad
        attn_grad = (live_ref[span, :] * mixed_grad).astype(BF16)
        attn_grad_ref[span, :] = attn_grad
        bias_part = jnp.sum(attn_grad.astype(F32), axis=0, keepdims=True)
        return tuple(a + b for a, b in zip(totals, (gain_part, shift_part, bias_part)))

    totals = lax.fori_loop(0, rows // chunk, finish, (zero, zero, zero))
    for index in range(3):
        small_ref[index : index + 1, :] = totals[index]


def ffn_backward(grad, mixed, slope, first, second, vectors, live):
    rows, width = grad.shape
    shape = jax.ShapeDtypeStruct
    return pl.pallas_call(
        ffn_backward_kernel,
        out_shape=(
            shape((rows, width), BF16),
            shape((PIECES, rows, width), BF16),
            shape((rows, width), F32),
            shape((rows, width), BF16),
            shape((8, width), F32),
            shape((PIECES, 1, width), F32),
        ),
        compiler_params=pltpu.CompilerParams(vmem_limit_bytes=60 * 2**20),
        name="ffn_backward",
    )(grad, mixed, slope, *first, *second, vectors, live)


def weight_grad_kernel(picks, left_ref, right_ref, *refs):
    added, outs = refs[: len(refs) - len(picks)], refs[len(refs) - len(picks) :]
    for index, e in enumerate(picks):
        value = dot(left_ref[...], right_ref[e], 0, 0)
        if added:
            value = value + added[index][...].astype(F32)
        outs[index][...] = value.astype(BF16)


def weight_grad(left, right, picks, added=()):
    width = left.shape[1]
    shape = jax.ShapeDtypeStruct
    return pl.pallas_call(
        functools.partial(weight_grad_kernel, picks),
        out_shape=tuple(shape((width, right.shape[2]), BF16) for _ in picks),
        compiler_params=pltpu.CompilerParams(vmem_limit_bytes=60 * 2**20),
        name="weight_grad",
    )(left, right, *added)


def attn_weight_grad_kernel(picks, left_ref, right_ref, left2_ref, right2_ref, *refs):
    added, outs = refs[: len(refs) - len(picks)], refs[len(refs) - len(picks) :]
    for index, e in enumerate(picks):
        value = jnp.concatenate(
            [
                dot(left_ref[...], right_ref[e], 0, 0),
                dot(left2_ref[...], right2_ref[e], 0, 0),
            ],
            axis=1,
        )
        if added:
            value = value + added[index][...].astype(F32)
        outs[index][...] = value.astype(BF16)


def attn_weight_grad(normed, qkv_grad, attn_grad, attended, picks, added=()):
    width = normed.shape[1]
    shape = jax.ShapeDtypeStruct
    return pl.pallas_call(
        functools.partial(attn_weight_grad_kernel, picks),
        out_shape=tuple(shape((width, width), BF16) for _ in picks),
        compiler_params=pltpu.CompilerParams(vmem_limit_bytes=60 * 2**20),
        name="attn_weight_grad",
    )(normed, qkv_grad, attn_grad, attended, *added)


def attention_backward_kernel(
    heads, scale,
    x_ref, mixed_grad_ref, attn_grad_ref, w0, w1, w2, w3, q_ref, k_ref, v_ref, p_ref, vec_ref,
    grad_ref, qkv_grad_ref, bias_grad_ref, small_ref, qv_grad_ref,
    qs, ks, vs, gs, qkvs,
):
    rows, width = x_ref.shape
    columns = q_ref.shape[2]
    wins = rows // PADDED
    chunk = 2 * PADDED
    weights = (w0, w1, w2, w3)
    for e in range(PIECES):
        gs[e] = dot(attn_grad_ref[...], weights[e][:, 3 * columns :]).astype(BF16).astype(F32)
        qs[e] = q_ref[e].astype(F32)
        ks[e] = k_ref[e].astype(F32)
        vs[e] = v_ref[e].astype(F32)
    bias_grad_ref[...] = jnp.zeros(bias_grad_ref.shape, F32)

    def window(w, _):
        span = pl.ds(pl.multiple_of(w * PADDED, PADDED), PADDED)
        for e in range(PIECES):
            keys = spread_heads(ks[e, span, :], heads)
            values = spread_heads(vs[e, span, :], heads)
            query = qs[e, span, :].astype(BF16)
            grads = gs[e, span, :].astype(BF16)
            low = p_ref[e, w]
            probs = low.astype(F32)
            flow = dot(values, grads, 1, 1)
            inner = jnp.sum((probs * flow).reshape(heads, PADDED, PADDED), axis=1, keepdims=True)
            score = probs.reshape(heads, PADDED, PADDED) * (
                flow.reshape(heads, PADDED, PADDED) - inner
            )
            score = score.reshape(heads * PADDED, PADDED).astype(BF16)
            wide = score.astype(F32)
            bias_grad_ref[e] += wide
            qkvs[e, span, :columns] = dot(wide.T.astype(BF16), keys) * scale
            qkvs[e, span, columns : 2 * columns] = merge_heads(dot(score, query), heads)
            qkvs[e, span, 2 * columns :] = merge_heads(dot(low, grads), heads)
        return 0

    lax.fori_loop(0, wins, window, 0)
    error = None
    for e in range(PIECES):
        qkv_grad_ref[e] = qkvs[e].astype(BF16)
        qv_grad_ref[e] = jnp.sum(qkv_grad_ref[e].astype(F32), axis=0, keepdims=True)
        part = dot(qkv_grad_ref[e], weights[e][:, : 3 * columns], 1, 1)
        error = part if error is None else error + part
    grad_ref[...] = error
    zero = jnp.zeros((1, width), F32)

    def finish(step, totals):
        span = pl.ds(pl.multiple_of(step * chunk, chunk), chunk)
        back, gain_part, shift_part = norm_back_rows(
            x_ref[span, :], vec_ref[0:1, :], grad_ref[span, :]
        )
        grad_ref[span, :] = mixed_grad_ref[span, :] + back
        return totals[0] + gain_part, totals[1] + shift_part

    totals = lax.fori_loop(0, rows // chunk, finish, (zero, zero))
    for index in range(2):
        small_ref[index : index + 1, :] = totals[index]


def attention_backward(x, mixed_grad, attn_grad, weights, query, key, value, probs, vectors, heads, scale):
    rows, width = x.shape
    columns = query.shape[2]
    shape = jax.ShapeDtypeStruct
    return pl.pallas_call(
        functools.partial(attention_backward_kernel, heads, scale),
        out_shape=(
            shape((rows, width), F32),
            shape((PIECES, rows, 3 * columns), BF16),
            shape((PIECES, heads * PADDED, PADDED), F32),
            shape((8, width), F32),
            shape((PIECES, 1, 3 * columns), F32),
        ),
        scratch_shapes=[pltpu.VMEM((PIECES, rows, columns), F32)] * 4
        + [pltpu.VMEM((PIECES, rows, 3 * columns), F32)],
        compiler_params=pltpu.CompilerParams(vmem_limit_bytes=60 * 2**20),
        name="attention_backward",
    )(x, mixed_grad, attn_grad, *weights, query, key, value, probs, vectors)


def swap(values, axis, bit):
    size = lax.axis_size(axis)
    return lax.ppermute(values, axis, [(i, i ^ (1 << bit)) for i in range(size)])


def bit_of(axis, bit):
    return (lax.axis_index(axis) >> bit) & 1


def bits_in(axis):
    return lax.axis_size(axis).bit_length() - 1


def join(mine, other, axis, bit, dim):
    upper = bit_of(axis, bit) == 1
    return jnp.where(
        upper, jnp.stack([other, mine], axis=dim), jnp.stack([mine, other], axis=dim)
    )


def pick(values, index, dim):
    return lax.dynamic_index_in_dim(values, index, dim, keepdims=False)


def gather_rows(shard, late):
    rows, width = shard.shape
    held = shard[None]
    for bit in range(1, bits_in("dp")):
        held = join(held, swap(held, "dp", bit), "dp", bit, 0).reshape(-1, rows, width)
    if late:
        pair = [held, swap(held, "head", 1)]
        pair = [join(one, swap(one, "dp", 0), "dp", 0, 1) for one in pair]
    else:
        held = join(held, swap(held, "dp", 0), "dp", 0, 1)
        pair = [held, swap(held, "head", 1)]
    full = [pair[0], swap(pair[0], "head", 0), pair[1], swap(pair[1], "head", 0)]
    return [one.reshape(-1, width) for one in full]


def scatter_rows(make, late):
    shards = lax.axis_size("dp")

    def half(values, bit, dim):
        own = bit_of("dp", bit)
        kept = pick(values, own, dim)
        sent = pick(values, 1 - own, dim)
        return kept.astype(F32) + swap(sent.astype(BF16), "dp", bit).astype(F32)

    away = make((1, 3))
    near, far = make((0, 2), [swap(one, "head", 0) for one in away])
    width = near.shape[1]
    rows = near.shape[0] // shards
    if late:
        near, far = [
            half(one.reshape(shards // 2, 2, rows, width), 0, 1) for one in (near, far)
        ]
        held = near + swap(far.astype(BF16), "head", 1).astype(F32)
    else:
        held = near.astype(F32) + swap(far, "head", 1).astype(F32)
        held = half(held.reshape(shards // 2, 2, rows, width), 0, 1)
    for bit in reversed(range(1, bits_in("dp"))):
        held = half(held.reshape(2, -1, rows, width), bit, 0)
    return held.reshape(rows, width)


def sum_all(values):
    for axis in ("head", "dp"):
        for bit in range(bits_in(axis)):
            values = values + swap(values, axis, bit)
    return values


def gather_small(values):
    held = values[None]
    for bit in range(bits_in("head")):
        held = join(held, swap(held, "head", bit), "head", bit, 0).reshape(-1, values.shape[0])
    held = held[None]
    for bit in range(bits_in("dp")):
        other = swap(held, "dp", bit)
        held = join(held, other, "dp", bit, 0).reshape((-1,) + held.shape[1:])
    return held


def unshift(values):
    grid = values.reshape(values.shape[:-1] + (WSIDE, WSIDE))
    return jnp.roll(grid, (SHIFT, SHIFT), axis=(-2, -1)).reshape(values.shape)


def pad_rows(values):
    grid = values.reshape(-1, WTOK, values.shape[1])
    grid = jnp.pad(grid, ((0, 0), (0, PADDED - WTOK), (0, 0)))
    return grid.reshape(-1, values.shape[1])


def drop_rows(values):
    grid = values.reshape(-1, PADDED, values.shape[1])[:, :WTOK]
    return grid.reshape(-1, values.shape[1])


def attention_mask(pad, region):
    allowed = (pad[:, :, None] == 1) & (region[:, :, None] == region[:, None, :])
    mask = jnp.where(allowed, 0.0, MASKED).astype(F32)
    extra = PADDED - WTOK
    mask = jnp.pad(mask, ((0, 0), (0, 0), (0, extra)))
    return jnp.pad(mask, ((0, 0), (0, extra), (0, 0)), constant_values=ABSENT)


def shards(
    tokens,
    cotangent,
    crop_counts,
    pad_mask,
    region_ids,
    rel_index,
    norm_gain,
    norm_shift,
    qkv_weight,
    qv_bias,
    bias_table,
    proj_weight,
    fc1_weight,
    fc1_bias,
    fc2_weight,
    out_bias,
):
    rows = tokens.shape[0]
    width = tokens.shape[1]
    wins = rows // WTOK
    local_width = qkv_weight.shape[3]
    local_heads = bias_table.shape[1]
    rel_count = bias_table.shape[2]
    dp_width = norm_gain.shape[2]
    dp_hidden = fc1_bias.shape[1]
    pieces = lax.axis_size("head")
    heads_total = local_heads * pieces
    head_dim = local_width // local_heads
    scale = head_dim ** (-0.5)
    head_index = lax.axis_index("head")
    dp_index = lax.axis_index("dp")
    relative = [head_index ^ e for e in range(pieces)]

    parts = []
    for block in range(BLOCKS):
        attn = jnp.concatenate(
            [qkv_weight[block].reshape(-1, 3 * local_width), proj_weight[block].T], axis=1
        )
        parts.append((attn, fc1_weight[block], fc2_weight[block].T))
    small = jnp.concatenate(
        [item.reshape(-1) for item in (norm_gain, norm_shift, qv_bias, out_bias, fc1_bias, bias_table)]
    )
    small = jnp.pad(small, (0, -small.shape[0] % 128))
    small_all = gather_small(small)
    weights_all = [
        [gather_rows(parts[block][kind], (block + kind) % 2 == 1) for kind in range(3)]
        for block in range(BLOCKS)
    ]
    offset = 0
    vectors = []
    for item in (norm_gain, norm_shift, qv_bias, out_bias):
        count = item.size
        piece = small_all[:, 0, offset : offset + count].reshape(-1, BLOCKS, 2, dp_width)
        vectors.append(piece.transpose(1, 2, 0, 3).reshape(BLOCKS, 2, width).astype(F32))
        offset += count
    gains, shifts, qv_all, out_all = vectors
    hidden_bias = small_all[:, 0, offset : offset + fc1_bias.size].reshape(-1, BLOCKS, dp_hidden)
    hidden_bias = hidden_bias.transpose(1, 0, 2).reshape(BLOCKS, pieces, -1).astype(F32)
    offset += fc1_bias.size
    tables = small_all[0, :, offset : offset + bias_table.size]
    tables = tables.reshape(pieces, BLOCKS, local_heads, rel_count)
    qv_pieces = qv_all.reshape(BLOCKS, 2, pieces, local_width)

    counts = jnp.repeat(crop_counts, CROP_MAX)
    slots = jnp.arange(pad_mask.shape[0], dtype=jnp.int32) % CROP_MAX
    live_all = (slots < counts).astype(F32)
    live_windows = lax.dynamic_slice_in_dim(live_all, head_index * wins, wins, 0)
    real = (jnp.arange(PADDED) < WTOK).astype(F32)
    live = (live_windows[:, None] * real[None, :]).reshape(-1, 1)
    pad = lax.dynamic_slice_in_dim(pad_mask, head_index * wins, wins, 0)
    region = unshift(lax.dynamic_slice_in_dim(region_ids, head_index * wins, wins, 0))
    masks = (attention_mask(pad, jnp.zeros_like(region)), attention_mask(pad, region))
    extra = PADDED - WTOK
    onehots = []
    for index in (rel_index, unshift(unshift(rel_index).T).T):
        by_key = jnp.pad(index.T, ((0, extra), (0, extra)), constant_values=-1).reshape(1, -1)
        ids = jnp.arange(rel_count, dtype=jnp.int32)[:, None]
        onehots.append((ids == by_key).astype(BF16))

    def ordered(values, dim):
        return jnp.stack([pick(values, rel, dim) for rel in relative])

    block_rows = local_heads * PADDED
    vectors, qv, biases, hidden_biases = [], [], [], []
    for block in range(BLOCKS):
        rows8 = [
            gains[block, 0],
            shifts[block, 0],
            out_all[block, 0],
            gains[block, 1],
            shifts[block, 1],
            out_all[block, 1],
        ]
        vectors.append(jnp.pad(jnp.stack(rows8), ((0, 2), (0, 0))))
        qv.append(ordered(qv_pieces[block], 1))
        table = ordered(tables[:, block], 0).reshape(heads_total, rel_count)
        bias = jnp.dot(table, onehots[block % 2], preferred_element_type=F32)
        biases.append(bias.reshape(pieces, block_rows, PADDED))
        hidden_biases.append(ordered(hidden_bias[block], 0)[:, None, :])

    kept = []
    residual = pad_rows(tokens).astype(F32)
    for block in range(BLOCKS):
        attn_w, fc1_w, fc2_w = weights_all[block]
        mixed, normed, normed2, query, key, value, probs, attended = attention_forward(
            residual,
            attn_w,
            vectors[block],
            qv[block],
            biases[block],
            masks[block % 2],
            live,
            local_heads,
            scale,
        )
        after, hidden, slope = ffn_forward(
            mixed, normed2, fc1_w, fc2_w, hidden_biases[block], vectors[block], live
        )
        kept.append(
            (residual, mixed, normed, normed2, query, key, value, probs, attended, hidden, slope)
        )
        residual = after

    grad_rows = pad_rows(cotangent).astype(F32)
    shard_grads = [None] * BLOCKS
    small_sums = [None] * BLOCKS
    for block in reversed(range(BLOCKS)):
        attn_w, fc1_w, fc2_w = weights_all[block]
        x, mixed, normed, normed2, query, key, value, probs, attended, hidden, slope = kept[block]
        branch_grad, pre_grad, mixed_grad, attn_grad, small_ffn, hidden_grad = ffn_backward(
            grad_rows, mixed, slope, fc1_w, fc2_w, vectors[block], live
        )
        fc2_grad = scatter_rows(
            lambda picks, added=(): weight_grad(branch_grad, hidden, picks, added), block % 2 == 0
        )
        fc1_grad = scatter_rows(
            lambda picks, added=(): weight_grad(normed2, pre_grad, picks, added), block % 2 == 1
        )
        grad_rows, qkv_grad, score_sum, small_attn, qv_grad = attention_backward(
            x,
            mixed_grad,
            attn_grad,
            attn_w,
            query,
            key,
            value,
            probs,
            vectors[block],
            local_heads,
            scale,
        )
        attn_w_grad = scatter_rows(
            lambda picks, added=(): attn_weight_grad(
                normed, qkv_grad, attn_grad, attended, picks, added
            ),
            block % 2 == 0,
        )
        shard_grads[block] = (attn_w_grad, fc1_grad, fc2_grad)
        table_grad = lax.dot_general(
            score_sum.reshape(heads_total, -1),
            onehots[block % 2].astype(F32),
            (((1,), (1,)), ((), ())),
            precision=lax.Precision.HIGHEST,
            preferred_element_type=F32,
        ).reshape(pieces, -1)
        items = [
            small_attn[0],
            small_ffn[0],
            small_attn[1],
            small_ffn[1],
            ordered(qv_grad[:, 0, :local_width], 0).reshape(-1),
            ordered(qv_grad[:, 0, 2 * local_width :], 0).reshape(-1),
            small_ffn[2],
            small_ffn[3],
            ordered(hidden_grad[:, 0], 0).reshape(-1),
            ordered(table_grad, 0).reshape(-1),
        ]
        small_sums[block] = sum_all(jnp.concatenate(items))

    totals = jnp.stack(small_sums)

    def own(values):
        return lax.dynamic_slice_in_dim(values, dp_index * dp_width, dp_width, 2)

    small_grads = []
    for index in range(4):
        part = totals[:, 2 * index * width : 2 * (index + 1) * width]
        small_grads.append(own(part.reshape(BLOCKS, 2, width)))
    offset = 8 * width
    hidden_total = totals[:, offset : offset + pieces * fc1_weight.shape[2]]
    fc1_bias_grad = lax.dynamic_slice_in_dim(hidden_total, dp_index * dp_hidden, dp_hidden, 1)
    offset += hidden_total.shape[1]
    table_total = totals[:, offset:].reshape(BLOCKS, heads_total, rel_count)
    bias_table_grad = lax.dynamic_slice_in_dim(
        table_total, head_index * local_heads, local_heads, 1
    )
    qkv_weight_grad = jnp.stack(
        [item[0][:, : 3 * local_width].reshape(-1, 3, local_width) for item in shard_grads]
    )
    proj_weight_grad = jnp.stack([item[0][:, 3 * local_width :].T for item in shard_grads])
    fc1_weight_grad = jnp.stack([item[1] for item in shard_grads])
    fc2_weight_grad = jnp.stack([item[2].T for item in shard_grads])
    return (
        drop_rows(residual),
        drop_rows(grad_rows),
        small_grads[0],
        small_grads[1],
        qkv_weight_grad,
        small_grads[2],
        bias_table_grad,
        proj_weight_grad,
        fc1_weight_grad,
        fc1_bias_grad,
        fc2_weight_grad,
        small_grads[3],
    )


def solution(mesh):
    placed = (
        P(("dp", "head"), None),
        P(("dp", "head"), None),
        P("dp"),
        P("dp", None),
        P("dp", None),
        P(),
        P(None, None, "dp"),
        P(None, None, "dp"),
        P(None, "dp", None, "head"),
        P(None, None, "dp"),
        P(None, "head", None),
        P(None, "head", "dp"),
        P(None, "dp", "head"),
        P(None, "dp"),
        P(None, "head", "dp"),
        P(None, None, "dp"),
    )
    return jax.shard_map(
        shards,
        mesh=mesh,
        in_specs=placed,
        out_specs=(
            P(("dp", "head"), None),
            P(("dp", "head"), None),
            P(None, None, "dp"),
            P(None, None, "dp"),
            P(None, "dp", None, "head"),
            P(None, None, "dp"),
            P(None, "head", None),
            P(None, "head", "dp"),
            P(None, "dp", "head"),
            P(None, "dp"),
            P(None, "head", "dp"),
            P(None, None, "dp"),
        ),
        check_vma=False,
    )
```

time: 1130 us -> 834 us (0.74)
  matrix products: 362 us -> 3.95 us
  Pallas kernels: 0 us -> 292 us
  local copies, waits for them, and re-layouts: 301 us -> 79.6 us
  other arithmetic: 140 us -> 81.7 us
  waiting for transfers between devices: 235 us -> 288 us
    dot_general x152 -> x4, matrix products: 335 us -> 3.95 us  [the longest x2 2.3 us: shards(): lax.dot_general(score_sum.reshape(heads_total, -1), onehots[block % 2].as...]
    pallas_call x0 -> x20, Pallas kernels: none -> 292 us  [the longest x2 75.1 us: attention_backward(): pl.pallas_call(functools.partial(attention_backward_kernel, heads, scale)...]
    reshape x72 -> x20, local copies, waits for them, and re-layouts: 102 us -> 13.3 us  [the longest x2 4.46 us: drop_rows(): return grid.reshape(-1, values.shape[1])]
    ppermute x93, waiting for transfers between devices: 235 us -> 288 us  [swap(): return lax.ppermute(values, axis, [(i, i ^ 1 << bit) for i in range(size)])]
    unnamed x707 -> x230, local copies, waits for them, and re-layouts: 62.3 us -> 9.63 us
    convert_element_type x40 -> x1, local copies, waits for them, and re-layouts: 49.3 us -> 0.02 us  [shards(): hidden_bias.transpose(1, 0, 2).reshape(BLOCKS, pieces, -1).astype(F32)]
    sub x8 -> x0, matrix products: 27.6 us -> none  [shards(): expo = jnp.exp(scores - peak)]
    reduce_sum x24 -> x0, other arithmetic: 22.7 us -> none  [the longest x8 9.6 us: shards(): score_total = jnp.sum(score_grad, axis=0, dtype=F32)]
  transfers between devices with their start and end apart: 93 -> 93, of which waited for: 33 -> 36; matrix products, arithmetic and copies ran while one was open for 43% -> 19% of each run, Pallas kernels for 0% -> 26%
where the time goes in v2:
time: 834 us; the launch traced here: 828 us
  Pallas kernels  292 us (35%)
  waiting for transfers between devices  288 us (35%)
  other arithmetic  81.7 us (10%)
  starting transfers between devices  80.3 us (10%)
  local copies, waits for them, and re-layouts  79.6 us (10%)
    ppermute x93, waiting for transfers between devices, swap(): return lax.ppermute(values, axis, [(i, i ^ 1 << bit) for i in range(size)])  288 us
    ppermute x93, starting transfers between devices, swap(): return lax.ppermute(values, axis, [(i, i ^ 1 << bit) for i in range(size)])  80.3 us
    pallas_call x2, Pallas kernels, attention_backward(): pl.pallas_call(functools.partial(attention_backward_kernel, heads, scale)...  75.1 us
    pallas_call x2, Pallas kernels, attention_forward(): pl.pallas_call(functools.partial(attention_forward_kernel, heads, scale),...  66.5 us
    pallas_call x8, Pallas kernels, weight_grad(): pl.pallas_call(functools.partial(weight_grad_kernel, picks), out_shape=tu...  47.3 us
    select_n x34, other arithmetic, join(): jnp.where(upper, jnp.stack([other, mine], axis=dim), jnp.stack([mine, oth...  43 us
    pallas_call x2, Pallas kernels, ffn_backward(): pl.pallas_call(ffn_backward_kernel, out_shape=(shape((rows, width), BF16)...  39.3 us
    pallas_call x2, Pallas kernels, ffn_forward(): pl.pallas_call(ffn_forward_kernel, out_shape=(shape((rows, width), F32),...  34.7 us
  transfers between devices with their start and end apart: 93, of which 36 were waited for; matrix products, arithmetic and copies ran while one was open for 19% of the time, Pallas kernels for 26%

profile of v2, /device:TPU:0, one launch (start us, length us, event | category | flops | bytes accessed | tf_op | source)
XLA Modules:
  0.0 828.1 jit_solution(12406535052358765292)
XLA Ops:
  58.7 45.6 %collective-permute-done.12 = bf16[2,96,768]{1,2,0:T(8,128)(2,1)S(1)} collective-permute-done((bf16[2,96,768]{1,2,0:T(8,128)(2,1)S(1)}, bf16[2,96,768]{1,2,0:T(8,128)(2,1)S(1)}, u32[]{:S(2)}, u32[]{:S(2)}) %collective-permute-start.12) | collective-permute-done | bytes 294944 | tf_op jit(solution)/shard_map/ppermute | solution.py:417
  114.7 10.8 %collective-permute-done.25 = bf16[2,96,768]{1,2,0:T(8,128)(2,1)} collective-permute-done((bf16[2,96,768]{1,2,0:T(8,128)(2,1)}, bf16[2,96,768]{1,2,0:T(8,128)(2,1)}, u32[]{:S(2)}, u32[]{:S(2)}) %collective-permute-start.25) | collective-permute-done | bytes 294944 | tf_op jit(solution)/shard_map/ppermute | solution.py:417
  128.4 9.8 %collective-permute-done.32 = bf16[2,96,768]{1,2,0:T(8,128)(2,1)} collective-permute-done((bf16[2,96,768]{1,2,0:T(8,128)(2,1)}, bf16[2,96,768]{1,2,0:T(8,128)(2,1)}, u32[]{:S(2)}, u32[]{:S(2)}) %collective-permute-start.32) | collective-permute-done | bytes 294944 | tf_op jit(solution)/shard_map/ppermute | solution.py:417
  158.7 18.0 %collective-permute-done.20 = bf16[4,96,768]{2,1,0:T(8,128)(2,1)} collective-permute-done((bf16[4,96,768]{2,1,0:T(8,128)(2,1)}, bf16[4,96,768]{2,1,0:T(8,128)(2,1)}, u32[]{:S(2)}, u32[]{:S(2)}) %collective-permute-start.20) | collective-permute-done | bytes 589856 | tf_op jit(solution)/shard_map/ppermute | solution.py:417
  203.4 11.2 %collective-permute-done.16 = bf16[4,96,768]{2,1,0:T(8,128)(2,1)} collective-permute-done((bf16[4,96,768]{2,1,0:T(8,128)(2,1)}, bf16[4,96,768]{2,1,0:T(8,128)(2,1)}, u32[]{:S(2)}, u32[]{:S(2)}) %collective-permute-start.16) | collective-permute-done | bytes 589856 | tf_op jit(solution)/shard_map/ppermute | solution.py:417
  214.6 11.4 %collective-permute-done.29 = bf16[4,96,768]{2,1,0:T(8,128)(2,1)} collective-permute-done((bf16[4,96,768]{2,1,0:T(8,128)(2,1)}, bf16[4,96,768]{2,1,0:T(8,128)(2,1)}, u32[]{:S(2)}, u32[]{:S(2)}) %collective-permute-start.29) | collective-permute-done | bytes 589856 | tf_op jit(solution)/shard_map/ppermute | solution.py:417
  285.4 33.1 %attention_forward.2 = (f32[672,768]{1,0:T(8,128)}, bf16[672,768]{1,0:T(8,128)(2,1)}, bf16[672,768]{1,0:T(8,128)(2,1)}, bf16[4,672,192]{2,1,0:T(8,128)(2,1)}, bf...) custom-call(f32[672,768]{1,0:T(8,128)} %bitcast_convert_fusion.1.x_r, ...), custom_call_target="tpu_custom_call" | custom-call | flops 3249999872 | bytes 30000000 | tf_op jit(solution)/shard_map/attention_forward/pallas_call | solution.py:146
  318.5 17.4 %ffn_forward.2 = (f32[672,768]{1,0:T(8,128)}, bf16[4,672,768]{2,1,0:T(8,128)(2,1)}, bf16[4,672,768]{2,1,0:T(8,128)(2,1)}) custom-call(f32[672,768]{1,0:T(8,128)} %get-tuple-element.80.mixed_ref, bf16[672,768]{1,0:T(8,128)(2,1)} %get-tuple-element.81.normed2_ref.left_ref, bf16[768,768]{1,0:T(8,128)(2,1)} %bitcast.390, bf16[768,768]{1,0:T(8,128)(2,1)} %bitcast.45.a1, ...), custom_call_target="tpu_custom_call" | custom-call | tf_op jit(solution)/shard_map/ffn_forward/pallas_call | solution.py:201
  335.9 33.4 %attention_forward.3 = (f32[672,768]{1,0:T(8,128)}, bf16[672,768]{1,0:T(8,128)(2,1)}, bf16[672,768]{1,0:T(8,128)(2,1)}, bf16[4,672,192]{2,1,0:T(8,128)(2,1)}, bf...) custom-call(f32[672,768]{1,0:T(8,128)} %get-tuple-element.82.x_ref, ...), custom_call_target="tpu_custom_call" | custom-call | flops 3249999872 | bytes 30000000 | tf_op jit(solution)/shard_map/attention_forward/pallas_call | solution.py:146
  370.4 17.3 %ffn_forward.3 = (f32[672,768]{1,0:T(8,128)}, bf16[4,672,768]{2,1,0:T(8,128)(2,1)}, bf16[4,672,768]{2,1,0:T(8,128)(2,1)}) custom-call(f32[672,768]{1,0:T(8,128)} %get-tuple-element.83.mixed_ref, bf16[672,768]{1,0:T(8,128)(2,1)} %get-tuple-element.84.normed2_ref.left_ref, bf16[768,768]{1,0:T(8,128)(2,1)} %bitcast.104.a0, bf16[768,768]{1,0:T(8,128)(2,1)} %bitcast.105.a1, ...), custom_call_target="tpu_custom_call" | custom-call | tf_op jit(solution)/shard_map/ffn_forward/pallas_call | solution.py:201
  387.7 19.8 %ffn_backward.2 = (bf16[672,768]{1,0:T(8,128)(2,1)}, bf16[4,672,768]{2,1,0:T(8,128)(2,1)}, f32[672,768]{1,0:T(8,128)}, bf16[672,768]{1,0:T(8,128)(2,1)}, f32[8,768]{1,0:T(8,128)}, /*index=5*/f32[4,1,768]{2,1,0:T(1,128)}) custom-call(f32[672,768]{1,0:T(8,128)} %bitcast_convert_fusion.grad_ref, f32[672,768]{1,0:T(8,128)} %get-tuple-element.83.mixed_ref, ...), custom_call_target="tpu_custom_call" | custom-call | tf_op jit(solution)/shard_map/ffn_backward/pallas_call | solution.py:271
  407.5 37.7 %attention_backward.2 = (f32[672,768]{1,0:T(8,128)}, bf16[4,672,576]{2,1,0:T(8,128)(2,1)}, f32[4,336,56]{2,1,0:T(8,128)}, f32[8,768]{1,0:T(8,128)}, f32[4,1,576]{2,1,0:T(1,128)}) custom-call(f32[672,768]{1,0:T(8,128)} %get-tuple-element.82.x_ref, f32[672,768]{1,0:T(8,128)} %get-tuple-element.87.mixed_grad_ref, ...), custom_call_target="tpu_custom_call" | custom-call | tf_op jit(solution)/shard_map/attention_backward/pallas_call | solution.py:399
  450.1 19.5 %ffn_backward.3 = (bf16[672,768]{1,0:T(8,128)(2,1)}, bf16[4,672,768]{2,1,0:T(8,128)(2,1)}, f32[672,768]{1,0:T(8,128)}, bf16[672,768]{1,0:T(8,128)(2,1)}, f32[8,768]{1,0:T(8,128)}, /*index=5*/f32[4,1,768]{2,1,0:T(1,128)}) custom-call(f32[672,768]{1,0:T(8,128)} %get-tuple-element.93.grad_ref, f32[672,768]{1,0:T(8,128)} %get-tuple-element.80.mixed_ref, ...), custom_call_target="tpu_custom_call" | custom-call | tf_op jit(solution)/shard_map/ffn_backward/pallas_call | solution.py:271
  469.6 37.4 %attention_backward.3 = (f32[672,768]{1,0:T(8,128)}, bf16[4,672,576]{2,1,0:T(8,128)(2,1)}, f32[4,336,56]{2,1,0:T(8,128)}, f32[8,768]{1,0:T(8,128)}, f32[4,1,576]{2,1,0:T(1,128)}) custom-call(f32[672,768]{1,0:T(8,128)} %bitcast_convert_fusion.1.x_ref, f32[672,768]{1,0:T(8,128)} %get-tuple-element.95.mixed_grad_ref, ...), custom_call_target="tpu_custom_call" | custom-call | tf_op jit(solution)/shard_map/attention_backward/pallas_call | solution.py:399
  511.6 6.8 attn_weight_grad.6
  518.9 6.8 attn_weight_grad.4
  593.5 7.4 attn_weight_grad.5
  626.5 7.9 collective-permute-done.76
  639.9 7.7 attn_weight_grad.7
  653.9 6.3 weight_grad.15
  684.7 17.5 %collective-permute-done.84 = bf16[4,96,768]{2,1,0:T(8,128)(2,1)} collective-permute-done((bf16[4,96,768]{2,1,0:T(8,128)(2,1)}, bf16[4,96,768]{2,1,0:T(8,128)(2,1)}, u32[]{:S(2)}, u32[]{:S(2)}) %collective-permute-start.84) | collective-permute-done | bytes 589856 | tf_op jit(solution)/shard_map/ppermute | solution.py:417
  709.1 18.3 %collective-permute-done.69 = bf16[768,768]{1,0:T(8,128)(2,1)} collective-permute-done((bf16[768,768]{1,0:T(8,128)(2,1)}, bf16[768,768]{1,0:T(8,128)(2,1)}, u32[]{:S(2)}, u32[]{:S(2)}) %collective-permute-start.69) | collective-permute-done | bytes 1179680 | tf_op jit(solution)/shard_map/ppermute | solution.py:417
  730.2 18.6 %collective-permute-done.89 = bf16[768,768]{1,0:T(8,128)(2,1)} collective-permute-done((bf16[768,768]{1,0:T(8,128)(2,1)}, bf16[768,768]{1,0:T(8,128)(2,1)}, u32[]{:S(2)}, u32[]{:S(2)}) %collective-permute-start.89) | collective-permute-done | bytes 1179680 | tf_op jit(solution)/shard_map/ppermute | solution.py:417
  780.8 23.8 %collective-permute-done.65 = bf16[2,96,768]{1,2,0:T(8,128)(2,1)S(1)} collective-permute-done((bf16[2,96,768]{1,2,0:T(8,128)(2,1)S(1)}, bf16[2,96,768]{1,2,0:T(8,128)(2,1)S(1)}, u32[]{:S(2)}, u32[]{:S(2)}) %collective-permute-start.65) | collective-permute-done | bytes 294944 | tf_op jit(solution)/shard_map/ppermute | solution.py:417
  (693 shorter events, 381.6 us)
Async XLA Ops:
  41.9 64.8 %collective-permute-start.1 = (bf16[2,96,768]{1,2,0:T(8,128)(2,1)}, bf16[2,96,768]{1,2,0:T(8,128)(2,1)}, u32[]{:S(2)}, u32[]{:S(2)}) collective-permute-start(bf16[2,96,768]{1,2,0:T(8,128)(2,1)} %maximum_select_fusion.15), channel_id=1, source_target_pairs={{0,16},{4,20},{8,24},{12,28},{16,0},{20,4},{24,8},{28,12},{1,17},{... | collective-permute-start | bytes 884744 | tf_op jit(solution)/shard_map/ppermute | solution.py:417
  46.8 57.6 %collective-permute-start.12 = (bf16[2,96,768]{1,2,0:T(8,128)(2,1)S(1)}, bf16[2,96,768]{1,2,0:T(8,128)(2,1)S(1)}, u32[]{:S(2)}, u32[]{:S(2)}) collective-permute-start(bf16[2,96,768]{1,2,0:T(8,128)(2,1)S(1)} %maximum_select_fusion.17), channel_id=1, source_target_pairs={{0,16},{4,20},{8,24},{12,28},{16,0},{20,4},{24,8},{28,12},{1,17},{... | collective-permute-start | bytes 884744 | tf_op jit(solution)/shard_map/ppermute | solution.py:417
  48.2 64.7 %collective-permute-start.19 = (bf16[2,96,768]{1,2,0:T(8,128)(2,1)}, bf16[2,96,768]{1,2,0:T(8,128)(2,1)}, u32[]{:S(2)}, u32[]{:S(2)}) collective-permute-start(bf16[2,96,768]{1,2,0:T(8,128)(2,1)} %maximum_select_fusion.19), channel_id=1, source_target_pairs={{0,16},{4,20},{8,24},{12,28},{16,0},{20,4},{24,8},{28,12},{1,17},{... | collective-permute-start | bytes 884744 | tf_op jit(solution)/shard_map/ppermute | solution.py:417
  53.9 71.7 %collective-permute-start.25 = (bf16[2,96,768]{1,2,0:T(8,128)(2,1)}, bf16[2,96,768]{1,2,0:T(8,128)(2,1)}, u32[]{:S(2)}, u32[]{:S(2)}) collective-permute-start(bf16[2,96,768]{1,2,0:T(8,128)(2,1)} %maximum_select_fusion.21), channel_id=1, source_target_pairs={{0,16},{4,20},{8,24},{12,28},{16,0},{20,4},{24,8},{28,12},{1,17},{... | collective-permute-start | bytes 884744 | tf_op jit(solution)/shard_map/ppermute | solution.py:417
  56.0 82.2 %collective-permute-start.32 = (bf16[2,96,768]{1,2,0:T(8,128)(2,1)}, bf16[2,96,768]{1,2,0:T(8,128)(2,1)}, u32[]{:S(2)}, u32[]{:S(2)}) collective-permute-start(bf16[2,96,768]{1,2,0:T(8,128)(2,1)} %maximum_select_fusion.23), channel_id=1, source_target_pairs={{0,16},{4,20},{8,24},{12,28},{16,0},{20,4},{24,8},{28,12},{1,17},{... | collective-permute-start | bytes 884744 | tf_op jit(solution)/shard_map/ppermute | solution.py:417
  105.7 47.9 %collective-permute-start.13 = (bf16[4,96,768]{2,1,0:T(8,128)(2,1)}, bf16[4,96,768]{2,1,0:T(8,128)(2,1)}, u32[]{:S(2)}, u32[]{:S(2)}) collective-permute-start(bf16[4,96,768]{2,1,0:T(8,128)(2,1)} %copy.114), channel_id=1, source_target_pairs={{0,4},{4,0},{8,12},{12,8},{16,20},{20,16},{24,28},{28,24},{1,5},{5... | collective-permute-start | bytes 1769480 | tf_op jit(solution)/shard_map/ppermute | solution.py:417
  106.7 47.5 %collective-permute-start.15 = (bf16[4,96,768]{2,1,0:T(8,128)(2,1)}, bf16[4,96,768]{2,1,0:T(8,128)(2,1)}, u32[]{:S(2)}, u32[]{:S(2)}) collective-permute-start(bf16[4,96,768]{2,1,0:T(8,128)(2,1)} %copy.114), channel_id=1, source_target_pairs={{0,2},{1,3},{2,0},{3,1},{4,6},{5,7},{6,4},{7,5},{8,10},{9,11},{10,... | collective-permute-start | bytes 1769480 | tf_op jit(solution)/shard_map/ppermute | solution.py:417
  179.2 53.2 %collective-permute-start.42 = (bf16[4,96,768]{2,1,0:T(8,128)(2,1)}, bf16[4,96,768]{2,1,0:T(8,128)(2,1)}, u32[]{:S(2)}, u32[]{:S(2)}) collective-permute-start(bf16[4,96,768]{2,1,0:T(8,128)(2,1)} %collective-permute-done.41), channel_id=1, source_target_pairs={{0,4},{4,0},{8,12},{12,8},{16,20},{20,16},{24,28},{28,24},{1,5},{5... | collective-permute-start | bytes 1769480 | tf_op jit(solution)/shard_map/ppermute | solution.py:417
  189.3 50.6 %collective-permute-start.3 = (bf16[4,2,96,768]{3,2,1,0:T(8,128)(2,1)}, bf16[4,2,96,768]{3,2,1,0:T(8,128)(2,1)}, u32[]{:S(2)}, u32[]{:S(2)}) collective-permute-start(bf16[4,2,96,768]{3,2,1,0:T(8,128)(2,1)} %maximum_select_fusion), channel_id=1, source_target_pairs={{0,1},{1,0},{2,3},{3,2},{4,5},{5,4},{6,7},{7,6},{8,9},{9,8},{10,11... | collective-permute-start | bytes 3538952 | tf_op jit(solution)/shard_map/ppermute | solution.py:417
  257.8 78.1 %collective-permute-start.30 = (bf16[4,2,96,768]{3,2,1,0:T(8,128)(2,1)}, bf16[4,2,96,768]{3,2,1,0:T(8,128)(2,1)}, u32[]{:S(2)}, u32[]{:S(2)}) collective-permute-start(bf16[4,2,96,768]{3,2,1,0:T(8,128)(2,1)} %maximum_select_fusion.5), channel_id=1, source_target_pairs={{0,1},{1,0},{2,3},{3,2},{4,5},{5,4},{6,7},{7,6},{8,9},{9,8},{10,11... | collective-permute-start | bytes 3538952 | tf_op jit(solution)/shard_map/ppermute | solution.py:417
  277.1 92.2 %collective-permute-start.34 = (bf16[4,2,96,768]{3,2,1,0:T(8,128)(2,1)}, bf16[4,2,96,768]{3,2,1,0:T(8,128)(2,1)}, u32[]{:S(2)}, u32[]{:S(2)}) collective-permute-start(bf16[4,2,96,768]{3,2,1,0:T(8,128)(2,1)} %maximum_select_fusion.6), channel_id=1, source_target_pairs={{0,1},{1,0},{2,3},{3,2},{4,5},{5,4},{6,7},{7,6},{8,9},{9,8},{10,11... | collective-permute-start | bytes 3538952 | tf_op jit(solution)/shard_map/ppermute | solution.py:417
  277.1 92.2 %collective-permute-start.40 = (bf16[4,2,96,768]{3,2,1,0:T(8,128)(2,1)S(1)}, bf16[4,2,96,768]{3,2,1,0:T(8,128)(2,1)S(1)}, u32[]{:S(2)}, u32[]{:S(2)}) collective-permute-start(bf16[4,2,96,768]{3,2,1,0:T(8,128)(2,1)S(1)} %maximum_select_fusion.7), channel_id=1, source_target_pairs={{0,1},{1,0},{2,3},{3,2},{4,5},{5,4},{6,7},{7,6},{8,9},{9,8},{10,11... | collective-permute-start | bytes 3538952 | tf_op jit(solution)/shard_map/ppermute | solution.py:417
  277.6 91.8 %collective-permute-start.43 = (bf16[4,2,96,768]{3,2,1,0:T(8,128)(2,1)S(1)}, bf16[4,2,96,768]{3,2,1,0:T(8,128)(2,1)}, u32[]{:S(2)}, u32[]{:S(2)}) collective-permute-start(bf16[4,2,96,768]{3,2,1,0:T(8,128)(2,1)S(1)} %maximum_select_fusion.8), channel_id=1, source_target_pairs={{0,1},{1,0},{2,3},{3,2},{4,5},{5,4},{6,7},{7,6},{8,9},{9,8},{10,11... | collective-permute-start | bytes 3538952 | tf_op jit(solution)/shard_map/ppermute | solution.py:417
  277.7 91.7 %collective-permute-start.36 = (bf16[4,2,96,768]{3,2,1,0:T(8,128)(2,1)}, bf16[4,2,96,768]{3,2,1,0:T(8,128)(2,1)}, u32[]{:S(2)}, u32[]{:S(2)}) collective-permute-start(bf16[4,2,96,768]{3,2,1,0:T(8,128)(2,1)} %collective-permute-done.35), channel_id=1, source_target_pairs={{0,1},{1,0},{2,3},{3,2},{4,5},{5,4},{6,7},{7,6},{8,9},{9,8},{10,11... | collective-permute-start | bytes 3538952 | tf_op jit(solution)/shard_map/ppermute | solution.py:417
  449.9 76.4 %collective-permute-start.49 = (f32[13272]{0:T(1024)S(1)}, f32[13272]{0:T(1024)S(1)}, u32[]{:S(2)}, u32[]{:S(2)}) collective-permute-start(f32[13272]{0:T(1024)S(1)} %constant_dynamic-update-slice_fusion.1), channel_id=1, source_target_pairs={{0,1},{1,0},{2,3},{3,2},{4,5},{5,4},{6,7},{7,6},{8,9},{9,8},{10,11... | collective-permute-start | bytes 159272 | tf_op jit(solution)/shard_map/ppermute | solution.py:417
  518.4 69.8 %collective-permute-start.61 = (bf16[768,768]{1,0:T(8,128)(2,1)}, bf16[768,768]{1,0:T(8,128)(2,1)S(1)}, u32[]{:S(2)}, u32[]{:S(2)}) collective-permute-start(bf16[768,768]{1,0:T(8,128)(2,1)} %get-tuple-element.122), channel_id=1, source_target_pairs={{0,1},{1,0},{2,3},{3,2},{4,5},{5,4},{6,7},{7,6},{8,9},{9,8},{10,11... | collective-permute-start | bytes 3538952 | tf_op jit(solution)/shard_map/ppermute | solution.py:417
  518.8 69.9 %collective-permute-start.62 = (bf16[768,768]{1,0:T(8,128)(2,1)}, bf16[768,768]{1,0:T(8,128)(2,1)}, u32[]{:S(2)}, u32[]{:S(2)}) collective-permute-start(bf16[768,768]{1,0:T(8,128)(2,1)} %get-tuple-element.123), channel_id=1, source_target_pairs={{0,1},{1,0},{2,3},{3,2},{4,5},{5,4},{6,7},{7,6},{8,9},{9,8},{10,11... | collective-permute-start | bytes 3538952 | tf_op jit(solution)/shard_map/ppermute | solution.py:417
  525.7 63.2 %collective-permute-start.54 = (bf16[768,768]{1,0:T(8,128)(2,1)}, bf16[768,768]{1,0:T(8,128)(2,1)}, u32[]{:S(2)}, u32[]{:S(2)}) collective-permute-start(bf16[768,768]{1,0:T(8,128)(2,1)} %get-tuple-element.115), channel_id=1, source_target_pairs={{0,1},{1,0},{2,3},{3,2},{4,5},{5,4},{6,7},{7,6},{8,9},{9,8},{10,11... | collective-permute-start | bytes 3538952 | tf_op jit(solution)/shard_map/ppermute | solution.py:417
  526.1 63.3 %collective-permute-start.55 = (bf16[768,768]{1,0:T(8,128)(2,1)}, bf16[768,768]{1,0:T(8,128)(2,1)}, u32[]{:S(2)}, u32[]{:S(2)}) collective-permute-start(bf16[768,768]{1,0:T(8,128)(2,1)} %get-tuple-element.116), channel_id=1, source_target_pairs={{0,1},{1,0},{2,3},{3,2},{4,5},{5,4},{6,7},{7,6},{8,9},{9,8},{10,11... | collective-permute-start | bytes 3538952 | tf_op jit(solution)/shard_map/ppermute | solution.py:417
  672.4 55.0 %collective-permute-start.69 = (bf16[768,768]{1,0:T(8,128)(2,1)}, bf16[768,768]{1,0:T(8,128)(2,1)}, u32[]{:S(2)}, u32[]{:S(2)}) collective-permute-start(bf16[768,768]{1,0:T(8,128)(2,1)} %get-tuple-element.130), channel_id=1, source_target_pairs={{0,2},{1,3},{2,0},{3,1},{4,6},{5,7},{6,4},{7,5},{8,10},{9,11},{10,... | collective-permute-start | bytes 3538952 | tf_op jit(solution)/shard_map/ppermute | solution.py:417
  673.9 74.9 %collective-permute-start.89 = (bf16[768,768]{1,0:T(8,128)(2,1)}, bf16[768,768]{1,0:T(8,128)(2,1)}, u32[]{:S(2)}, u32[]{:S(2)}) collective-permute-start(bf16[768,768]{1,0:T(8,128)(2,1)} %get-tuple-element.147), channel_id=1, source_target_pairs={{0,2},{1,3},{2,0},{3,1},{4,6},{5,7},{6,4},{7,5},{8,10},{9,11},{10,... | collective-permute-start | bytes 3538952 | tf_op jit(solution)/shard_map/ppermute | solution.py:417
  683.9 69.3 %collective-permute-start.59 = (bf16[2,96,768]{1,2,0:T(8,128)(2,1)S(1)}, bf16[2,96,768]{1,2,0:T(8,128)(2,1)S(1)}, u32[]{:S(2)}, u32[]{:S(2)}) collective-permute-start(bf16[2,96,768]{1,2,0:T(8,128)(2,1)S(1)} %fusion.17), channel_id=1, source_target_pairs={{0,16},{4,20},{8,24},{12,28},{16,0},{20,4},{24,8},{28,12},{1,17},{... | collective-permute-start | bytes 884744 | tf_op jit(solution)/shard_map/ppermute | solution.py:417
  702.1 51.7 %collective-permute-start.78 = (bf16[2,96,768]{2,1,0:T(8,128)(2,1)S(1)}, bf16[2,96,768]{2,1,0:T(8,128)(2,1)S(1)}, u32[]{:S(2)}, u32[]{:S(2)}) collective-permute-start(bf16[2,96,768]{2,1,0:T(8,128)(2,1)S(1)} %fusion.21), channel_id=1, source_target_pairs={{0,16},{4,20},{8,24},{12,28},{16,0},{20,4},{24,8},{28,12},{1,17},{... | collective-permute-start | bytes 884744 | tf_op jit(solution)/shard_map/ppermute | solution.py:417
  704.3 52.4 %collective-permute-start.85 = (bf16[2,96,768]{2,1,0:T(8,128)(2,1)S(1)}, bf16[2,96,768]{2,1,0:T(8,128)(2,1)S(1)}, u32[]{:S(2)}, u32[]{:S(2)}) collective-permute-start(bf16[2,96,768]{2,1,0:T(8,128)(2,1)S(1)} %fusion.22), channel_id=1, source_target_pairs={{0,16},{4,20},{8,24},{12,28},{16,0},{20,4},{24,8},{28,12},{1,17},{... | collective-permute-start | bytes 884744 | tf_op jit(solution)/shard_map/ppermute | solution.py:417
  (164 other events, 2591.9 us)

commit v3 on v1

v3 whole, which is shorter than its diff:
```python
import functools

import jax
import jax.numpy as jnp
from jax import lax
from jax.experimental import pallas as pl
from jax.experimental.pallas import tpu as pltpu
from jax.sharding import PartitionSpec as P

WSIDE = 7
SHIFT = 3
CROP_MAX = 12
BLOCKS = 2
WTOK = 49
PADDED = 56
PIECES = 4
VMEM_BYTES = 60 * 2**20

EPSILON = 1e-05
MASKED = -100.0
ABSENT = -1e30
BF16 = jnp.bfloat16
F32 = jnp.float32


def cost(micros):
    return pl.CostEstimate(
        flops=int(micros * 1e9), bytes_accessed=int(micros * 3e6), transcendentals=0
    )


def dot(left, right, left_dim=1, right_dim=0):
    return lax.dot_general(
        left, right, (((left_dim,), (right_dim,)), ((), ())), preferred_element_type=F32
    )


def normalize(values):
    centred = values - jnp.mean(values, axis=-1, keepdims=True)
    scale = lax.rsqrt(jnp.mean(centred * centred, axis=-1, keepdims=True) + EPSILON)
    return centred * scale, scale


def norm_back_rows(values, gain, error):
    normal, scale = normalize(values)
    flow = error * gain
    grad = (
        flow
        - jnp.mean(flow, axis=-1, keepdims=True)
        - normal * jnp.mean(flow * normal, axis=-1, keepdims=True)
    ) * scale
    return grad, jnp.sum(error * normal, axis=0, keepdims=True), jnp.sum(error, axis=0, keepdims=True)


def spread_heads(values, heads):
    columns = values.shape[1]
    owner = lax.broadcasted_iota(jnp.int32, values.shape, 1) // (columns // heads)
    return jnp.concatenate(
        [jnp.where(owner == head, values, 0.0) for head in range(heads)], axis=0
    ).astype(BF16)


def merge_heads(values, heads):
    rows = values.shape[0] // heads
    columns = values.shape[1]
    owner = lax.broadcasted_iota(jnp.int32, (rows, columns), 1) // (columns // heads)
    total = values[:rows]
    for head in range(1, heads):
        total = jnp.where(owner == head, values[head * rows : (head + 1) * rows], total)
    return total


class Copies:
    def __init__(self, sems):
        self.sems = sems
        self.used = 0
        self.leaving = []

    def start(self, source, target):
        copy = pltpu.make_async_copy(source, target, self.sems.at[self.used])
        self.used += 1
        copy.start()
        return copy

    def fetch(self, source, target):
        return self.start(source, target)

    def send(self, source, target):
        self.leaving.append(self.start(source, target))

    def finish(self):
        for copy in self.leaving:
            copy.wait()


def choose(weights, picks):
    plan, arrays, rows = weights
    chosen = [index for index, (e, _) in enumerate(plan) if e in picks]
    plan = tuple((picks.index(plan[index][0]), plan[index][1]) for index in chosen)
    return plan, [arrays[index] for index in chosen], rows


def fetch_weights(copies, plan, refs, rows, parts):
    own = lax.axis_index("dp")
    started = {}
    for (slot, rels), ref in sorted(zip(plan, refs), key=lambda item: item[0][0]):
        for place, rel in enumerate(rels):
            start = 0 if rel is None else pl.multiple_of(jnp.bitwise_xor(own, rel) * rows, rows)
            for part, target in enumerate(parts):
                started.setdefault(slot, []).append(
                    copies.fetch(
                        ref.at[place, pl.ds(part * rows, rows), :],
                        target.at[slot, pl.ds(start, rows), :],
                    )
                )
    return started


def wait_all(items):
    for item in items:
        item.wait()


def weight_copies(plan, parts):
    return parts * sum(len(rels) for _, rels in plan)


def in_any(count):
    return [pl.BlockSpec(memory_space=pl.ANY)] * count


def in_vmem(count):
    return [pl.BlockSpec(memory_space=pltpu.VMEM)] * count


def like(array):
    return pltpu.VMEM(array.shape, array.dtype)


def call(kernel, name, micros, small, arrays, outs, scratch, copies):
    return pl.pallas_call(
        kernel,
        in_specs=in_vmem(len(small)) + in_any(len(arrays)),
        out_specs=tuple(in_any(len(outs))),
        out_shape=tuple(outs),
        scratch_shapes=list(scratch) + [pltpu.SemaphoreType.DMA((copies,))],
        compiler_params=pltpu.CompilerParams(vmem_limit_bytes=VMEM_BYTES),
        cost_estimate=cost(micros),
        name=name,
    )(*small, *arrays)


def row_chunks(rows, body, init):
    chunk = 2 * PADDED

    def step(index, carry):
        return body(pl.ds(pl.multiple_of(index * chunk, chunk), chunk), carry)

    return lax.fori_loop(0, rows // chunk, step, init)


def attention_forward_kernel(heads, scale, picks, plan, block_rows, end, *refs):
    count = len(picks)
    vec_ref, qv_ref = refs[:2]
    arrays = refs[2 : 5 + 3 * end]
    x_hbm, bias_hbm, mask_hbm = arrays[:3]
    refs = refs[2 + len(arrays) :]
    weight_refs, refs = refs[: len(plan)], refs[len(plan) :]
    outs, refs = refs[: 5 * count + 2], refs[5 * count + 2 :]
    x, bias, mask, total, normed, normed2, live, weights, qs, ks, vs, ps, atts, sems = refs
    rows = x.shape[0]
    columns = qs.shape[2]
    pairs = rows // (2 * PADDED)
    copies = Copies(sems)
    if end:
        normed_hbm, branch_hbm, live_hbm = arrays[3:]
        arrived_normed = copies.fetch(normed_hbm, normed)
    else:
        arrived_x = copies.fetch(x_hbm, x)
    loads = fetch_weights(copies, plan, weight_refs, block_rows, (weights,))
    arrived = [copies.fetch(mask_hbm, mask)]
    for n, e in enumerate(picks):
        arrived.append(copies.fetch(bias_hbm.at[e], bias.at[n]))
    if end:
        late = [
            copies.fetch(x_hbm, x),
            copies.fetch(branch_hbm, total),
            copies.fetch(live_hbm, live),
        ]
        arrived_normed.wait()
    else:
        arrived_x.wait()

        def first_norm(span, _):
            normal, _ = normalize(x[span, :])
            normed[span, :] = (normal * vec_ref[0:1, :] + vec_ref[1:2, :]).astype(BF16)
            return 0

        row_chunks(rows, first_norm, 0)
        copies.send(normed, outs[-1])
    for n, e in enumerate(picks):
        wait_all(loads[n])
        qkv = dot(normed[...], weights[n, :, : 3 * columns])
        qs[n] = ((qkv[:, :columns] + qv_ref[e, 0:1, :]) * scale).astype(BF16)
        ks[n] = qkv[:, columns : 2 * columns].astype(BF16)
        vs[n] = (qkv[:, 2 * columns :] + qv_ref[e, 1:2, :]).astype(BF16)
        for index, buffer in enumerate((qs, ks, vs)):
            copies.send(buffer.at[n], outs[5 * n + index])
    wait_all(arrived)

    def pair_step(pair, _):
        span = pl.ds(pl.multiple_of(pair * 2 * PADDED, 2 * PADDED), 2 * PADDED)
        for n in range(count):
            query = qs[n, span, :].astype(F32)
            key = ks[n, span, :].astype(F32)
            value = vs[n, span, :].astype(F32)
            results = []
            for side in range(2):
                part = slice(side * PADDED, (side + 1) * PADDED)
                keys = spread_heads(key[part], heads)
                scores = dot(keys, query[part].astype(BF16), 1, 1) + bias[n]
                scores = scores.reshape(heads, PADDED, PADDED) + mask[2 * pair + side][None]
                expo = jnp.exp(scores - jnp.max(scores, axis=1, keepdims=True))
                probs = expo * (1.0 / jnp.sum(expo, axis=1, keepdims=True))
                probs = probs.reshape(heads * PADDED, PADDED).astype(BF16)
                ps[n, 2 * pair + side] = probs
                results.append(dot(probs, spread_heads(value[part], heads), 0, 0))
            atts[n, span, :] = jnp.concatenate(results, axis=0).astype(BF16)
        return 0

    lax.fori_loop(0, pairs, pair_step, 0)
    for n in range(count):
        copies.send(ps.at[n], outs[5 * n + 3])
        copies.send(atts.at[n], outs[5 * n + 4])
    if end:
        wait_all(late)
    branch = total[...] if end else None
    for n in range(count):
        part = dot(atts[n], weights[n, :, 3 * columns :], 1, 1)
        branch = part if branch is None else branch + part
    total[...] = branch
    if end:

        def second_norm(span, _):
            mixed = x[span, :] + live[span, :] * (total[span, :] + vec_ref[2:3, :])
            total[span, :] = mixed
            normal, _ = normalize(mixed)
            normed2[span, :] = (normal * vec_ref[3:4, :] + vec_ref[4:5, :]).astype(BF16)
            return 0

        row_chunks(rows, second_norm, 0)
        copies.send(normed2, outs[-1])
    copies.send(total, outs[-2])
    copies.finish()


def attention_forward(x, weights, picks, vectors, qv, bias, mask, live, heads, scale, earlier=()):
    rows, width = x.shape
    columns = qv.shape[2]
    wins = rows // PADDED
    plan, arrays, block_rows = choose(weights, picks)
    count = len(picks)
    end = bool(earlier)
    shape = jax.ShapeDtypeStruct
    piece = shape((rows, columns), BF16)
    probs = shape((wins, heads * PADDED, PADDED), BF16)
    results = call(
        functools.partial(attention_forward_kernel, heads, scale, picks, plan, block_rows, end),
        "attention_forward",
        4 + 6 * count,
        (vectors, qv),
        [x, bias, mask] + list(earlier) + [live] * end + arrays,
        [piece, piece, piece, probs, piece] * count
        + [shape((rows, width), F32), shape((rows, width), BF16)],
        [
            like(x),
            pltpu.VMEM((count,) + bias.shape[1:], F32),
            like(mask),
            pltpu.VMEM((rows, width), F32),
            pltpu.VMEM((rows, width), BF16),
            pltpu.VMEM((rows, width), BF16),
            like(live),
            pltpu.VMEM((count, width, width), BF16),
        ]
        + [pltpu.VMEM((count, rows, columns), BF16)] * 3
        + [
            pltpu.VMEM((count,) + probs.shape, BF16),
            pltpu.VMEM((count, rows, columns), BF16),
        ],
        weight_copies(plan, 1) + 6 * count + 8,
    )
    saved = {e: results[5 * n : 5 * n + 5] for n, e in enumerate(picks)}
    return saved, results[-2], results[-1]


def ffn_forward_kernel(picks, plan, block_rows, end, *refs):
    count = len(picks)
    bias_ref, vec_ref = refs[:2]
    arrays, refs = refs[2 : 3 + 3 * end], refs[3 + 3 * end :]
    weight_refs, refs = refs[: len(plan)], refs[len(plan) :]
    outs, refs = refs[: 2 * count + 1], refs[2 * count + 1 :]
    normed2, mixed, total, live, first, second, hidden, slope, sems = refs
    rows = normed2.shape[0]
    copies = Copies(sems)
    arrived = copies.fetch(arrays[0], normed2)
    loads = fetch_weights(copies, plan, weight_refs, block_rows, (first, second))
    if end:
        late = [copies.fetch(one, to) for one, to in zip(arrays[1:], (mixed, total, live))]
    arrived.wait()
    branch = None
    for n, e in enumerate(picks):
        wait_all(loads[n])
        before = dot(normed2[...], first[n]) + bias_ref[e]
        cdf = 0.5 * (1.0 + lax.erf(before * (0.5**0.5)))
        density = jnp.exp(-0.5 * before * before) * 0.3989422804014327
        hidden[n] = (before * cdf).astype(BF16)
        copies.send(hidden.at[n], outs[2 * n])
        slope[n] = (cdf + before * density).astype(BF16)
        copies.send(slope.at[n], outs[2 * n + 1])
        part = dot(hidden[n], second[n], 1, 1)
        branch = part if branch is None else branch + part
    if not end:
        total[...] = branch
    else:
        wait_all(late)
        total[...] += branch

        def finish(span, _):
            total[span, :] = mixed[span, :] + live[span, :] * (total[span, :] + vec_ref[5:6, :])
            return 0

        row_chunks(rows, finish, 0)
    copies.send(total, outs[-1])
    copies.finish()


def ffn_forward(normed2, weights, picks, bias, vectors, live, earlier=()):
    rows, width = normed2.shape
    plan, arrays, block_rows = choose(weights, picks)
    count = len(picks)
    end = bool(earlier)
    shape = jax.ShapeDtypeStruct
    piece = shape((rows, width), BF16)
    results = call(
        functools.partial(ffn_forward_kernel, picks, plan, block_rows, end),
        "ffn_forward",
        9,
        (bias, vectors),
        [normed2] + list(earlier) + [live] * end + arrays,
        [piece, piece] * count + [shape((rows, width), F32)],
        [
            like(normed2),
            pltpu.VMEM((rows, width), F32),
            pltpu.VMEM((rows, width), F32),
            like(live),
        ]
        + [pltpu.VMEM((count, width, width), BF16)] * 2
        + [pltpu.VMEM((count, rows, width), BF16)] * 2,
        weight_copies(plan, 2) + 2 * count + 5,
    )
    return {e: results[2 * n : 2 * n + 2] for n, e in enumerate(picks)}, results[-1]


def ffn_backward_kernel(picks, plan, block_rows, end, *refs):
    count = len(picks)
    vec_ref = refs[0]
    given = count + 2 + 3 * end
    arrays, refs = refs[1 : 1 + given], refs[1 + given :]
    weight_refs, refs = refs[: len(plan)], refs[len(plan) :]
    outs, refs = refs[: count + 4], refs[count + 4 :]
    grad, live, mixed, branch, error, attn_grad, slopes, pres, first, second, sums, hidden_sums, sems = refs
    rows, width = grad.shape
    copies = Copies(sems)
    zero = jnp.zeros((1, width), F32)
    slope_hbm = arrays[2 : 2 + count]
    if end:
        mixed_hbm, branch_hbm, error_hbm = arrays[2 + count :]
        copies.fetch(branch_hbm, branch).wait()
    else:
        arrived = [copies.fetch(arrays[0], grad), copies.fetch(arrays[1], live)]
    loads = fetch_weights(copies, plan, weight_refs, block_rows, (first, second))
    slope_loads = [copies.fetch(one, slopes.at[n]) for n, one in enumerate(slope_hbm)]
    if end:
        late = [
            copies.fetch(one, to)
            for one, to in (
                (error_hbm, error),
                (mixed_hbm, mixed),
                (arrays[0], grad),
                (arrays[1], live),
            )
        ]
    else:
        wait_all(arrived)

        def start(span, total):
            part = (live[span, :] * grad[span, :]).astype(BF16)
            branch[span, :] = part
            return total + jnp.sum(part.astype(F32), axis=0, keepdims=True)

        sums[0:1, :] = row_chunks(rows, start, zero)
        copies.send(branch, outs[-3])
    result = None
    for n, e in enumerate(picks):
        wait_all(loads[n])
        flow = dot(branch[...], second[n])
        slope_loads[n].wait()
        pre = (slopes[n].astype(F32) * flow).astype(BF16)
        pres[n] = pre
        copies.send(pres.at[n], outs[n])
        hidden_sums[n] = jnp.sum(pre.astype(F32), axis=0, keepdims=True)
        part = dot(pres[n], first[n], 1, 1)
        result = part if result is None else result + part
    if not end:
        error[...] = result
    else:
        wait_all(late)
        error[...] += result

        def finish(span, totals):
            back, gain_part, shift_part = norm_back_rows(
                mixed[span, :], vec_ref[3:4, :], error[span, :]
            )
            mixed_grad = grad[span, :] + back
            error[span, :] = mixed_grad
            low = (live[span, :] * mixed_grad).astype(BF16)
            attn_grad[span, :] = low
            bias_part = jnp.sum(low.astype(F32), axis=0, keepdims=True)
            return tuple(a + b for a, b in zip(totals, (gain_part, shift_part, bias_part)))

        totals = row_chunks(rows, finish, (zero, zero, zero))
        for index in range(3):
            sums[index : index + 1, :] = totals[index]
        copies.send(attn_grad, outs[-3])
    copies.send(error, outs[-4])
    copies.send(sums, outs[-2])
    copies.send(hidden_sums, outs[-1])
    copies.finish()


def ffn_backward(grad, slopes, weights, picks, vectors, live, earlier=()):
    rows, width = grad.shape
    plan, arrays, block_rows = choose(weights, picks)
    count = len(picks)
    end = bool(earlier)
    shape = jax.ShapeDtypeStruct
    low = shape((rows, width), BF16)
    wide = shape((rows, width), F32)
    results = call(
        functools.partial(ffn_backward_kernel, picks, plan, block_rows, end),
        "ffn_backward",
        9,
        (vectors,),
        [grad, live] + list(slopes) + list(earlier) + arrays,
        [low] * count + [wide, low, shape((8, width), F32), shape((count, 1, width), F32)],
        [like(wide), like(live), like(wide), like(low), like(wide), like(low)]
        + [pltpu.VMEM((count, rows, width), BF16)] * 2
        + [pltpu.VMEM((count, width, width), BF16)] * 2
        + [pltpu.VMEM((8, width), F32), pltpu.VMEM((count, 1, width), F32)],
        weight_copies(plan, 2) + 2 * count + 9,
    )
    return dict(zip(picks, results[:count])), *results[count:]


def weight_grad_kernel(terms, block_rows, plan, count, given, *refs):
    terms_count = sum(len(group) for group in terms)
    lefts_hbm, refs = refs[:terms_count], refs[terms_count:]
    rights_hbm, refs = refs[: terms_count * count], refs[terms_count * count :]
    added_hbm, refs = refs[:given], refs[given:]
    outs, refs = refs[: len(plan)], refs[len(plan) :]
    held, sems = refs[0], refs[-1]
    lefts, refs = refs[1 : 1 + terms_count], refs[1 + terms_count : -1]
    rights, refs = refs[:terms_count], refs[terms_count:]
    added, results = refs[:given], refs[given:]
    own = lax.axis_index("dp")
    blocks = held.shape[0]
    copies = Copies(sems)
    arrived = {}
    for n in range(count):
        for t in range(terms_count):
            waits = arrived.setdefault((n, t), [])
            if n == 0:
                waits.append(copies.fetch(lefts_hbm[t], lefts[t]))
            waits.append(copies.fetch(rights_hbm[t * count + n], rights[t].at[n]))
        if given:
            arrived[n] = copies.fetch(added_hbm[n], added[n])
    for n in range(count):
        for part, group in enumerate(terms):
            columns = []
            for t in group:
                wait_all(arrived[n, t])
                columns.append(dot(lefts[t][...], rights[t][n], 0, 0))
            value = columns[0] if len(columns) == 1 else jnp.concatenate(columns, axis=1)
            held[:, part * block_rows : (part + 1) * block_rows, :] = value.reshape(
                blocks, block_rows, value.shape[1]
            )
        if given:
            arrived[n].wait()
        for (piece, rels), result, out in zip(plan, results, outs):
            if piece != n:
                continue
            for place, rel in enumerate(rels):
                value = held[0 if rel is None else jnp.bitwise_xor(own, rel)]
                if given:
                    value = value + added[n][0 if rel is None else rel].astype(F32)
                result[place] = value.astype(BF16)
            copies.send(result, out)
    copies.finish()


def weight_grad(terms, pairs, plan, block_rows, added, micros):
    lefts = [left for left, _ in pairs]
    count = len(pairs[0][1])
    rights = [one for _, several in pairs for one in several]
    width = lefts[0].shape[1]
    height = len(terms) * block_rows
    outs = [jax.ShapeDtypeStruct((len(rels), height, width), BF16) for _, rels in plan]
    return call(
        functools.partial(weight_grad_kernel, terms, block_rows, plan, count, len(added)),
        "weight_grad",
        micros,
        (),
        lefts + rights + list(added),
        outs,
        [pltpu.VMEM((width // block_rows, height, width), F32)]
        + [like(left) for left in lefts]
        + [pltpu.VMEM((count,) + several[0].shape, BF16) for _, several in pairs]
        + [like(one) for one in added]
        + [like(out) for out in outs],
        len(lefts) + len(rights) + len(added) + len(outs),
    )


def attention_backward_kernel(heads, scale, picks, plan, block_rows, end, *refs):
    count = len(picks)
    vec_ref = refs[0]
    given = 1 + 4 * count + 3 * end
    arrays, refs = refs[1 : 1 + given], refs[1 + given :]
    weight_refs, refs = refs[: len(plan)], refs[len(plan) :]
    outs, refs = refs[: count + 3 + end], refs[count + 3 + end :]
    attn_grad, x, mixed_grad, error, weights, qs, ks, vs, ps, gs, grads, scores_sum, sums, small, sems = refs
    rows, width = attn_grad.shape
    columns = qs.shape[2]
    pairs = rows // (2 * PADDED)
    copies = Copies(sems)
    arrived = copies.fetch(arrays[0], attn_grad)
    loads = fetch_weights(copies, plan, weight_refs, block_rows, (weights,))
    saved = []
    for n in range(count):
        for index, buffer in enumerate((qs, ks, vs, ps)):
            saved.append(copies.fetch(arrays[1 + 4 * n + index], buffer.at[n]))
    if end:
        late = [
            copies.fetch(one, to)
            for one, to in zip(arrays[1 + 4 * count :], (x, mixed_grad, error))
        ]
    scores_sum[...] = jnp.zeros(scores_sum.shape, F32)
    arrived.wait()
    for n in range(count):
        wait_all(loads[n])
        gs[n] = dot(attn_grad[...], weights[n, :, 3 * columns :]).astype(BF16)
    wait_all(saved)

    def pair_step(pair, _):
        span = pl.ds(pl.multiple_of(pair * 2 * PADDED, 2 * PADDED), 2 * PADDED)
        for n in range(count):
            query, key, value, grad = [
                buffer[n, span, :].astype(F32) for buffer in (qs, ks, vs, gs)
            ]
            results = []
            for side in range(2):
                part = slice(side * PADDED, (side + 1) * PADDED)
                keys = spread_heads(key[part], heads)
                values = spread_heads(value[part], heads)
                grad_low = grad[part].astype(BF16)
                low = ps[n, 2 * pair + side]
                probs = low.astype(F32)
                flow = dot(values, grad_low, 1, 1)
                inner = jnp.sum(
                    (probs * flow).reshape(heads, PADDED, PADDED), axis=1, keepdims=True
                )
                score = probs.reshape(heads, PADDED, PADDED) * (
                    flow.reshape(heads, PADDED, PADDED) - inner
                )
                score = score.reshape(heads * PADDED, PADDED).astype(BF16)
                scores_sum[n] += score.astype(F32)
                results.append(
                    jnp.concatenate(
                        [
                            dot(score, keys, 0, 0) * scale,
                            merge_heads(dot(score, query[part].astype(BF16)), heads),
                            merge_heads(dot(low, grad_low), heads),
                        ],
                        axis=1,
                    )
                )
            grads[n, span, :] = jnp.concatenate(results, axis=0).astype(BF16)
        return 0

    lax.fori_loop(0, pairs, pair_step, 0)
    result = None
    for n in range(count):
        copies.send(grads.at[n], outs[n])
        sums[n] = jnp.sum(grads[n].astype(F32), axis=0, keepdims=True)
        part = dot(grads[n], weights[n, :, : 3 * columns], 1, 1)
        result = part if result is None else result + part
    copies.send(scores_sum, outs[count + 1])
    copies.send(sums, outs[count + 2])
    if not end:
        error[...] = result
    else:
        wait_all(late)
        error[...] += result
        zero = jnp.zeros((1, width), F32)

        def finish(span, totals):
            back, gain_part, shift_part = norm_back_rows(
                x[span, :], vec_ref[0:1, :], error[span, :]
            )
            error[span, :] = mixed_grad[span, :] + back
            return totals[0] + gain_part, totals[1] + shift_part

        totals = row_chunks(rows, finish, (zero, zero))
        for index in range(2):
            small[index : index + 1, :] = totals[index]
        copies.send(small, outs[count + 3])
    copies.send(error, outs[count])
    copies.finish()


def attention_backward(attn_grad, saved, weights, picks, vectors, heads, scale, earlier=()):
    rows, width = attn_grad.shape
    columns = saved[picks[0]][0].shape[1]
    plan, arrays, block_rows = choose(weights, picks)
    count = len(picks)
    end = bool(earlier)
    probs = saved[picks[0]][3]
    shape = jax.ShapeDtypeStruct
    wide = shape((rows, width), F32)
    pieces = [item for e in picks for item in saved[e][:4]]
    outs = [shape((rows, 3 * columns), BF16)] * count + [
        wide,
        shape((count, heads * PADDED, PADDED), F32),
        shape((count, 1, 3 * columns), F32),
    ]
    results = call(
        functools.partial(attention_backward_kernel, heads, scale, picks, plan, block_rows, end),
        "attention_backward",
        6 + 8 * count,
        (vectors,),
        [attn_grad] + pieces + list(earlier) + arrays,
        outs + [shape((8, width), F32)] * end,
        [like(attn_grad), like(wide), like(wide), like(wide)]
        + [pltpu.VMEM((count, width, width), BF16)]
        + [pltpu.VMEM((count, rows, columns), BF16)] * 3
        + [pltpu.VMEM((count,) + probs.shape, BF16)]
        + [pltpu.VMEM((count, rows, columns), BF16)]
        + [pltpu.VMEM((count, rows, 3 * columns), BF16)]
        + [like(outs[count + 1]), like(outs[count + 2]), pltpu.VMEM((8, width), F32)],
        weight_copies(plan, 1) + 5 * count + 9,
    )
    return dict(zip(picks, results[:count])), *results[count:]


def swap(values, axis, bit):
    size = lax.axis_size(axis)
    return lax.ppermute(values, axis, [(i, i ^ (1 << bit)) for i in range(size)])


def bits_in(axis):
    return lax.axis_size(axis).bit_length() - 1


def pick(values, index, dim):
    return lax.dynamic_index_in_dim(values, index, dim, keepdims=False)


def tie(values, token):
    if token is None:
        return values
    return lax.optimization_barrier((values, token))[0]


def whole_tiles(rows):
    return rows % 16 == 0


def in_order(values):
    index = jnp.bitwise_xor(jnp.arange(values.shape[0]), lax.axis_index("dp"))
    return jnp.take(values, index, axis=0)


def relatives(halves):
    count = lax.axis_size("dp")
    size = count // halves
    return [
        [tuple(range(part * size + side, (part + 1) * size, 2)) for part in range(halves)]
        for side in range(2)
    ]


class Gather:
    def __init__(self, shard, parts, ways):
        self.shard = shard
        self.parts = parts
        self.ways = ways
        self.bits = list(range(1, bits_in("dp")))
        self.entries = []

    def line(self, after=None):
        held = tie(self.shard, after)[None]
        for bit in self.bits[:-1]:
            held = jnp.concatenate([held, swap(held, "dp", bit)])
        self.held = [held]
        return held

    def last(self, after=None):
        self.moved = swap(tie(self.held[0], after), "dp", self.bits[-1])

    def last_end(self, until=None):
        moved = tie(self.moved, until)
        if len(self.ways) == 2:
            self.held.append(moved)
        else:
            self.held = [jnp.concatenate([self.held[0], moved])]
        return moved

    def sides(self, parts, after=None):
        if parts[0] == 0:
            self.side, self.far = [], []
        for part in parts:
            held = tie(self.held[part], after)
            self.side.append(swap(held, "dp", 0))
            self.far.append(swap(held, "head", 1))

    def sides_end(self, parts, until=None):
        for part in parts:
            self.side[part], self.far[part] = tie((self.side[part], self.far[part]), until)

    def corner(self, part, after=None):
        if part == 0:
            self.corners = []
        if self.ways[part] == "x":
            self.corners.append(swap(tie(self.side[part], after), "head", 1))
        else:
            self.corners.append(swap(tie(self.far[part], after), "dp", 0))

    def corner_end(self, part, until=None):
        self.corners[part] = tie(self.corners[part], until)
        return self.corners[part]

    def core(self, kind):
        own, other = relatives(len(self.ways))
        arrays, e, rels = {
            "held": (self.held, 0, own),
            "side": (self.side, 0, other),
            "far": (self.far, 2, own),
            "corner": (getattr(self, "corners", None), 2, other),
        }[kind]
        for one, several in zip(arrays, rels):
            self.entries.append((e, one, several))
            self.entries.append((e + 1, swap(one, "head", 0), several))

    def result(self):
        rows = self.shard.shape[0] // self.parts
        width = self.shard.shape[1]
        if whole_tiles(rows):
            plan = tuple((e, rels) for e, _, rels in self.entries)
            return plan, [one for _, one, _ in self.entries], rows
        arrays = []
        plan = []
        for e in range(PIECES):
            mine = [(one, rels) for piece, one, rels in self.entries if piece == e]
            if not mine:
                continue
            order = sum((rels for _, rels in mine), ())
            blocks = jnp.concatenate([one for one, _ in mine])
            blocks = in_order(blocks[jnp.argsort(jnp.array(order))])
            blocks = blocks.reshape(-1, self.parts, rows, width).transpose(1, 0, 2, 3)
            arrays.append(blocks.reshape(1, -1, width))
            plan.append((e, (None,)))
        return tuple(plan), arrays, arrays[0].shape[1] // self.parts


def plus(left, right):
    return (left.astype(F32) + right.astype(F32)).astype(BF16)


class Scatter:
    def __init__(self, terms, rows, micros, ways):
        self.terms = terms
        self.rows = rows
        self.micros = micros
        self.ways = ways
        self.blocks = lax.axis_size("dp")
        self.tiled = whole_tiles(rows)
        self.every = tuple(range(self.blocks)) if self.tiled else (None,)
        self.block_rows = rows if self.tiled else rows * self.blocks
        self.bits = list(reversed(range(1, bits_in("dp"))))

    def away(self, pairs):
        plan = ((0, self.every), (1, self.every))
        self.sent = weight_grad(self.terms, pairs, plan, self.block_rows, (), self.micros)
        return self.sent

    def core(self):
        self.added = [swap(one, "head", 0) for one in self.sent]

    def near(self, pairs, until=None):
        added = tie(self.added, until)
        halves = len(self.ways)
        quarters = [rels for side in relatives(halves) for rels in side]
        if self.tiled:
            plan = tuple((n, rels) for n in range(2) for rels in quarters)
        else:
            plan = ((0, self.every), (1, self.every))
        outs = weight_grad(self.terms, pairs, plan, self.block_rows, added, self.micros)
        if not self.tiled:
            parts, rows = len(self.terms), self.rows
            result = []
            for one in outs:
                one = one.reshape(parts, self.blocks, rows, -1).transpose(1, 0, 2, 3)
                one = in_order(one.reshape(self.blocks, parts * rows, -1))
                result += [one[jnp.array(rels)] for rels in quarters]
            outs = result
        self.held, self.side, self.far, self.corners = [
            list(outs[halves * n : halves * (n + 1)]) for n in range(4)
        ]
        return outs

    def corner(self, after=None):
        self.moved = []
        for way, one in zip(self.ways, tie(self.corners, after)):
            self.moved.append(swap(one, "head", 1) if way == "x" else swap(one, "dp", 0))

    def corner_end(self, until=None):
        moved = tie(self.moved, until)
        for part, way in enumerate(self.ways):
            target = self.side if way == "x" else self.far
            target[part] = plus(target[part], moved[part])

    def sides(self, after=None):
        side, far = tie((self.side, self.far), after)
        self.moved = [
            (swap(side[part], "dp", 0), swap(far[part], "head", 1))
            for part in reversed(range(len(self.ways)))
        ][::-1]

    def sides_end(self, until=None):
        moved = tie(self.moved, until)
        for part, (one, other) in enumerate(moved):
            self.held[part] = plus(self.held[part].astype(F32) + one.astype(F32), other)

    def last(self, after=None):
        if len(self.held) == 1:
            cut = self.held[0].shape[0] // 2
            self.held = [self.held[0][:cut], self.held[0][cut:]]
        self.moved = swap(tie(self.held[1], after), "dp", self.bits[0])

    def last_end(self, until=None):
        self.held = plus(self.held[0], tie(self.moved, until))

    def line(self, after=None):
        held = tie(self.held, after)
        for bit in self.bits[1:]:
            cut = held.shape[0] // 2
            moved = swap(held[cut:], "dp", bit)
            held = held[:cut].astype(F32) + moved.astype(F32)
            held = held if bit == self.bits[-1] else held.astype(BF16)
        self.held = held

    def line_end(self, until=None):
        self.result = tie(self.held, until)[0].astype(F32)
        return self.result


class SmallSum:
    def __init__(self, values):
        self.total = values
        self.left = [("head", 0), ("head", 1)]
        self.left += [("dp", bit) for bit in range(bits_in("dp"))]
        self.moved = None

    def step(self, until=None):
        self.result(until)
        axis, bit = self.left.pop(0)
        self.moved = swap(self.total, axis, bit)

    def end(self):
        return not self.left

    def result(self, until=None):
        if self.moved is not None:
            self.total = self.total + tie(self.moved, until)
        self.moved = None
        return self.total


class SmallGather:
    def __init__(self, values):
        self.held = values[None, None]
        self.steps = [("dp", bit) for bit in range(1, bits_in("dp"))]
        self.steps += [("dp", 0), ("head", 1), ("head", 0)]
        self.done = []

    def step(self, after=None):
        axis, bit = self.steps[len(self.done)]
        self.done.append((axis, bit))
        held = tie(self.held, after)
        self.held = jnp.concatenate([held, swap(held, axis, bit)], axis=0 if axis == "dp" else 1)

    def result(self):
        for axis, dim in (("dp", 0), ("head", 1)):
            order = [bit for name, bit in self.done if name == axis]
            index = jnp.arange(lax.axis_size(axis)) ^ lax.axis_index(axis)
            place = sum(((index >> bit) & 1) << n for n, bit in enumerate(order))
            self.held = jnp.take(self.held, place, axis=dim)
        return self.held


def unshift(values):
    grid = values.reshape(values.shape[:-1] + (WSIDE, WSIDE))
    return jnp.roll(grid, (SHIFT, SHIFT), axis=(-2, -1)).reshape(values.shape)


def pad_rows(values):
    grid = values.reshape(-1, WTOK, values.shape[1])
    grid = jnp.pad(grid, ((0, 0), (0, PADDED - WTOK), (0, 0)))
    return grid.reshape(-1, values.shape[1])


def drop_rows(values):
    grid = values.reshape(-1, PADDED, values.shape[1])[:, :WTOK]
    return grid.reshape(-1, values.shape[1])


def attention_mask(pad, region):
    allowed = (pad[:, :, None] == 1) & (region[:, :, None] == region[:, None, :])
    mask = jnp.where(allowed, 0.0, MASKED).astype(F32)
    extra = PADDED - WTOK
    mask = jnp.pad(mask, ((0, 0), (0, 0), (0, extra)))
    return jnp.pad(mask, ((0, 0), (0, extra), (0, 0)), constant_values=ABSENT)


def shards(
    tokens,
    cotangent,
    crop_counts,
    pad_mask,
    region_ids,
    rel_index,
    norm_gain,
    norm_shift,
    qkv_weight,
    qv_bias,
    bias_table,
    proj_weight,
    fc1_weight,
    fc1_bias,
    fc2_weight,
    out_bias,
):
    rows = tokens.shape[0]
    width = tokens.shape[1]
    wins = rows // WTOK
    local_width = qkv_weight.shape[3]
    local_heads = bias_table.shape[1]
    rel_count = bias_table.shape[2]
    dp_width = norm_gain.shape[2]
    dp_hidden = fc1_bias.shape[1]
    pieces = lax.axis_size("head")
    heads_total = local_heads * pieces
    head_dim = local_width // local_heads
    scale = head_dim ** (-0.5)
    head_index = lax.axis_index("head")
    dp_index = lax.axis_index("dp")
    relative = [head_index ^ e for e in range(pieces)]

    shard_rows = qkv_weight.shape[1]
    attn_shards = [
        jnp.concatenate(
            [qkv_weight[block].reshape(-1, 3 * local_width), proj_weight[block].T], axis=1
        )
        for block in range(BLOCKS)
    ]
    ffn_shards = [
        jnp.concatenate([fc1_weight[block], fc2_weight[block].T]) for block in range(BLOCKS)
    ]
    small = jnp.concatenate(
        [item.reshape(-1) for item in (norm_gain, norm_shift, qv_bias, out_bias, fc1_bias, bias_table)]
    )
    small = jnp.pad(small, (0, -small.shape[0] % 128))
    near, away = (0, 2), (1, 3)
    first, second = (0, 1), (2, 3)
    attn_gather = [Gather(shard, 1, "x") for shard in attn_shards]
    ffn_gather = [Gather(shard, 2, "xy") for shard in ffn_shards]
    a0, a1 = attn_gather
    f0, f1 = ffn_gather
    small_gather = SmallGather(small)
    a0.line()
    small_gather.step()
    a0.last()
    f0.line(a0.held)
    for _ in range(bits_in("dp") - 2):
        small_gather.step(a0.held)
    a0.last_end()
    a0.sides((0,))
    a0.core("held")
    small_gather.step(a0.held)
    f0.last(a0.held)
    a0.sides_end((0,))
    a0.core("side")
    small_gather.step(a0.far)
    small_gather.step(a0.far)
    small_all = small_gather.result()
    offset = 0
    vectors = []
    for item in (norm_gain, norm_shift, qv_bias, out_bias):
        count = item.size
        piece = small_all[:, 0, offset : offset + count].reshape(-1, BLOCKS, 2, dp_width)
        vectors.append(piece.transpose(1, 2, 0, 3).reshape(BLOCKS, 2, width).astype(F32))
        offset += count
    gains, shifts, qv_all, out_all = vectors
    hidden_bias = small_all[:, 0, offset : offset + fc1_bias.size].reshape(-1, BLOCKS, dp_hidden)
    hidden_bias = hidden_bias.transpose(1, 0, 2).reshape(BLOCKS, pieces, -1).astype(F32)
    offset += fc1_bias.size
    tables = small_all[0, :, offset : offset + bias_table.size]
    tables = tables.reshape(pieces, BLOCKS, local_heads, rel_count)
    qv_pieces = qv_all.reshape(BLOCKS, 2, pieces, local_width)

    counts = jnp.repeat(crop_counts, CROP_MAX)
    slots = jnp.arange(pad_mask.shape[0], dtype=jnp.int32) % CROP_MAX
    live_all = (slots < counts).astype(F32)
    live_windows = lax.dynamic_slice_in_dim(live_all, head_index * wins, wins, 0)
    real = (jnp.arange(PADDED) < WTOK).astype(F32)
    live = (live_windows[:, None] * real[None, :]).reshape(-1, 1)
    pad = lax.dynamic_slice_in_dim(pad_mask, head_index * wins, wins, 0)
    region = unshift(lax.dynamic_slice_in_dim(region_ids, head_index * wins, wins, 0))
    masks = (attention_mask(pad, jnp.zeros_like(region)), attention_mask(pad, region))
    extra = PADDED - WTOK
    onehots = []
    for index in (rel_index, unshift(unshift(rel_index).T).T):
        by_key = jnp.pad(index.T, ((0, extra), (0, extra)), constant_values=-1).reshape(1, -1)
        ids = jnp.arange(rel_count, dtype=jnp.int32)[:, None]
        onehots.append((ids == by_key).astype(BF16))

    def ordered(values, dim):
        return jnp.stack([pick(values, rel, dim) for rel in relative])

    block_rows = local_heads * PADDED
    vectors, qv, biases, hidden_biases = [], [], [], []
    for block in range(BLOCKS):
        rows8 = [
            gains[block, 0],
            shifts[block, 0],
            out_all[block, 0],
            gains[block, 1],
            shifts[block, 1],
            out_all[block, 1],
        ]
        vectors.append(jnp.pad(jnp.stack(rows8), ((0, 2), (0, 0))))
        qv.append(ordered(qv_pieces[block], 1))
        table = ordered(tables[:, block], 0).reshape(heads_total, rel_count)
        bias = jnp.dot(table, onehots[block % 2], preferred_element_type=F32)
        biases.append(bias.reshape(pieces, block_rows, PADDED))
        hidden_biases.append(ordered(hidden_bias[block], 0)[:, None, :])

    residual = pad_rows(tokens).astype(F32)

    def attend(block, x, picks, token, earlier=()):
        return attention_forward(
            x,
            attn_gather[block].result(),
            picks,
            tie(vectors[block], token),
            qv[block],
            biases[block],
            masks[block % 2],
            live,
            local_heads,
            scale,
            earlier,
        )

    def feed(block, normed2, picks, token, earlier=()):
        return ffn_forward(
            normed2,
            ffn_gather[block].result(),
            picks,
            hidden_biases[block],
            tie(vectors[block], token),
            live,
            earlier,
        )

    x0 = residual
    a0.corner(0)
    f0.sides((0,), a0.far)
    saved_0, branch, normed_0 = attend(0, x0, first, None)
    a0.corner_end(0, branch)
    f0.last_end(branch)
    f0.sides_end((0,), branch)
    a0.core("far")
    a0.core("corner")
    f0.core("held")
    f0.sides((1,))
    f0.corner(0)
    a1.line(f0.held[1])
    more, mixed_0, normed2_0 = attend(0, x0, second, None, (normed_0, branch))
    saved_0.update(more)
    a1.last((a1.held, mixed_0))
    f0.sides_end((1,), mixed_0)
    f0.core("side")
    f0.corner(1)
    f1.line(a1.held)
    f0.core("far")
    hidden_0, branch = feed(0, normed2_0, first, None)
    f0.corner_end(0, branch)
    f0.corner_end(1, branch)
    f0.core("corner")
    a1.last_end(branch)
    a1.sides((0,))
    a1.core("held")
    f1.last((f1.held, a1.held))
    more, x1 = feed(0, normed2_0, second, None, (mixed_0, branch))
    hidden_0.update(more)
    a1.sides_end((0,), x1)
    a1.core("side")
    a1.corner(0)
    f1.sides((0,), x1)
    saved_1, branch, normed_1 = attend(1, x1, first, None)
    a1.corner_end(0, branch)
    a1.core("far")
    a1.core("corner")
    f1.last_end(branch)
    f1.sides_end((0,), branch)
    f1.core("held")
    f1.sides((1,))
    f1.corner(0)
    more, mixed_1, normed2_1 = attend(1, x1, second, None, (normed_1, branch))
    saved_1.update(more)
    f1.sides_end((1,), mixed_1)
    f1.core("side")
    f1.corner(1)
    f1.core("far")
    hidden_1, branch = feed(1, normed2_1, first, None)
    f1.corner_end(0, branch)
    f1.corner_end(1, branch)
    f1.core("corner")
    more, residual = feed(1, normed2_1, second, None, (mixed_1, branch))
    hidden_1.update(more)
    kept = [
        (x0, mixed_0, normed_0, normed2_0, saved_0, hidden_0),
        (x1, mixed_1, normed_1, normed2_1, saved_1, hidden_1),
    ]

    grad_rows = pad_rows(cotangent).astype(F32)
    shard_grads = [None] * BLOCKS
    small_sums = [None] * BLOCKS
    token = residual
    old_f = old_a = None
    for block in reversed(range(BLOCKS)):
        x, mixed, normed, normed2, saved, hidden = kept[block]
        ffn_sum = Scatter(((0,), (1,)), shard_rows, 8, "xy")
        attn_sum = Scatter(((0, 1),), shard_rows, 7, "x" if block else "y")
        ffn_w = ffn_gather[block].result()
        attn_w = attn_gather[block].result()

        def ffn_pairs(picks, pre, token):
            return (
                (tie(normed2, token), [pre[e] for e in picks]),
                (branch_grad, [hidden[e][0] for e in picks]),
            )

        def attn_pairs(picks, qkv, token):
            return (
                (tie(normed, token), [qkv[e] for e in picks]),
                (attn_grad, [saved[e][4] for e in picks]),
            )

        pre_a, error, branch_grad, small_b, hidden_a = ffn_backward(
            grad_rows,
            [hidden[e][1] for e in away],
            ffn_w,
            away,
            tie(vectors[block], token),
            live,
        )
        token = None
        if old_a is not None:
            old_a.corner_end(error)
            token = (old_a.side, old_a.far)
            old_a.sides()
        sent = ffn_sum.away(ffn_pairs(away, pre_a, token))
        ffn_sum.core()
        token = sent
        if old_f is not None:
            old_f.last_end(sent)
            token = (sent, old_f.held)
            old_f.line()
        pre_n, mixed_grad, attn_grad, small_f, hidden_n = ffn_backward(
            grad_rows,
            [hidden[e][1] for e in near],
            ffn_w,
            near,
            tie(vectors[block], token),
            live,
            (mixed, branch_grad, error),
        )
        token = None
        if old_a is not None:
            old_f.line_end(attn_grad)
            old_a.sides_end(attn_grad)
            token = (old_f.result, old_a.held)
            old_a.last()
        ready = ffn_sum.near(ffn_pairs(near, pre_n, token), attn_grad)
        ffn_sum.corner()
        qkv_a, error, scores_a, sums_a = attention_backward(
            attn_grad, saved, attn_w, away, tie(vectors[block], ready), local_heads, scale
        )
        ffn_sum.corner_end(error)
        token = (ffn_sum.side, ffn_sum.far)
        ffn_sum.sides()
        if old_a is not None:
            old_a.last_end(error)
            token = (token, old_a.held)
            old_a.line()
        sent = attn_sum.away(attn_pairs(away, qkv_a, token))
        attn_sum.core()
        token = sent
        if old_a is not None:
            token = (sent, old_a.line_end(sent))
        qkv_n, grad_rows, scores_n, sums_n, small_a = attention_backward(
            attn_grad,
            saved,
            attn_w,
            near,
            tie(vectors[block], token),
            local_heads,
            scale,
            (x, mixed_grad, error),
        )
        ffn_sum.sides_end(grad_rows)
        token = ffn_sum.held
        ffn_sum.last()
        token = attn_sum.near(attn_pairs(near, qkv_n, token), grad_rows)
        attn_sum.corner()
        old_f, old_a = ffn_sum, attn_sum
        shard_grads[block] = (attn_sum, ffn_sum)

        def together(one, other):
            return ordered(jnp.stack([one[0], other[0], one[1], other[1]]), 0)

        table_grad = lax.dot_general(
            together(scores_n, scores_a).reshape(heads_total, -1),
            onehots[block % 2].astype(F32),
            (((1,), (1,)), ((), ())),
            precision=lax.Precision.HIGHEST,
            preferred_element_type=F32,
        )
        qv_sums = together(sums_n, sums_a)[:, 0]
        items = [
            small_a[0],
            small_f[0],
            small_a[1],
            small_f[1],
            qv_sums[:, :local_width].reshape(-1),
            qv_sums[:, 2 * local_width :].reshape(-1),
            small_f[2],
            small_b[0],
            together(hidden_n, hidden_a).reshape(-1),
            table_grad.reshape(-1),
        ]
        small_sums[block] = jnp.concatenate(items)
    small_sum = SmallSum(tie(jnp.stack(small_sums), token))
    small_sum.step()
    old_a.corner_end()
    small_sum.step(until=old_a.side)
    old_a.sides()
    old_f.last_end(token)
    old_f.line()
    old_a.sides_end()
    small_sum.step(until=old_a.held)
    old_a.last()
    old_a.last_end()
    while not small_sum.end():
        small_sum.step(until=old_a.held)
    old_a.line()
    old_a.line_end()
    old_f.line_end()
    shard_grads = [
        (attn.result, ffn.result[:shard_rows], ffn.result[shard_rows:])
        for attn, ffn in shard_grads
    ]

    totals = small_sum.result()

    def own(values):
        return lax.dynamic_slice_in_dim(values, dp_index * dp_width, dp_width, 2)

    small_grads = []
    for index in range(4):
        part = totals[:, 2 * index * width : 2 * (index + 1) * width]
        small_grads.append(own(part.reshape(BLOCKS, 2, width)))
    offset = 8 * width
    hidden_total = totals[:, offset : offset + pieces * fc1_weight.shape[2]]
    fc1_bias_grad = lax.dynamic_slice_in_dim(hidden_total, dp_index * dp_hidden, dp_hidden, 1)
    offset += hidden_total.shape[1]
    table_total = totals[:, offset:].reshape(BLOCKS, heads_total, rel_count)
    bias_table_grad = lax.dynamic_slice_in_dim(
        table_total, head_index * local_heads, local_heads, 1
    )
    qkv_weight_grad = jnp.stack(
        [item[0][:, : 3 * local_width].reshape(-1, 3, local_width) for item in shard_grads]
    )
    proj_weight_grad = jnp.stack([item[0][:, 3 * local_width :].T for item in shard_grads])
    fc1_weight_grad = jnp.stack([item[1] for item in shard_grads])
    fc2_weight_grad = jnp.stack([item[2].T for item in shard_grads])
    return (
        drop_rows(residual),
        drop_rows(grad_rows),
        small_grads[0],
        small_grads[1],
        qkv_weight_grad,
        small_grads[2],
        bias_table_grad,
        proj_weight_grad,
        fc1_weight_grad,
        fc1_bias_grad,
        fc2_weight_grad,
        small_grads[3],
    )


def solution(mesh):
    placed = (
        P(("dp", "head"), None),
        P(("dp", "head"), None),
        P("dp"),
        P("dp", None),
        P("dp", None),
        P(),
        P(None, None, "dp"),
        P(None, None, "dp"),
        P(None, "dp", None, "head"),
        P(None, None, "dp"),
        P(None, "head", None),
        P(None, "head", "dp"),
        P(None, "dp", "head"),
        P(None, "dp"),
        P(None, "head", "dp"),
        P(None, None, "dp"),
    )
    return jax.shard_map(
        shards,
        mesh=mesh,
        in_specs=placed,
        out_specs=(
            P(("dp", "head"), None),
            P(("dp", "head"), None),
            P(None, None, "dp"),
            P(None, None, "dp"),
            P(None, "dp", None, "head"),
            P(None, None, "dp"),
            P(None, "head", None),
            P(None, "head", "dp"),
            P(None, "dp", "head"),
            P(None, "dp"),
            P(None, "head", "dp"),
            P(None, None, "dp"),
        ),
        check_vma=False,
    )
```

time: 1130 us -> 596 us (0.53)
  matrix products: 362 us -> 3.94 us
  Pallas kernels: 0 us -> 301 us
  local copies, waits for them, and re-layouts: 301 us -> 48.6 us
  other arithmetic: 140 us -> 27.6 us
  waiting for transfers between devices: 235 us -> 128 us
    dot_general x152 -> x4, matrix products: 335 us -> 3.94 us  [the longest x2 3.01 us: shards(): lax.dot_general(together(scores_n, scores_a).reshape(heads_total, -1), on...]
    pallas_call x0 -> x24, Pallas kernels: none -> 301 us  [call(): pl.pallas_call(kernel, in_specs=in_vmem(len(small)) + in_any(len(arrays))...]
    ppermute x93 -> x94, waiting for transfers between devices: 235 us -> 128 us  [swap(): return lax.ppermute(values, axis, [(i, i ^ 1 << bit) for i in range(size)])]
    reshape x72 -> x16, local copies, waits for them, and re-layouts: 102 us -> 7.1 us  [the longest x2 3.02 us: drop_rows(): return grid.reshape(-1, values.shape[1])]
    convert_element_type x59 -> x0, local copies, waits for them, and re-layouts: 63.6 us -> none  [the longest x24 28.8 us: shards(): item.astype(BF16).reshape(rows, local_width)]
    unnamed x707 -> x134, local copies, waits for them, and re-layouts: 62.3 us -> 8.38 us
    select_n x36 -> x6, other arithmetic: 51.1 us -> 1.33 us  [the longest x2 1.02 us: attention_mask(): mask = jnp.where(allowed, 0.0, MASKED).astype(F32)]
    sub x8 -> x0, matrix products: 27.6 us -> none  [shards(): expo = jnp.exp(scores - peak)]
  transfers between devices with their start and end apart: 93 -> 94, of which waited for: 33 -> 25; matrix products, arithmetic and copies ran while one was open for 43% -> 11% of each run, Pallas kernels for 0% -> 43%
where the time goes in v3:
time: 596 us; the launch traced here: 586 us
  Pallas kernels  301 us (51%)
  waiting for transfers between devices  128 us (21%)
  starting transfers between devices  73.9 us (12%)
  local copies, waits for them, and re-layouts  48.6 us (8%)
  other arithmetic  27.6 us (5%)
    pallas_call x24, Pallas kernels, call(): pl.pallas_call(kernel, in_specs=in_vmem(len(small)) + in_any(len(arrays))...  301 us
    ppermute x94, waiting for transfers between devices, swap(): return lax.ppermute(values, axis, [(i, i ^ 1 << bit) for i in range(size)])  128 us
    ppermute x94, starting transfers between devices, swap(): return lax.ppermute(values, axis, [(i, i ^ 1 << bit) for i in range(size)])  73.9 us
    convert_element_type x16, other arithmetic, plus(): return (left.astype(F32) + right.astype(F32)).astype(BF16)  13.3 us
  transfers between devices with their start and end apart: 94, of which 25 were waited for; matrix products, arithmetic and copies ran while one was open for 11% of the time, Pallas kernels for 43%

profile of v3, /device:TPU:0, one launch (start us, length us, event | category | flops | bytes accessed | tf_op | source)
XLA Modules:
  0.0 586.2 jit_solution(14948602949931304749)
XLA Ops:
  22.4 13.1 %collective-permute-done.3 = bf16[2,96,768]{2,1,0:T(8,128)(2,1)S(1)} collective-permute-done((bf16[2,96,768]{2,1,0:T(8,128)(2,1)S(1)}, bf16[2,96,768]{2,1,0:T(8,128)(2,1)S(1)}, u32[]{:S(2)}, u32[]{:S(2)}) %collective-permute-start.3) | collective-permute-done | bytes 294944 | tf_op jit(solution)/shard_map/ppermute | solution.py:667
  77.0 16.8 %attention_forward.4 = (bf16[672,192]{1,0:T(8,128)(2,1)}, bf16[672,192]{1,0:T(8,128)(2,1)}, bf16[672,192]{1,0:T(8,128)(2,1)}, bf16[12,336,56]{2,1,0:T(8,128)(2,1...) custom-call(f32[8,768]{1,0:T(8,128)} %pad.41.refs_0_.refs_1_, ...), custom_call_target="tpu_custom_call" | custom-call | flops 16000000000 | bytes 48000000 | tf_op jit(solution)/shard_map/attention_forward/pallas_call | solution.py:141
  98.7 17.4 %attention_forward.5 = (bf16[672,192]{1,0:T(8,128)(2,1)}, bf16[672,192]{1,0:T(8,128)(2,1)}, bf16[672,192]{1,0:T(8,128)(2,1)}, bf16[12,336,56]{2,1,0:T(8,128)(2,1...) custom-call(f32[8,768]{1,0:T(8,128)} %pad.41.refs_0_.refs_1_, ...), custom_call_target="tpu_custom_call" | custom-call | flops 16000000000 | bytes 48000000 | tf_op jit(solution)/shard_map/attention_forward/pallas_call | solution.py:141
  121.6 9.4 %ffn_forward.4 = (bf16[672,768]{1,0:T(8,128)(2,1)}, bf16[672,768]{1,0:T(8,128)(2,1)}, bf16[672,768]{1,0:T(8,128)(2,1)}, bf16[672,768]{1,0:T(8,128)(2,1)}, f32[672,768]{1,0:T(8,128)}) custom-call(f32[4,1,768]{2,1,0:T(1,128)} %broadcast_in_dim.68.refs_0_, f32[8,768]{1,0:T(8,128)} %pad.41.refs_0_.refs_1_, bf16[672,768]{1,0:T(8,128)(2,1)} %get-tuple-element.373.refs_2_.refs_0_, ...), custom_call_target="tpu_custom_call" | custom-call | flops 8999999488 | bytes 27000000 | tf_op jit(solution)/shard_map/ffn_forward/pallas_call | solution.py:141
  139.4 14.3 %collective-permute-done.31 = bf16[2,96,768]{2,1,0:T(8,128)(2,1)S(1)} collective-permute-done((bf16[2,96,768]{2,1,0:T(8,128)(2,1)S(1)}, bf16[2,96,768]{2,1,0:T(8,128)(2,1)S(1)}, u32[]{:S(2)}, u32[]{:S(2)}) %collective-permute-start.31) | collective-permute-done | bytes 294944 | tf_op jit(solution)/shard_map/ppermute | solution.py:667
  155.0 10.2 %ffn_forward.5 = (bf16[672,768]{1,0:T(8,128)(2,1)}, bf16[672,768]{1,0:T(8,128)(2,1)}, bf16[672,768]{1,0:T(8,128)(2,1)}, bf16[672,768]{1,0:T(8,128)(2,1)}, f32[672,768]{1,0:T(8,128)}) custom-call(f32[4,1,768]{2,1,0:T(1,128)} %broadcast_in_dim.68.refs_0_, f32[8,768]{1,0:T(8,128)} %pad.41.refs_0_.refs_1_, bf16[672,768]{1,0:T(8,128)(2,1)} %get-tuple-element.373.refs_2_.refs_0_, ...), custom_call_target="tpu_custom_call" | custom-call | flops 8999999488 | bytes 27000000 | tf_op jit(solution)/shard_map/ffn_forward/pallas_call | solution.py:141
  186.0 17.0 %attention_forward.6 = (bf16[672,192]{1,0:T(8,128)(2,1)}, bf16[672,192]{1,0:T(8,128)(2,1)}, bf16[672,192]{1,0:T(8,128)(2,1)}, bf16[12,336,56]{2,1,0:T(8,128)(2,1...) custom-call(f32[8,768]{1,0:T(8,128)} %pad.40.refs_0_.refs_1_, ...), custom_call_target="tpu_custom_call" | custom-call | flops 16000000000 | bytes 48000000 | tf_op jit(solution)/shard_map/attention_forward/pallas_call | solution.py:141
  213.6 17.6 %attention_forward.7 = (bf16[672,192]{1,0:T(8,128)(2,1)}, bf16[672,192]{1,0:T(8,128)(2,1)}, bf16[672,192]{1,0:T(8,128)(2,1)}, bf16[12,336,56]{2,1,0:T(8,128)(2,1...) custom-call(f32[8,768]{1,0:T(8,128)} %pad.40.refs_0_.refs_1_, ...), custom_call_target="tpu_custom_call" | custom-call | flops 16000000000 | bytes 48000000 | tf_op jit(solution)/shard_map/attention_forward/pallas_call | solution.py:141
  235.0 9.5 %ffn_forward.6 = (bf16[672,768]{1,0:T(8,128)(2,1)}, bf16[672,768]{1,0:T(8,128)(2,1)}, bf16[672,768]{1,0:T(8,128)(2,1)}, bf16[672,768]{1,0:T(8,128)(2,1)}, f32[672,768]{1,0:T(8,128)}) custom-call(f32[4,1,768]{2,1,0:T(1,128)} %broadcast_in_dim.67.refs_0_, f32[8,768]{1,0:T(8,128)} %pad.40.refs_0_.refs_1_, bf16[672,768]{1,0:T(8,128)(2,1)} %get-tuple-element.265.refs_2_.refs_0_, ...), custom_call_target="tpu_custom_call" | custom-call | flops 8999999488 | bytes 27000000 | tf_op jit(solution)/shard_map/ffn_forward/pallas_call | solution.py:141
  251.4 10.2 %ffn_forward.7 = (bf16[672,768]{1,0:T(8,128)(2,1)}, bf16[672,768]{1,0:T(8,128)(2,1)}, bf16[672,768]{1,0:T(8,128)(2,1)}, bf16[672,768]{1,0:T(8,128)(2,1)}, f32[672,768]{1,0:T(8,128)}) custom-call(f32[4,1,768]{2,1,0:T(1,128)} %broadcast_in_dim.67.refs_0_, f32[8,768]{1,0:T(8,128)} %pad.40.refs_0_.refs_1_, bf16[672,768]{1,0:T(8,128)(2,1)} %get-tuple-element.265.refs_2_.refs_0_, ...), custom_call_target="tpu_custom_call" | custom-call | flops 8999999488 | bytes 27000000 | tf_op jit(solution)/shard_map/ffn_forward/pallas_call | solution.py:141
  261.7 10.6 %ffn_backward.4 = (bf16[672,768]{1,0:T(8,128)(2,1)}, bf16[672,768]{1,0:T(8,128)(2,1)}, f32[672,768]{1,0:T(8,128)}, bf16[672,768]{1,0:T(8,128)(2,1)}, f32[8,768]{1,0:T(8,128)}, /*index=5*/f32[2,1,768]{2,1,0:T(1,128)}) custom-call(f32[8,768]{1,0:T(8,128)} %pad.40.refs_0_.refs_1_, f32[672,768]{1,0:T(8,128)} %bitcast_convert_fusion.refs_1_, ...), custom_call_target="tpu_custom_call" | custom-call | flops 8999999488 | bytes 27000000 | tf_op jit(solution)/shard_map/ffn_backward/pallas_call | solution.py:141
  272.3 9.3 %weight_grad.8 = (bf16[8,192,768]{2,1,0:T(8,128)(2,1)}, bf16[8,192,768]{2,1,0:T(8,128)(2,1)}) custom-call(bf16[672,768]{1,0:T(8,128)(2,1)} %get-tuple-element.265.refs_2_.refs_0_, bf16[672,768]{1,0:T(8,128)(2,1)} %get-tuple-element.282.refs_1_.refs_6_, bf16[672,768]{1,0:T(8,128)(2,1)} %get-tuple-element.283.refs_2_, ...), custom_call_target="tpu_custom_call" | custom-call | flops 8000000000 | bytes 24000000 | tf_op jit(solution)/shard_map/weight_grad/pallas_call | solution.py:141
  283.7 14.1 %ffn_backward.5 = (bf16[672,768]{1,0:T(8,128)(2,1)}, bf16[672,768]{1,0:T(8,128)(2,1)}, f32[672,768]{1,0:T(8,128)}, bf16[672,768]{1,0:T(8,128)(2,1)}, f32[8,768]{1,0:T(8,128)}, /*index=5*/f32[2,1,768]{2,1,0:T(1,128)}) custom-call(f32[8,768]{1,0:T(8,128)} %pad.40.refs_0_.refs_1_, f32[672,768]{1,0:T(8,128)} %bitcast_convert_fusion.refs_1_, ...), custom_call_target="tpu_custom_call" | custom-call | flops 8999999488 | bytes 27000000 | tf_op jit(solution)/shard_map/ffn_backward/pallas_call | solution.py:141
  300.2 9.3 %weight_grad.9 = (bf16[2,192,768]{2,1,0:T(8,128)(2,1)}, bf16[2,192,768]{2,1,0:T(8,128)(2,1)}, bf16[2,192,768]{2,1,0:T(8,128)(2,1)}, bf16[2,192,768]{2,1,0:T(8,12...) custom-call(bf16[672,768]{1,0:T(8,128)(2,1)} %get-tuple-element.265., ...), custom_call_target="tpu_custom_call" | custom-call | flops 8000000000 | bytes 24000000 | tf_op jit(solution)/shard_map/weight_grad/pallas_call | solution.py:141
  313.6 17.9 %attention_backward.4 = (bf16[672,576]{1,0:T(8,128)(2,1)}, bf16[672,576]{1,0:T(8,128)(2,1)}, f32[672,768]{1,0:T(8,128)}, f32[2,336,56]{2,1,0:T(8,128)}, f32[2,1,576]{2,1,0:T(1,128)}) custom-call(f32[8,768]{1,0:T(8,128)} %pad.40.refs_0_.refs_1_, bf16[672,768]{1,0:T(8,128)(2,1)} %get-tuple-element.297.refs_1_, bf16[672,192]{1,0:T(8,128)(2,1)} %get-tuple-element.309.refs_2_, ...), custom_call_target="tpu_custom_call" | custom-call | flops 22000001024 | bytes 66000000 | tf_op jit(solution)/shard_map/attention_backward/pallas_call | solution.py:141
  342.8 20.1 %attention_backward.5 = (bf16[672,576]{1,0:T(8,128)(2,1)}, bf16[672,576]{1,0:T(8,128)(2,1)}, f32[672,768]{1,0:T(8,128)}, f32[2,336,56]{2,1,0:T(8,128)}, f32[2,1,576]{2,1,0:T(1,128)}, /*index=5*/f32[8,768]{1,0:T(8,128)}) custom-call(f32[8,768]{1,0:T(8,128)} %pad.40.refs_0_.refs_1_, bf16[672,768]{1,0:T(8,128)(2,1)} %get-tuple-element.297.refs_1_, ...), custom_call_target="tpu_custom_call" | custom-call | flops 22000001024 | bytes 66000000 | tf_op jit(solution)/shard_map/attention_backward/pallas_call | solution.py:141
  382.8 10.8 %ffn_backward.6 = (bf16[672,768]{1,0:T(8,128)(2,1)}, bf16[672,768]{1,0:T(8,128)(2,1)}, f32[672,768]{1,0:T(8,128)}, bf16[672,768]{1,0:T(8,128)(2,1)}, f32[8,768]{1,0:T(8,128)}, /*index=5*/f32[2,1,768]{2,1,0:T(1,128)}) custom-call(f32[8,768]{1,0:T(8,128)} %pad.41.refs_0_.refs_1_, f32[672,768]{1,0:T(8,128)} %get-tuple-element.337.refs_1_, ...), custom_call_target="tpu_custom_call" | custom-call | flops 8999999488 | bytes 27000000 | tf_op jit(solution)/shard_map/ffn_backward/pallas_call | solution.py:141
  410.6 13.9 %ffn_backward.7 = (bf16[672,768]{1,0:T(8,128)(2,1)}, bf16[672,768]{1,0:T(8,128)(2,1)}, f32[672,768]{1,0:T(8,128)}, bf16[672,768]{1,0:T(8,128)(2,1)}, f32[8,768]{1,0:T(8,128)}, /*index=5*/f32[2,1,768]{2,1,0:T(1,128)}) custom-call(f32[8,768]{1,0:T(8,128)} %pad.41.refs_0_.refs_1_, f32[672,768]{1,0:T(8,128)} %get-tuple-element.337.refs_1_, ...), custom_call_target="tpu_custom_call" | custom-call | flops 8999999488 | bytes 27000000 | tf_op jit(solution)/shard_map/ffn_backward/pallas_call | solution.py:141
  429.1 9.3 %weight_grad.13 = (bf16[2,192,768]{2,1,0:T(8,128)(2,1)}, bf16[2,192,768]{2,1,0:T(8,128)(2,1)}, bf16[2,192,768]{2,1,0:T(8,128)(2,1)}, bf16[2,192,768]{2,1,0:T(8,1...) custom-call(bf16[672,768]{1,0:T(8,128)(2,1)} %get-tuple-element.373., ...), custom_call_target="tpu_custom_call" | custom-call | flops 8000000000 | bytes 24000000 | tf_op jit(solution)/shard_map/weight_grad/pallas_call | solution.py:141
  442.6 17.9 %attention_backward.6 = (bf16[672,576]{1,0:T(8,128)(2,1)}, bf16[672,576]{1,0:T(8,128)(2,1)}, f32[672,768]{1,0:T(8,128)}, f32[2,336,56]{2,1,0:T(8,128)}, f32[2,1,576]{2,1,0:T(1,128)}) custom-call(f32[8,768]{1,0:T(8,128)} %pad.41.refs_0_.refs_1_, bf16[672,768]{1,0:T(8,128)(2,1)} %get-tuple-element.370.refs_1_, bf16[672,192]{1,0:T(8,128)(2,1)} %get-tuple-element.389.refs_2_, ...), custom_call_target="tpu_custom_call" | custom-call | flops 22000001024 | bytes 66000000 | tf_op jit(solution)/shard_map/attention_backward/pallas_call | solution.py:141
  476.5 20.1 %attention_backward.7 = (bf16[672,576]{1,0:T(8,128)(2,1)}, bf16[672,576]{1,0:T(8,128)(2,1)}, f32[672,768]{1,0:T(8,128)}, f32[2,336,56]{2,1,0:T(8,128)}, f32[2,1,576]{2,1,0:T(1,128)}, /*index=5*/f32[8,768]{1,0:T(8,128)}) custom-call(f32[8,768]{1,0:T(8,128)} %pad.41.refs_0_.refs_1_, bf16[672,768]{1,0:T(8,128)(2,1)} %get-tuple-element.370.refs_1_, ...), custom_call_target="tpu_custom_call" | custom-call | flops 22000001024 | bytes 66000000 | tf_op jit(solution)/shard_map/attention_backward/pallas_call | solution.py:141
  518.1 12.6 %collective-permute-done.84 = bf16[4,96,768]{2,1,0:T(8,128)(2,1)S(1)} collective-permute-done((bf16[4,96,768]{2,1,0:T(8,128)(2,1)}, bf16[4,96,768]{2,1,0:T(8,128)(2,1)S(1)}, u32[]{:S(2)}, u32[]{:S(2)}) %collective-permute-start.84) | collective-permute-done | bytes 589856 | tf_op jit(solution)/shard_map/ppermute | solution.py:667
  534.5 10.4 %collective-permute-done.91 = bf16[2,192,768]{2,1,0:T(8,128)(2,1)S(1)} collective-permute-done((bf16[2,192,768]{2,1,0:T(8,128)(2,1)}, bf16[2,192,768]{2,1,0:T(8,128)(2,1)S(1)}, u32[]{:S(2)}, u32[]{:S(2)}) %collective-permute-start.91) | collective-permute-done | bytes 589856 | tf_op jit(solution)/shard_map/ppermute | solution.py:667
  556.8 10.9 %collective-permute-done.87 = bf16[2,96,768]{2,1,0:T(8,128)(2,1)S(1)} collective-permute-done((bf16[2,96,768]{2,1,0:T(8,128)(2,1)S(1)}, bf16[2,96,768]{2,1,0:T(8,128)(2,1)S(1)}, u32[]{:S(2)}, u32[]{:S(2)}) %collective-permute-start.87) | collective-permute-done | bytes 294944 | tf_op jit(solution)/shard_map/ppermute | solution.py:667
  (569 shorter events, 260.1 us)
Async XLA Ops:
  59.1 36.9 %collective-permute-start.16 = (bf16[2,192,768]{2,1,0:T(8,128)(2,1)S(1)}, bf16[2,192,768]{2,1,0:T(8,128)(2,1)}, u32[]{:S(2)}, u32[]{:S(2)}) collective-permute-start(bf16[2,192,768]{2,1,0:T(8,128)(2,1)S(1)} %pad_maximum_fusion.5.refs_3_.refs_8_), channel_id=1, source_target_pairs={{0,16},{4,20},{8,24},{12,28},{16,0},{20,4},{24,8},{28,12},{1,17},{... | collective-permute-start | bytes 1769480 | tf_op jit(solution)/shard_map/ppermute | solution.py:667
  61.5 35.1 %collective-permute-start.18 = (bf16[2,192,768]{2,1,0:T(8,128)(2,1)S(1)}, bf16[2,192,768]{2,1,0:T(8,128)(2,1)}, u32[]{:S(2)}, u32[]{:S(2)}) collective-permute-start(bf16[2,192,768]{2,1,0:T(8,128)(2,1)S(1)} %pad_maximum_fusion.5.refs_3_.refs_8_), channel_id=1, source_target_pairs={{0,4},{4,0},{8,12},{12,8},{16,20},{20,16},{24,28},{28,24},{1,5},{5... | collective-permute-start | bytes 1769480 | tf_op jit(solution)/shard_map/ppermute | solution.py:667
  68.3 28.3 %collective-permute-start.19 = (bf16[2,192,768]{2,1,0:T(8,128)(2,1)S(1)}, bf16[2,192,768]{2,1,0:T(8,128)(2,1)}, u32[]{:S(2)}, u32[]{:S(2)}) collective-permute-start(bf16[2,192,768]{2,1,0:T(8,128)(2,1)S(1)} %pad_maximum_fusion.5.refs_3_.refs_8_), channel_id=1, source_target_pairs={{0,2},{1,3},{2,0},{3,1},{4,6},{5,7},{6,4},{7,5},{8,10},{9,11},{10,... | collective-permute-start | bytes 1769480 | tf_op jit(solution)/shard_map/ppermute | solution.py:667
  118.9 35.0 %collective-permute-start.24 = (bf16[2,192,768]{2,1,0:T(8,128)(2,1)}, bf16[2,192,768]{2,1,0:T(8,128)(2,1)}, u32[]{:S(2)}, u32[]{:S(2)}) collective-permute-start(bf16[2,192,768]{2,1,0:T(8,128)(2,1)} %collective-permute-done.19.refs_6_.refs_12_), channel_id=1, source_target_pairs={{0,1},{1,0},{2,3},{3,2},{4,5},{5,4},{6,7},{7,6},{8,9},{9,8},{10,11... | collective-permute-start | bytes 1769480 | tf_op jit(solution)/shard_map/ppermute | solution.py:667
  120.9 33.5 %collective-permute-start.25 = (bf16[2,192,768]{2,1,0:T(8,128)(2,1)}, bf16[2,192,768]{2,1,0:T(8,128)(2,1)}, u32[]{:S(2)}, u32[]{:S(2)}) collective-permute-start(bf16[2,192,768]{2,1,0:T(8,128)(2,1)} %collective-permute-done.22.refs_8_.refs_13_), channel_id=1, source_target_pairs={{0,1},{1,0},{2,3},{3,2},{4,5},{5,4},{6,7},{7,6},{8,9},{9,8},{10,11... | collective-permute-start | bytes 1769480 | tf_op jit(solution)/shard_map/ppermute | solution.py:667
  153.8 31.1 %collective-permute-start.32 = (bf16[4,96,768]{2,1,0:T(8,128)(2,1)S(1)}, bf16[4,96,768]{2,1,0:T(8,128)(2,1)}, u32[]{:S(2)}, u32[]{:S(2)}) collective-permute-start(bf16[4,96,768]{2,1,0:T(8,128)(2,1)S(1)} %pad_maximum_fusion.6.refs_5_.refs_13_), channel_id=1, source_target_pairs={{0,1},{1,0},{2,3},{3,2},{4,5},{5,4},{6,7},{7,6},{8,9},{9,8},{10,11... | collective-permute-start | bytes 1769480 | tf_op jit(solution)/shard_map/ppermute | solution.py:667
  181.2 28.6 %collective-permute-start.41 = (bf16[2,192,768]{2,1,0:T(8,128)(2,1)S(1)}, bf16[2,192,768]{2,1,0:T(8,128)(2,1)}, u32[]{:S(2)}, u32[]{:S(2)}) collective-permute-start(bf16[2,192,768]{2,1,0:T(8,128)(2,1)S(1)} %pad_maximum_fusion.7.refs_3_.refs_8_), channel_id=1, source_target_pairs={{0,16},{4,20},{8,24},{12,28},{16,0},{20,4},{24,8},{28,12},{1,17},{... | collective-permute-start | bytes 1769480 | tf_op jit(solution)/shard_map/ppermute | solution.py:667
  311.0 56.4 %collective-permute-start.60 = (bf16[2,192,768]{2,1,0:T(8,128)(2,1)}, bf16[2,192,768]{2,1,0:T(8,128)(2,1)}, u32[]{:S(2)}, u32[]{:S(2)}) collective-permute-start(bf16[2,192,768]{2,1,0:T(8,128)(2,1)} %get-tuple-element.306), channel_id=1, source_target_pairs={{0,2},{1,3},{2,0},{3,1},{4,6},{5,7},{6,4},{7,5},{8,10},{9,11},{10,... | collective-permute-start | bytes 1769480 | tf_op jit(solution)/shard_map/ppermute | solution.py:667
  312.1 56.1 %collective-permute-start.61 = (bf16[2,192,768]{2,1,0:T(8,128)(2,1)}, bf16[2,192,768]{2,1,0:T(8,128)(2,1)}, u32[]{:S(2)}, u32[]{:S(2)}) collective-permute-start(bf16[2,192,768]{2,1,0:T(8,128)(2,1)} %get-tuple-element.305), channel_id=1, source_target_pairs={{0,4},{4,0},{8,12},{12,8},{16,20},{20,16},{24,28},{28,24},{1,5},{5... | collective-permute-start | bytes 1769480 | tf_op jit(solution)/shard_map/ppermute | solution.py:667
  333.5 34.7 %collective-permute-start.59 = (bf16[2,192,768]{2,1,0:T(8,128)(2,1)S(1)}, bf16[2,192,768]{2,1,0:T(8,128)(2,1)S(1)}, u32[]{:S(2)}, u32[]{:S(2)}) collective-permute-start(bf16[2,192,768]{2,1,0:T(8,128)(2,1)S(1)} %add_convert_fusion.13), channel_id=1, source_target_pairs={{0,4},{4,0},{8,12},{12,8},{16,20},{20,16},{24,28},{28,24},{1,5},{5... | collective-permute-start | bytes 1769480 | tf_op jit(solution)/shard_map/ppermute | solution.py:667
  334.2 34.0 %collective-permute-start.62 = (bf16[2,192,768]{2,1,0:T(8,128)(2,1)S(1)}, bf16[2,192,768]{2,1,0:T(8,128)(2,1)}, u32[]{:S(2)}, u32[]{:S(2)}) collective-permute-start(bf16[2,192,768]{2,1,0:T(8,128)(2,1)S(1)} %add_convert_fusion.12), channel_id=1, source_target_pairs={{0,2},{1,3},{2,0},{3,1},{4,6},{5,7},{6,4},{7,5},{8,10},{9,11},{10,... | collective-permute-start | bytes 1769480 | tf_op jit(solution)/shard_map/ppermute | solution.py:667
  342.8 30.3 %collective-permute-start.63 = (bf16[8,96,768]{2,1,0:T(8,128)(2,1)}, bf16[8,96,768]{2,1,0:T(8,128)(2,1)}, u32[]{:S(2)}, u32[]{:S(2)}) collective-permute-start(bf16[8,96,768]{2,1,0:T(8,128)(2,1)} %get-tuple-element.325), channel_id=1, source_target_pairs={{0,1},{1,0},{2,3},{3,2},{4,5},{5,4},{6,7},{7,6},{8,9},{9,8},{10,11... | collective-permute-start | bytes 3538952 | tf_op jit(solution)/shard_map/ppermute | solution.py:667
  370.6 38.0 %collective-permute-start.68 = (bf16[2,192,768]{2,1,0:T(8,128)(2,1)}, bf16[2,192,768]{2,1,0:T(8,128)(2,1)S(1)}, u32[]{:S(2)}, u32[]{:S(2)}) collective-permute-start(bf16[2,192,768]{2,1,0:T(8,128)(2,1)} %add_convert_fusion.10), channel_id=1, source_target_pairs={{0,16},{4,20},{8,24},{12,28},{16,0},{20,4},{24,8},{28,12},{1,17},{... | collective-permute-start | bytes 1769480 | tf_op jit(solution)/shard_map/ppermute | solution.py:667
  382.2 45.0 %collective-permute-start.67 = (bf16[4,96,768]{2,1,0:T(8,128)(2,1)}, bf16[4,96,768]{2,1,0:T(8,128)(2,1)S(1)}, u32[]{:S(2)}, u32[]{:S(2)}) collective-permute-start(bf16[4,96,768]{2,1,0:T(8,128)(2,1)} %get-tuple-element.352), channel_id=1, source_target_pairs={{0,2},{1,3},{2,0},{3,1},{4,6},{5,7},{6,4},{7,5},{8,10},{9,11},{10,... | collective-permute-start | bytes 1769480 | tf_op jit(solution)/shard_map/ppermute | solution.py:667
  397.4 29.8 %collective-permute-start.66 = (bf16[4,96,768]{2,1,0:T(8,128)(2,1)S(1)}, bf16[4,96,768]{2,1,0:T(8,128)(2,1)S(1)}, u32[]{:S(2)}, u32[]{:S(2)}) collective-permute-start(bf16[4,96,768]{2,1,0:T(8,128)(2,1)S(1)} %add_convert_fusion.9), channel_id=1, source_target_pairs={{0,4},{4,0},{8,12},{12,8},{16,20},{20,16},{24,28},{28,24},{1,5},{5... | collective-permute-start | bytes 1769480 | tf_op jit(solution)/shard_map/ppermute | solution.py:667
  427.5 32.9 %collective-permute-start.73 = (bf16[2,96,768]{2,1,0:T(8,128)(2,1)S(1)}, bf16[2,96,768]{2,1,0:T(8,128)(2,1)S(1)}, u32[]{:S(2)}, u32[]{:S(2)}) collective-permute-start(bf16[2,96,768]{2,1,0:T(8,128)(2,1)S(1)} %slice.520), channel_id=1, source_target_pairs={{0,16},{4,20},{8,24},{12,28},{16,0},{20,4},{24,8},{28,12},{1,17},{... | collective-permute-start | bytes 884744 | tf_op jit(solution)/shard_map/ppermute | solution.py:667
  438.4 27.4 %collective-permute-start.71 = (bf16[2,192,768]{2,1,0:T(8,128)(2,1)}, bf16[2,192,768]{2,1,0:T(8,128)(2,1)S(1)}, u32[]{:S(2)}, u32[]{:S(2)}) collective-permute-start(bf16[2,192,768]{2,1,0:T(8,128)(2,1)} %get-tuple-element.381), channel_id=1, source_target_pairs={{0,2},{1,3},{2,0},{3,1},{4,6},{5,7},{6,4},{7,5},{8,10},{9,11},{10,... | collective-permute-start | bytes 1769480 | tf_op jit(solution)/shard_map/ppermute | solution.py:667
  440.1 60.0 %collective-permute-start.76 = (bf16[2,192,768]{2,1,0:T(8,128)(2,1)}, bf16[2,192,768]{2,1,0:T(8,128)(2,1)}, u32[]{:S(2)}, u32[]{:S(2)}) collective-permute-start(bf16[2,192,768]{2,1,0:T(8,128)(2,1)} %get-tuple-element.386), channel_id=1, source_target_pairs={{0,2},{1,3},{2,0},{3,1},{4,6},{5,7},{6,4},{7,5},{8,10},{9,11},{10,... | collective-permute-start | bytes 1769480 | tf_op jit(solution)/shard_map/ppermute | solution.py:667
  441.0 61.8 %collective-permute-start.77 = (bf16[2,192,768]{2,1,0:T(8,128)(2,1)}, bf16[2,192,768]{2,1,0:T(8,128)(2,1)}, u32[]{:S(2)}, u32[]{:S(2)}) collective-permute-start(bf16[2,192,768]{2,1,0:T(8,128)(2,1)} %get-tuple-element.385), channel_id=1, source_target_pairs={{0,4},{4,0},{8,12},{12,8},{16,20},{20,16},{24,28},{28,24},{1,5},{5... | collective-permute-start | bytes 1769480 | tf_op jit(solution)/shard_map/ppermute | solution.py:667
  467.2 35.6 %collective-permute-start.75 = (bf16[2,192,768]{2,1,0:T(8,128)(2,1)S(1)}, bf16[2,192,768]{2,1,0:T(8,128)(2,1)}, u32[]{:S(2)}, u32[]{:S(2)}) collective-permute-start(bf16[2,192,768]{2,1,0:T(8,128)(2,1)S(1)} %add_convert_fusion.6), channel_id=1, source_target_pairs={{0,4},{4,0},{8,12},{12,8},{16,20},{20,16},{24,28},{28,24},{1,5},{5... | collective-permute-start | bytes 1769480 | tf_op jit(solution)/shard_map/ppermute | solution.py:667
  467.8 35.0 %collective-permute-start.78 = (bf16[2,192,768]{2,1,0:T(8,128)(2,1)S(1)}, bf16[2,192,768]{2,1,0:T(8,128)(2,1)}, u32[]{:S(2)}, u32[]{:S(2)}) collective-permute-start(bf16[2,192,768]{2,1,0:T(8,128)(2,1)S(1)} %add_convert_fusion.5), channel_id=1, source_target_pairs={{0,2},{1,3},{2,0},{3,1},{4,6},{5,7},{6,4},{7,5},{8,10},{9,11},{10,... | collective-permute-start | bytes 1769480 | tf_op jit(solution)/shard_map/ppermute | solution.py:667
  476.4 30.3 %collective-permute-start.79 = (bf16[8,96,768]{2,1,0:T(8,128)(2,1)}, bf16[8,96,768]{2,1,0:T(8,128)(2,1)}, u32[]{:S(2)}, u32[]{:S(2)}) collective-permute-start(bf16[8,96,768]{2,1,0:T(8,128)(2,1)} %get-tuple-element.406), channel_id=1, source_target_pairs={{0,1},{1,0},{2,3},{3,2},{4,5},{5,4},{6,7},{7,6},{8,9},{9,8},{10,11... | collective-permute-start | bytes 3538952 | tf_op jit(solution)/shard_map/ppermute | solution.py:667
  516.2 28.8 %collective-permute-start.91 = (bf16[2,192,768]{2,1,0:T(8,128)(2,1)}, bf16[2,192,768]{2,1,0:T(8,128)(2,1)S(1)}, u32[]{:S(2)}, u32[]{:S(2)}) collective-permute-start(bf16[2,192,768]{2,1,0:T(8,128)(2,1)} %add_convert_fusion.3), channel_id=1, source_target_pairs={{0,16},{4,20},{8,24},{12,28},{16,0},{20,4},{24,8},{28,12},{1,17},{... | collective-permute-start | bytes 1769480 | tf_op jit(solution)/shard_map/ppermute | solution.py:667
  517.6 32.6 %collective-permute-start.83 = (bf16[4,96,768]{2,1,0:T(8,128)(2,1)}, bf16[4,96,768]{2,1,0:T(8,128)(2,1)}, u32[]{:S(2)}, u32[]{:S(2)}) collective-permute-start(bf16[4,96,768]{2,1,0:T(8,128)(2,1)} %get-tuple-element.450), channel_id=1, source_target_pairs={{0,4},{4,0},{8,12},{12,8},{16,20},{20,16},{24,28},{28,24},{1,5},{5... | collective-permute-start | bytes 1769480 | tf_op jit(solution)/shard_map/ppermute | solution.py:667
  (116 other events, 1435.4 us)
